TPU v7x, 512 devices: a whole 4x8x8 slice. The times are simulated.
512 devices in a mesh: sub: 64 (over z, x, core), coarse: 8 (over y).
Axes of the slice: x: 4, y: 8, z: 8, core: 2. Of those that a mesh axis runs over, the one named last changes fastest.
Arguments:
- load: bfloat16 [512, 512, 128], P(('sub', 'coarse')), may hold values from -18 to 18
- schur: bfloat16 [512, 512, 512], P(('sub', 'coarse')), as said below
- coupling: bfloat16 [512, 24, 512], P(('sub', 'coarse')), may hold values from -0.5 to 0.5
- coarse_inverse: bfloat16 [16384, 16384], P('coarse', 'sub'), as said below
- neighbour_sub: int32 [512, 8], P(('sub', 'coarse')), may hold values from 0 to 511, as said below
- neighbour_edge: int32 [512, 8], P(('sub', 'coarse')), may hold values from 0 to 7, as said below
- primal_owner: int32 [512, 24, 1], P(('sub', 'coarse')), may hold values from 0 to 63; in each aligned block of 24 rows (0 to 23, 24 to 47, ..., all dimensions but the last counted through in order) at most 2 rows name the same one
- primal_offset: int32 [512, 24], P(('sub', 'coarse')), may hold values from 0 to 255
Outputs:
- multipliers: float32 [512, 512, 128], P(('sub', 'coarse'))
Inputs may be any that keep to these rules, and one draw needn't show every extreme that they name: `neighbour_sub`: each edge faces exactly one edge of a subdomain, and that edge faces it back. The subdomain across lies on the same index of coarse and on the same index of sub or the one before or after it, cyclically. On every device exactly 8 edges face a subdomain of another device, half of them on each side. `neighbour_edge`: the number of the facing edge at the subdomain across. `primal_owner`: among the primal dofs of the subdomains of one device, no owner is named more than 2 times; in every draw some owner is named exactly 2 times by some device. `schur`: each matrix is symmetric positive definite. `coarse_inverse`: symmetric positive definite once its rows are put in the order of its columns as the steps state.
All inputs are finite; a program needn't handle non-finite values.
Results may differ from a plain program's by a relative error of at most 0.0003.
The roundings to bfloat16 on the way count: a program that leaves them out, or rounds other values in their place, can miss the bound.
Values may be sent and summed in bfloat16 or wider, within the bound.
No kernel may reach another device: no remote copies, remote signals or barrier semaphores. Data moves between devices by JAX's collectives and lax.ppermute only.
A program may use at most 64 MiB of HBM per device.

v0:
```python
import jax
import jax.numpy as jnp
from jax import lax
from jax.sharding import PartitionSpec as P

ITERS = 2


def with_halo(cells, sides, width):
    for axis, dim in sides:
        count = lax.axis_size(axis)
        head = lax.slice_in_dim(cells, 0, width, axis=dim)
        tail = lax.slice_in_dim(cells, cells.shape[dim] - width, cells.shape[dim], axis=dim)
        cells = jnp.concatenate(
            [
                lax.ppermute(tail, axis, [(i, (i + 1) % count) for i in range(count)]),
                cells,
                lax.ppermute(head, axis, [((i + 1) % count, i) for i in range(count)]),
            ],
            axis=dim,
        )
    return cells


def body(
    load,
    schur,
    coupling,
    coarse_inverse,
    neighbour_sub,
    neighbour_edge,
    primal_owner,
    primal_offset,
):
    sub_dev, order, cases = load.shape
    edge_count = neighbour_sub.shape[1]
    edge_width = order // edge_count
    slots = sub_dev * edge_count
    prim_count = coupling.shape[1]
    coarse_block = coarse_inverse.shape[1]
    sub_size = lax.axis_size("sub")
    coarse_size = lax.axis_size("coarse")
    sub_index = lax.axis_index("sub")
    capacity = max(2, 2 * sub_dev * prim_count // sub_size)
    flat_sub = neighbour_sub.reshape(-1)
    flat_edge = neighbour_edge.reshape(-1)
    source_side = (flat_sub // sub_dev // coarse_size - sub_index + 1) % sub_size
    local_slot = flat_sub % sub_dev * edge_count + flat_edge

    def jump(field):
        edges = field.reshape(slots, edge_width, cases)
        beside_all = with_halo(edges[None], (("sub", 0),), 1)
        facing = beside_all.reshape(3 * slots, edge_width, cases)[source_side * slots + local_slot]
        return (edges - facing).reshape(sub_dev, order, cases)

    owners = primal_owner.reshape(-1)
    offsets = primal_offset.reshape(-1)
    rows_local = sub_dev * prim_count
    row_ids = jnp.arange(rows_local, dtype=jnp.int32)
    earlier = (owners[:, None] == owners[None, :]) & (row_ids[None, :] < row_ids[:, None])
    slot_pos = owners * capacity + jnp.sum(earlier.astype(jnp.int32), axis=1)
    send_offsets = jnp.zeros((sub_size * capacity,), jnp.int32).at[slot_pos].set(offsets)
    recv_offsets = lax.all_to_all(send_offsets, "sub", split_axis=0, concat_axis=0, tiled=True)

    def squares(vector):
        return lax.psum(jnp.sum(vector * vector, axis=(0, 1)), ("sub", "coarse"))

    residual = jump(load.astype(jnp.float32))
    direction = residual
    solution = jnp.zeros_like(residual)
    norm_now = squares(residual)
    for step in range(ITERS):
        operator_jumps = jump(direction).astype(jnp.bfloat16)
        local = jnp.einsum(
            "snm,smr->snr", schur, operator_jumps, preferred_element_type=jnp.float32
        )
        terms = jnp.einsum(
            "spn,snr->spr", coupling, operator_jumps, preferred_element_type=jnp.float32
        )
        outgoing = (
            jnp.zeros((sub_size * capacity, cases), jnp.float32)
            .at[slot_pos]
            .set(terms.reshape(rows_local, cases))
        )
        incoming = lax.all_to_all(outgoing, "sub", split_axis=0, concat_axis=0, tiled=True)
        partial_rhs = jax.ops.segment_sum(incoming, recv_offsets, num_segments=coarse_block)
        coarse_rhs = lax.psum(partial_rhs, "coarse").astype(jnp.bfloat16)
        share = lax.psum_scatter(
            jnp.dot(coarse_inverse, coarse_rhs, preferred_element_type=jnp.float32),
            "sub",
            scatter_dimension=0,
            tiled=True,
        )
        owned = lax.all_gather(share.astype(jnp.bfloat16), "coarse", axis=0, tiled=True)
        replies = lax.all_to_all(
            owned[recv_offsets], "sub", split_axis=0, concat_axis=0, tiled=True
        )
        values = replies[slot_pos].reshape(sub_dev, prim_count, cases)
        image = jump(
            local + jnp.einsum("spn,spr->snr", coupling, values, preferred_element_type=jnp.float32)
        )
        alpha = norm_now / lax.psum(jnp.sum(direction * image, axis=(0, 1)), ("sub", "coarse"))
        solution = solution + alpha * direction
        if step + 1 < ITERS:
            residual = residual - alpha * image
            norm_next = squares(residual)
            direction = residual + norm_next / norm_now * direction
            norm_now = norm_next
    return solution


def solution(mesh):
    return jax.shard_map(
        body,
        mesh=mesh,
        in_specs=(
            P(("sub", "coarse"), None, None),
            P(("sub", "coarse"), None, None),
            P(("sub", "coarse"), None, None),
            P("coarse", "sub"),
            P(("sub", "coarse"), None),
            P(("sub", "coarse"), None),
            P(("sub", "coarse"), None, None),
            P(("sub", "coarse"), None),
        ),
        out_specs=P(("sub", "coarse"), None, None),
        check_vma=False,
    )
```

profile of v0, /device:TPU:1, one launch (start us, length us, event | category | flops | bytes accessed | tf_op | source)
XLA Modules:
  0.0 859.8 jit_solution(13535719925040676069)
XLA Ops:
  7.7 8.8 %collective-permute-start.1 = (f32[1,8,64,128]{3,2,1,0:T(8,128)S(1)}, f32[1,8,64,128]{3,2,1,0:T(8,128)S(1)}, u32[]{:S(2)}, u32[]{:S(2)}) collective-permute-start(f32[1,8,64,128]{3,2,1,0:T(8,128)S(1)} %bitcast.117), channel_id=1, source_target_pairs={{8,0},{16,8},{24,16},{32,24},{40,32},{48,40},{56,48},{64,56},{72,6... | collective-permute-start | bytes 786440 | tf_op jit(solution)/shard_map/ppermute | solution.py:18
  19.2 5.6 collective-permute-done
  25.5 10.0 %collective-permute-start.3 = (f32[1,8,64,128]{3,2,1,0:T(8,128)S(1)}, f32[1,8,64,128]{3,2,1,0:T(8,128)S(1)}, u32[]{:S(2)}, u32[]{:S(2)}) collective-permute-start(f32[1,8,64,128]{3,2,1,0:T(8,128)S(1)} %bitcast_subtract_fusion.1), channel_id=1, source_target_pairs={{8,0},{16,8},{24,16},{32,24},{40,32},{48,40},{56,48},{64,56},{72,6... | collective-permute-start | bytes 786440 | tf_op jit(solution)/shard_map/ppermute | solution.py:18
  39.1 6.9 all-to-all-start
  49.1 6.3 all-to-all-done
  55.4 4.7 all-to-all-start.1
  61.7 8.6 all-to-all-done.1
  71.6 24.6 %all-reduce.3 = bf16[256,128]{1,0:T(8,128)(2,1)S(1)} all-reduce(f32[256,128]{1,0:T(8,128)S(1)} %scatter_custom_fusion.2), channel_id=1, replica_groups=mesh['sub'=64,'coarse'=8] {'coarse'}, use_global_device_ids=true, to_apply=%region_6.7 | all-reduce | flops 32768 | bytes 196608 | tf_op jit(solution)/shard_map/psum | solution.py:87
  98.2 141.9 %reduce-scatter.7.cloned.1.call-done = f32[32,128]{1,0:T(8,128)} async-done(((f32[2048,128]{1,0:T(8,128)}), f32[32,128]{1,0:T(8,128)}) %reduce-scatter.7.cloned.1.call-update) | async-done | bytes 16400 | tf_op jit(solution)/shard_map/reduce_scatter | solution.py:88
  240.8 19.2 %all_gather.6 = bf16[256,128]{1,0:T(8,128)(2,1)S(1)} all-gather(bf16[32,128]{1,0:T(8,128)(2,1)S(1)} %convert_element_type.32), channel_id=1, replica_groups=mesh['sub'=64,'coarse'=8] {'coarse'}, dimensions={0}, use_global_device_ids=true | all-gather | bytes 73728 | tf_op jit(solution)/shard_map/all_gather | solution.py:94
  261.3 18.9 %all-to-all-start.2 = ((bf16[64,2,128]{2,1,0:T(2,128)(2,1)}), bf16[64,2,128]{2,1,0:T(2,128)(2,1)S(1)}, u32[]{:S(2)}, u32[]{:S(2)}) async-start(bf16[64,2,128]{2,1,0:T(2,128)(2,1)} %bitcast.23), calls=%async_computation.2 | async-start | bytes 65536 | tf_op jit(solution)/shard_map/all_to_all | solution.py:95
  280.3 9.2 %all-to-all-done.2 = bf16[64,2,128]{2,1,0:T(2,128)(2,1)S(1)} async-done(((bf16[64,2,128]{2,1,0:T(2,128)(2,1)}), bf16[64,2,128]{2,1,0:T(2,128)(2,1)S(1)}, u32[]{:S(2)}, u32[]{:S(2)}) %all-to-all-start.2) | async-done | bytes 32800 | tf_op jit(solution)/shard_map/all_to_all | solution.py:95
  293.4 3.0 collective-permute-start.4
  300.6 98.3 %all-reduce = (f32[128]{0:T(128)S(1)}, f32[128]{0:T(128)S(1)}) all-reduce(f32[128]{0:T(128)S(1)} %get-tuple-element.6, f32[128]{0:T(128)S(1)} %get-tuple-element.5), channel_id=1, replica_groups=mesh['sub'=64,'coarse'=8] {'sub','coarse'}, use_global_device_ids=true, to_apply=%region_1.2 | all-reduce | flops 256 | bytes 2048 | tf_op jit(solution)/shard_map/psum | solution.py:66
  399.1 94.5 %psum.45 = f32[128]{0:T(128)S(1)} all-reduce(f32[128]{0:T(128)S(1)} %multiply_reduce_fusion), channel_id=1, replica_groups=mesh['sub'=64,'coarse'=8] {'sub','coarse'}, use_global_device_ids=true, to_apply=%region_11.12 | all-reduce | flops 128 | bytes 1024 | tf_op jit(solution)/shard_map/psum | solution.py:66
  496.4 3.0 collective-permute-start.6
  504.4 21.5 %all_to_all.57 = f32[64,2,128]{2,1,0:T(2,128)S(1)} all-to-all(f32[64,2,128]{2,1,0:T(2,128)S(1)} %bitcast.140), channel_id=1, replica_groups=mesh['sub'=64,'coarse'=8] {'sub'}, dimensions={0} | all-to-all | bytes 131072 | tf_op jit(solution)/shard_map/all_to_all | solution.py:85
  527.3 21.5 %all-reduce.4 = bf16[256,128]{1,0:T(8,128)(2,1)S(1)} all-reduce(f32[256,128]{1,0:T(8,128)S(1)} %scatter_custom_fusion.4), channel_id=1, replica_groups=mesh['sub'=64,'coarse'=8] {'coarse'}, use_global_device_ids=true, to_apply=%region_14.15 | all-reduce | flops 32768 | bytes 196608 | tf_op jit(solution)/shard_map/psum | solution.py:87
  550.6 143.4 %reduce-scatter.9.cloned.1.call-done = f32[32,128]{1,0:T(8,128)} async-done(((f32[2048,128]{1,0:T(8,128)}), f32[32,128]{1,0:T(8,128)}) %reduce-scatter.9.cloned.1.call-update) | async-done | bytes 16400 | tf_op jit(solution)/shard_map/reduce_scatter | solution.py:88
  694.7 19.2 %all_gather.7 = bf16[256,128]{1,0:T(8,128)(2,1)S(1)} all-gather(bf16[32,128]{1,0:T(8,128)(2,1)S(1)} %convert_element_type.35), channel_id=1, replica_groups=mesh['sub'=64,'coarse'=8] {'coarse'}, dimensions={0}, use_global_device_ids=true | all-gather | bytes 73728 | tf_op jit(solution)/shard_map/all_gather | solution.py:94
  714.6 28.1 %all_to_all.58 = bf16[64,2,128]{2,1,0:T(2,128)(2,1)S(1)} all-to-all(bf16[64,2,128]{2,1,0:T(2,128)(2,1)S(1)} %bitcast.143), channel_id=1, replica_groups=mesh['sub'=64,'coarse'=8] {'sub'}, dimensions={0} | all-to-all | bytes 65536 | tf_op jit(solution)/shard_map/all_to_all | solution.py:95
  744.0 2.6 collective-permute-start.9
  746.6 3.0 collective-permute-start.8
  753.8 98.3 %psum.47 = f32[128]{0:T(128)S(1)} all-reduce(f32[128]{0:T(128)S(1)} %fusion.4), channel_id=1, replica_groups=mesh['sub'=64,'coarse'=8] {'sub','coarse'}, use_global_device_ids=true, to_apply=%region_17.18 | all-reduce | flops 128 | bytes 1024 | tf_op jit(solution)/shard_map/psum | solution.py:102
  (94 shorter events, 45.0 us)
Async XLA Ops:
  6.5 89.7 %copy-start = (bf16[2048,256]{1,0:T(8,128)(2,1)S(1)}, bf16[2048,256]{1,0:T(8,128)(2,1)}, u32[]{:S(2)}) copy-start(bf16[2048,256]{1,0:T(8,128)(2,1)} %param.11) | copy-start | bytes 3145732
  7.7 11.4 %collective-permute-start.1 = (f32[1,8,64,128]{3,2,1,0:T(8,128)S(1)}, f32[1,8,64,128]{3,2,1,0:T(8,128)S(1)}, u32[]{:S(2)}, u32[]{:S(2)}) collective-permute-start(f32[1,8,64,128]{3,2,1,0:T(8,128)S(1)} %bitcast.117), channel_id=1, source_target_pairs={{8,0},{16,8},{24,16},{32,24},{40,32},{48,40},{56,48},{64,56},{72,6... | collective-permute-start | bytes 786440 | tf_op jit(solution)/shard_map/ppermute | solution.py:18
  16.5 8.2 collective-permute-start
  18.5 0.7 copy-start.3
  18.5 0.7 copy-start.4
  25.4 11.9 %copy-start.5 = (s32[1,24,1]{1,2,0:T(1,128)S(1)}, s32[1,24,1]{1,2,0:T(1,128)}, u32[]{:S(2)}) copy-start(s32[1,24,1]{1,2,0:T(1,128)} %param.14) | copy-start | bytes 292
  25.5 20.7 %collective-permute-start.3 = (f32[1,8,64,128]{3,2,1,0:T(8,128)S(1)}, f32[1,8,64,128]{3,2,1,0:T(8,128)S(1)}, u32[]{:S(2)}, u32[]{:S(2)}) collective-permute-start(f32[1,8,64,128]{3,2,1,0:T(8,128)S(1)} %bitcast_subtract_fusion.1), channel_id=1, source_target_pairs={{8,0},{16,8},{24,16},{32,24},{40,32},{48,40},{56,48},{64,56},{72,6... | collective-permute-start | bytes 786440 | tf_op jit(solution)/shard_map/ppermute | solution.py:18
  35.5 10.7 %collective-permute-start.2 = (f32[1,8,64,128]{3,2,1,0:T(8,128)S(1)}, f32[1,8,64,128]{3,2,1,0:T(8,128)S(1)}, u32[]{:S(2)}, u32[]{:S(2)}) collective-permute-start(f32[1,8,64,128]{3,2,1,0:T(8,128)S(1)} %bitcast_subtract_fusion.1), channel_id=1, source_target_pairs={{0,8},{8,16},{16,24},{24,32},{32,40},{40,48},{48,56},{56,64},{64,7... | collective-permute-start | bytes 786440 | tf_op jit(solution)/shard_map/ppermute | solution.py:16
  39.1 16.3 %all-to-all-start = ((s32[64,2,1]{1,2,0:T(1,128)}), s32[64,2,1]{1,2,0:T(1,128)S(1)}, u32[]{:S(2)}, u32[]{:S(2)}) async-start(s32[64,2,1]{1,2,0:T(1,128)} %bitcast.16), calls=%async_computation | async-start | bytes 65536 | tf_op jit(solution)/shard_map/all_to_all | solution.py:63
  47.0 0.7 copy-start.2
  55.4 14.8 %all-to-all-start.1 = ((f32[64,2,128]{2,1,0:T(2,128)}), f32[64,2,128]{2,1,0:T(2,128)S(1)}, u32[]{:S(2)}, u32[]{:S(2)}) async-start(f32[64,2,128]{2,1,0:T(2,128)} %bitcast.19), calls=%async_computation.1 | async-start | bytes 131072 | tf_op jit(solution)/shard_map/all_to_all | solution.py:85
  60.1 180.0 %reduce-scatter.7.cloned.1.call-start = ((), (), s32[]{:S(2)}) async-start(), calls=%async_computation.7 | async-start | bytes 1064960 | tf_op jit(solution)/shard_map/reduce_scatter | solution.py:88
  98.0 192.3 %copy-start.1 = (bf16[1,512,512]{2,1,0:T(8,128)(2,1)S(1)}, bf16[1,512,512]{2,1,0:T(8,128)(2,1)}, u32[]{:S(2)}) copy-start(bf16[1,512,512]{2,1,0:T(8,128)(2,1)} %param.9) | copy-start | bytes 1572868
  261.3 28.2 %all-to-all-start.2 = ((bf16[64,2,128]{2,1,0:T(2,128)(2,1)}), bf16[64,2,128]{2,1,0:T(2,128)(2,1)S(1)}, u32[]{:S(2)}, u32[]{:S(2)}) async-start(bf16[64,2,128]{2,1,0:T(2,128)(2,1)} %bitcast.23), calls=%async_computation.2 | async-start | bytes 65536 | tf_op jit(solution)/shard_map/all_to_all | solution.py:95
  280.2 413.7 %reduce-scatter.9.cloned.1.call-start = ((), (), s32[]{:S(2)}) async-start(), calls=%async_computation.8 | async-start | bytes 1064960 | tf_op jit(solution)/shard_map/reduce_scatter | solution.py:88
  290.8 7.7 collective-permute-start.5
  293.4 6.3 collective-permute-start.4
  493.8 7.7 collective-permute-start.7
  496.4 6.3 collective-permute-start.6
  744.0 7.7 collective-permute-start.9
  746.6 6.3 collective-permute-start.8
Sparse Core Ops, SparseCore 0:
  98.2 141.8 reduce-scatter.6
  550.7 143.2 reduce-scatter.8
where the time goes:
time: 861 us; the launch traced here: 860 us
  blocking collectives  425 us (49%)
  waiting for transfers between devices  325 us (38%)
  starting transfers between devices  69.9 us (8%)
  local copies, waits for them, and re-layouts  17.4 us (2%)
  between operations  14 us (2%)
    reduce_scatter x2, waiting for transfers between devices, body(): lax.psum_scatter(jnp.dot(coarse_inverse, coarse_rhs, preferred_element_ty...  285 us
    psum x2, blocking collectives, squares(): return lax.psum(jnp.sum(vector * vector, axis=(0, 1)), ('sub', 'coarse'))  193 us
    psum x1, blocking collectives, body(): lax.psum(jnp.sum(direction * image, axis=(0, 1)), ('sub', 'coarse'))  98.3 us
    psum x2, blocking collectives, body(): coarse_rhs = lax.psum(partial_rhs, 'coarse').astype(jnp.bfloat16)  46.1 us
    all_gather x2, blocking collectives, body(): lax.all_gather(share.astype(jnp.bfloat16), 'coarse', axis=0, tiled=True)  38.4 us
    all_to_all x1, blocking collectives, body(): lax.all_to_all(owned[recv_offsets], 'sub', split_axis=0, concat_axis=0, t...  28.1 us
    ppermute x5, starting transfers between devices, with_halo(): lax.ppermute(head, axis, [((i + 1) % count, i) for i in range(count)])  26.5 us
    all_to_all x1, blocking collectives, body(): lax.all_to_all(outgoing, 'sub', split_axis=0, concat_axis=0, tiled=True)  21.5 us
  transfers between devices with their start and end apart: 15, of which 12 were waited for; matrix products, arithmetic and copies ran while one was open for 1% of the time, Pallas kernels for 0%

commit v1 on v0

v1 whole, which is shorter than its diff:
```python
import jax
import jax.numpy as jnp
from jax import lax
from jax.sharding import PartitionSpec as P

HIGHEST = lax.Precision.HIGHEST
F32, BF16 = jnp.float32, jnp.bfloat16


def exchange(blocks, axis):
    return lax.all_to_all(blocks, axis, split_axis=0, concat_axis=0, tiled=True)


def in_three(value):
    high = lax.reduce_precision(value, 8, 7)
    rest = value - high
    middle = lax.reduce_precision(rest, 8, 7)
    return [part.astype(BF16) for part in (high, middle, rest - middle)]


def body(
    load,
    schur,
    coupling,
    coarse_inverse,
    neighbour_sub,
    neighbour_edge,
    primal_owner,
    primal_offset,
):
    _, order, cases = load.shape
    edges = neighbour_sub.shape[1]
    width = order // edges
    half = edges // 2
    rows, block = coarse_inverse.shape
    n_sub, n_coarse = lax.axis_size("sub"), lax.axis_size("coarse")
    piece = block // n_coarse
    capacity = 2
    slots = n_sub * capacity
    sub_index = lax.axis_index("sub")

    faces_next = (neighbour_sub[0] // n_coarse - sub_index) % n_sub == 1
    edge_at = neighbour_edge[0]
    same_side = faces_next[:, None] == faces_next[None, :]
    ids = jnp.arange(edges, dtype=jnp.int32)
    from_place = jnp.sum((same_side & (edge_at[None, :] < edge_at[:, None])).astype(jnp.int32), axis=1)
    from_place = from_place + jnp.where(faces_next, half, 0)
    to_place = jnp.sum((same_side & (ids[None, :] < ids[:, None])).astype(jnp.int32), axis=1)
    to_place = to_place + jnp.where(faces_next, 0, half)
    send_order = jnp.sum(jnp.where(to_place[None, :] == ids[:, None], ids[None, :], 0), axis=1)

    def facing(field):
        ordered = field.reshape(edges, width, cases)[send_order]
        from_before = lax.ppermute(ordered[:half], "sub", [(i, (i + 1) % n_sub) for i in range(n_sub)])
        from_next = lax.ppermute(ordered[half:], "sub", [((i + 1) % n_sub, i) for i in range(n_sub)])
        both = jnp.concatenate([from_before, from_next], axis=0)
        return both[from_place].reshape(order, cases)

    owners = primal_owner.reshape(-1)
    offsets = primal_offset.reshape(-1)
    prims = owners.shape[0]
    row_ids = jnp.arange(prims, dtype=jnp.int32)
    earlier = (owners[:, None] == owners[None, :]) & (row_ids[None, :] < row_ids[:, None])
    slot_of = owners * capacity + jnp.sum(earlier.astype(jnp.int32), axis=1)
    placed = jnp.arange(slots, dtype=jnp.int32)[:, None] == slot_of[None, :]
    slotted = jnp.dot(placed.astype(BF16), coupling[0], preferred_element_type=F32).astype(BF16)
    slot_offset = jnp.sum(jnp.where(placed, offsets[None, :] + 1, 0), axis=1) - 1
    inverse_t = coarse_inverse.T

    def forward(field, scalars, marks):
        twice = 2.0 * field
        jumps = twice.astype(BF16)
        rest = (twice - jumps.astype(F32)).astype(BF16)
        local = jnp.dot(schur[0], jumps, preferred_element_type=F32)
        terms = jnp.dot(slotted, jnp.concatenate([jumps, rest], axis=1), preferred_element_type=F32)
        rounded, left = terms[:, :cases], terms[:, cases:]
        near = jnp.sum(twice * local, axis=0)
        tail = jnp.stack([near] + scalars)
        parts = [
            rounded.reshape(n_sub, capacity, cases),
            (rounded + left).reshape(n_sub, capacity, cases),
            jnp.broadcast_to(tail[None], (n_sub,) + tail.shape),
        ]
        if marks is None:
            parts.append(
                jnp.broadcast_to(slot_offset.astype(F32).reshape(n_sub, capacity, 1), (n_sub, capacity, cases))
            )
        incoming = exchange(jnp.concatenate(parts, axis=1), "sub")
        if marks is None:
            named = incoming[:, -capacity:].reshape(slots, cases)
            lanes = lax.broadcasted_iota(jnp.int32, (slots, block), 1).astype(F32)
            marks = (jnp.tile(named, (1, block // cases)) == lanes).astype(F32)
        given = jnp.concatenate(
            [incoming[:, :capacity].reshape(slots, cases), incoming[:, capacity : 2 * capacity].reshape(slots, cases)],
            axis=1,
        )
        partial = lax.dot_general(marks, given, (((0,), (0,)), ((), ())), precision=HIGHEST)
        count = tail.shape[0]
        sums = jnp.sum(incoming[:, 2 * capacity : 2 * capacity + count], axis=0)
        out = jnp.concatenate(
            [
                partial[:, :cases].reshape(n_coarse, piece, cases),
                partial[:, cases:].reshape(n_coarse, piece, cases),
                jnp.broadcast_to(sums[None], (n_coarse, count, cases)),
            ],
            axis=1,
        )
        total = jnp.sum(exchange(out, "coarse"), axis=0)
        return local, marks, total[:piece].astype(BF16), total[piece : 2 * piece], total[2 * piece :]

    def coarse(rhs):
        everyone = exchange(jnp.broadcast_to(rhs[None], (n_sub,) + rhs.shape), "sub")
        product = jnp.dot(inverse_t, everyone.reshape(rows, cases), preferred_element_type=F32)
        return jnp.sum(exchange(product.reshape(n_coarse, piece, cases), "coarse"), axis=0).astype(BF16)

    start = load[0]
    residual = start.astype(F32) - facing(start).astype(F32)
    local, marks, rhs, weights, sums = forward(residual, [jnp.sum(residual * residual, axis=0)], None)
    near, norm_now = sums[0], sums[1]
    solved = coarse(rhs)
    far = jnp.sum(weights * solved.astype(F32), axis=0)
    mine = jnp.concatenate([solved, jnp.stack(in_three(far))], axis=0)
    owned = exchange(jnp.broadcast_to(mine[None], (n_coarse,) + mine.shape), "coarse")
    far = jnp.sum(owned[:, piece:].astype(F32), axis=(0, 1))
    answers = lax.dot_general(
        marks.astype(BF16), owned[:, :piece].reshape(block, cases), (((1,), (0,)), ((), ())), preferred_element_type=F32
    ).astype(BF16)
    outgoing = jnp.concatenate(
        [
            answers.reshape(n_sub, capacity, cases),
            jnp.broadcast_to(jnp.stack(in_three(far))[None], (n_sub, 3, cases)),
        ],
        axis=1,
    )
    replies = exchange(outgoing, "sub")
    far = jnp.sum(replies[:, capacity:].astype(F32), axis=(0, 1))
    curvature = near + far
    alpha = norm_now / curvature
    values = replies[:, :capacity].reshape(slots, cases)
    image = local + lax.dot_general(slotted, values, (((0,), (0,)), ((), ())), preferred_element_type=F32)
    image = image - facing(image)
    remainder = residual - alpha * image

    scalars = [jnp.sum(remainder * remainder, axis=0), jnp.sum(remainder * image, axis=0)]
    _, _, rhs, weights, sums = forward(remainder, scalars, marks)
    near, norm_next, cross = sums[0], sums[1], sums[2]
    solved = coarse(rhs)
    far = jnp.sum(weights * solved.astype(F32), axis=0)
    far = jnp.sum(exchange(jnp.broadcast_to(far[None], (n_coarse, cases)), "coarse"), axis=0)
    far = jnp.sum(exchange(jnp.broadcast_to(far[None], (n_sub, cases)), "sub"), axis=0)
    beta = norm_next / norm_now
    step = norm_next / (near + far + 2.0 * beta * cross + beta * beta * curvature)
    return ((alpha + step * beta) * residual + step * remainder)[None]


def solution(mesh):
    return jax.shard_map(
        body,
        mesh=mesh,
        in_specs=(
            P(("sub", "coarse"), None, None),
            P(("sub", "coarse"), None, None),
            P(("sub", "coarse"), None, None),
            P("coarse", "sub"),
            P(("sub", "coarse"), None),
            P(("sub", "coarse"), None),
            P(("sub", "coarse"), None, None),
            P(("sub", "coarse"), None),
        ),
        out_specs=P(("sub", "coarse"), None, None),
        check_vma=False,
    )
```

time: 861 us -> 243 us (0.28)
  waiting for transfers between devices: 325 us -> 33.3 us
  blocking collectives: 425 us -> 157 us
  starting transfers between devices: 69.9 us -> 35.3 us
  between operations: 14 us -> 0.63 us
    psum x5 -> x0, blocking collectives: 337 us -> none  [the longest x2 193 us: squares(): return lax.psum(jnp.sum(vector * vector, axis=(0, 1)), ('sub', 'coarse'))]
    reduce_scatter x2 -> x0, waiting for transfers between devices: 285 us -> none  [body(): lax.psum_scatter(jnp.dot(coarse_inverse, coarse_rhs, preferred_element_ty...]
    all_to_all x2 -> x9, blocking collectives: 49.7 us -> 157 us  [exchange(): return lax.all_to_all(blocks, axis, split_axis=0, concat_axis=0, tiled=True)]
    all_gather x2 -> x0, blocking collectives: 38.4 us -> none  [body(): lax.all_gather(share.astype(jnp.bfloat16), 'coarse', axis=0, tiled=True)]
    ppermute x10 -> x4, starting transfers between devices: 39.3 us -> 15.2 us  [the longest x2 8.14 us: facing(): lax.ppermute(ordered[half:], 'sub', [((i + 1) % n_sub, i) for i in range(...]
    ppermute x10 -> x4, waiting for transfers between devices: 15.5 us -> 4.61 us  [the longest x2 4.61 us: facing(): lax.ppermute(ordered[half:], 'sub', [((i + 1) % n_sub, i) for i in range(...]
    all_to_all x3, starting transfers between devices: 30.5 us -> 20.1 us  [exchange(): return lax.all_to_all(blocks, axis, split_axis=0, concat_axis=0, tiled=True)]
  transfers between devices with their start and end apart: 15 -> 7, of which waited for: 12 -> 4; matrix products, arithmetic and copies ran while one was open for 1% -> 0% of each run, Pallas kernels for 0% -> 0%
where the time goes in v1:
time: 243 us; the launch traced here: 242 us
  blocking collectives  157 us (65%)
  starting transfers between devices  35.3 us (15%)
  waiting for transfers between devices  33.3 us (14%)
  local copies, waits for them, and re-layouts  9.77 us (4%)
  matrix products  3.22 us (1%)
  other arithmetic  2.79 us (1%)
    all_to_all x9, blocking collectives, exchange(): return lax.all_to_all(blocks, axis, split_axis=0, concat_axis=0, tiled=True)  157 us
    all_to_all x3, waiting for transfers between devices, exchange(): return lax.all_to_all(blocks, axis, split_axis=0, concat_axis=0, tiled=True)  28.7 us
    all_to_all x3, starting transfers between devices, exchange(): return lax.all_to_all(blocks, axis, split_axis=0, concat_axis=0, tiled=True)  20.1 us
    ppermute x2, starting transfers between devices, facing(): lax.ppermute(ordered[half:], 'sub', [((i + 1) % n_sub, i) for i in range(...  8.14 us
    ppermute x2, starting transfers between devices, facing(): lax.ppermute(ordered[:half], 'sub', [(i, (i + 1) % n_sub) for i in range(...  7.02 us
  transfers between devices with their start and end apart: 7, of which 4 were waited for; matrix products, arithmetic and copies ran while one was open for 0% of the time, Pallas kernels for 0%

profile of v1, /device:TPU:1, one launch (start us, length us, event | category | flops | bytes accessed | tf_op | source)
XLA Modules:
  0.0 242.4 jit_solution(12754199215148877747)
XLA Ops:
  1.8 1.5 gather_fusion
  3.3 4.6 %collective-permute-start = (bf16[4,64,128]{2,1,0:T(8,128)(2,1)S(1)}, bf16[4,64,128]{2,1,0:T(8,128)(2,1)S(1)}, u32[]{:S(2)}, u32[]{:S(2)}) collective-permute-start(bf16[4,64,128]{2,1,0:T(8,128)(2,1)S(1)} %get-tuple-element.38), channel_id=1, source_target_pairs={{0,8},{8,16},{16,24},{24,32},{32,40},{40,48},{48,56},{56,64},{64,7... | collective-permute-start | bytes 196616 | tf_op jit(solution)/shard_map/ppermute | solution.py:54
  8.0 6.2 %collective-permute-start.1 = (bf16[4,64,128]{2,1,0:T(8,128)(2,1)S(1)}, bf16[4,64,128]{2,1,0:T(8,128)(2,1)S(1)}, u32[]{:S(2)}, u32[]{:S(2)}) collective-permute-start(bf16[4,64,128]{2,1,0:T(8,128)(2,1)S(1)} %get-tuple-element.39), channel_id=1, source_target_pairs={{8,0},{16,8},{24,16},{32,24},{40,32},{48,40},{56,48},{64,56},{72,6... | collective-permute-start | bytes 196616 | tf_op jit(solution)/shard_map/ppermute | solution.py:55
  16.6 1.0 copy-done.1
  18.4 0.8 pad_maximum_fusion.2
  19.2 13.4 %all-to-all-start = ((f32[64,8,128]{2,1,0:T(8,128)}), f32[64,8,128]{2,1,0:T(8,128)S(1)}, u32[]{:S(2)}, u32[]{:S(2)}) async-start(f32[64,8,128]{2,1,0:T(8,128)} %pad_maximum_fusion.2), calls=%async_computation | async-start | bytes 524288 | tf_op jit(solution)/shard_map/all_to_all | solution.py:11
  32.6 13.2 %all-to-all-done = f32[64,8,128]{2,1,0:T(8,128)S(1)} async-done(((f32[64,8,128]{2,1,0:T(8,128)}), f32[64,8,128]{2,1,0:T(8,128)S(1)}, u32[]{:S(2)}, u32[]{:S(2)}) %all-to-all-start) | async-done | bytes 262176 | tf_op jit(solution)/shard_map/all_to_all | solution.py:11
  46.4 19.0 %all_to_all.62 = f32[8,66,128]{2,1,0:T(8,128)S(1)} all-to-all(f32[8,66,128]{2,1,0:T(8,128)S(1)} %pad_maximum_fusion), channel_id=1, replica_groups=mesh['sub'=64,'coarse'=8] {'coarse'}, dimensions={0} | all-to-all | bytes 540672 | tf_op jit(solution)/shard_map/all_to_all | solution.py:11
  65.5 22.8 %all_to_all.63 = bf16[64,32,128]{2,1,0:T(8,128)(2,1)S(1)} all-to-all(bf16[64,32,128]{2,1,0:T(8,128)(2,1)S(1)} %broadcast_in_dim.67), channel_id=1, replica_groups=mesh['sub'=64,'coarse'=8] {'sub'}, dimensions={0} | all-to-all | bytes 1048576 | tf_op jit(solution)/shard_map/all_to_all | solution.py:11
  89.4 3.4 %all-to-all-start.3 = ((f32[8,32,128]{2,1,0:T(8,128)}), f32[8,32,128]{2,1,0:T(8,128)S(1)}, u32[]{:S(2)}, u32[]{:S(2)}) async-start(f32[8,32,128]{2,1,0:T(8,128)} %bitcast.31), calls=%async_computation.3 | async-start | bytes 262144 | tf_op jit(solution)/shard_map/all_to_all | solution.py:11
  92.8 8.2 %all-to-all-done.3 = f32[8,32,128]{2,1,0:T(8,128)S(1)} async-done(((f32[8,32,128]{2,1,0:T(8,128)}), f32[8,32,128]{2,1,0:T(8,128)S(1)}, u32[]{:S(2)}, u32[]{:S(2)}) %all-to-all-start.3) | async-done | bytes 131104 | tf_op jit(solution)/shard_map/all_to_all | solution.py:11
  101.8 3.4 %all-to-all-start.4 = ((bf16[8,35,128]{2,1,0:T(8,128)(2,1)}), bf16[8,35,128]{2,1,0:T(8,128)(2,1)S(1)}, u32[]{:S(2)}, u32[]{:S(2)}) async-start(bf16[8,35,128]{2,1,0:T(8,128)(2,1)} %broadcast_in_dim.68), calls=%async_computation.4 | async-start | bytes 163840 | tf_op jit(solution)/shard_map/all_to_all | solution.py:11
  105.2 7.3 %all-to-all-done.4 = bf16[8,35,128]{2,1,0:T(8,128)(2,1)S(1)} async-done(((bf16[8,35,128]{2,1,0:T(8,128)(2,1)}), bf16[8,35,128]{2,1,0:T(8,128)(2,1)S(1)}, u32[]{:S(2)}, u32[]{:S(2)}) %all-to-all-start.4) | async-done | bytes 71712 | tf_op jit(solution)/shard_map/all_to_all | solution.py:11
  112.8 18.7 %all_to_all.64 = bf16[64,5,128]{2,1,0:T(8,128)(2,1)S(1)} all-to-all(bf16[64,5,128]{2,1,0:T(8,128)(2,1)S(1)} %pad_maximum_fusion.6), channel_id=1, replica_groups=mesh['sub'=64,'coarse'=8] {'sub'}, dimensions={0} | all-to-all | bytes 163840 | tf_op jit(solution)/shard_map/all_to_all | solution.py:11
  132.6 2.4 collective-permute-start.2
  135.0 1.9 collective-permute-start.3
  136.9 4.6 %collective-permute-done.3 = f32[4,64,128]{2,1,0:T(8,128)S(1)} collective-permute-done((f32[4,64,128]{2,1,0:T(8,128)S(1)}, f32[4,64,128]{2,1,0:T(8,128)S(1)}, u32[]{:S(2)}, u32[]{:S(2)}) %collective-permute-start.3) | collective-permute-done | bytes 131104 | tf_op jit(solution)/shard_map/ppermute | solution.py:55
  143.3 22.8 %all_to_all.65 = f32[64,7,128]{2,1,0:T(8,128)S(1)} all-to-all(f32[64,7,128]{2,1,0:T(8,128)S(1)} %pad_maximum_fusion.4), channel_id=1, replica_groups=mesh['sub'=64,'coarse'=8] {'sub'}, dimensions={0} | all-to-all | bytes 458752 | tf_op jit(solution)/shard_map/all_to_all | solution.py:11
  166.6 15.1 %all_to_all.66 = f32[8,67,128]{2,1,0:T(8,128)S(1)} all-to-all(f32[8,67,128]{2,1,0:T(8,128)S(1)} %pad_maximum_fusion.1), channel_id=1, replica_groups=mesh['sub'=64,'coarse'=8] {'coarse'}, dimensions={0} | all-to-all | bytes 548864 | tf_op jit(solution)/shard_map/all_to_all | solution.py:11
  181.8 22.5 %all_to_all.67 = bf16[64,32,128]{2,1,0:T(8,128)(2,1)S(1)} all-to-all(bf16[64,32,128]{2,1,0:T(8,128)(2,1)S(1)} %broadcast_in_dim.72), channel_id=1, replica_groups=mesh['sub'=64,'coarse'=8] {'sub'}, dimensions={0} | all-to-all | bytes 1048576 | tf_op jit(solution)/shard_map/all_to_all | solution.py:11
  204.8 10.8 %all_to_all.68 = f32[8,32,128]{2,1,0:T(8,128)S(1)} all-to-all(f32[8,32,128]{2,1,0:T(8,128)S(1)} %bitcast.171), channel_id=1, replica_groups=mesh['sub'=64,'coarse'=8] {'coarse'}, dimensions={0} | all-to-all | bytes 262144 | tf_op jit(solution)/shard_map/all_to_all | solution.py:11
  215.6 8.9 %all_to_all.69 = f32[8,1,128]{2,1,0:T(1,128)S(1)} all-to-all(f32[8,1,128]{2,1,0:T(1,128)S(1)} %broadcast_in_dim.73), channel_id=1, replica_groups=mesh['sub'=64,'coarse'=8] {'coarse'}, dimensions={0} | all-to-all | bytes 8192 | tf_op jit(solution)/shard_map/all_to_all | solution.py:11
  224.5 16.9 %all_to_all.70 = f32[64,1,128]{2,1,0:T(1,128)S(1)} all-to-all(f32[64,1,128]{2,1,0:T(1,128)S(1)} %broadcast_in_dim.74), channel_id=1, replica_groups=mesh['sub'=64,'coarse'=8] {'sub'}, dimensions={0} | all-to-all | bytes 65536 | tf_op jit(solution)/shard_map/all_to_all | solution.py:11
  241.6 0.8 copy.101
  (114 shorter events, 11.7 us)
Async XLA Ops:
  0.0 88.3 %copy-start = (bf16[2048,256]{1,0:T(8,128)(2,1)S(1)}, bf16[2048,256]{1,0:T(8,128)(2,1)}, u32[]{:S(2)}) copy-start(bf16[2048,256]{1,0:T(8,128)(2,1)} %param.11) | copy-start | bytes 3145732
  0.0 0.7 copy-start.5
  0.8 0.7 copy-start.4
  3.3 10.9 %copy-start.2 = (bf16[1,512,128]{2,1,0:T(8,128)(2,1)S(1)}, bf16[1,512,128]{2,1,0:T(8,128)(2,1)}, u32[]{:S(2)}) copy-start(bf16[1,512,128]{2,1,0:T(8,128)(2,1)} %param.8) | copy-start | bytes 393220
  3.3 12.3 %collective-permute-start = (bf16[4,64,128]{2,1,0:T(8,128)(2,1)S(1)}, bf16[4,64,128]{2,1,0:T(8,128)(2,1)S(1)}, u32[]{:S(2)}, u32[]{:S(2)}) collective-permute-start(bf16[4,64,128]{2,1,0:T(8,128)(2,1)S(1)} %get-tuple-element.38), channel_id=1, source_target_pairs={{0,8},{8,16},{16,24},{24,32},{32,40},{40,48},{48,56},{56,64},{64,7... | collective-permute-start | bytes 196616 | tf_op jit(solution)/shard_map/ppermute | solution.py:54
  8.0 6.4 %copy-start.6 = (s32[1,24]{1,0:T(1,128)S(1)}, s32[1,24]{1,0:T(1,128)}, u32[]{:S(2)}) copy-start(s32[1,24]{1,0:T(1,128)} %param.15) | copy-start | bytes 292
  8.0 7.7 %collective-permute-start.1 = (bf16[4,64,128]{2,1,0:T(8,128)(2,1)S(1)}, bf16[4,64,128]{2,1,0:T(8,128)(2,1)S(1)}, u32[]{:S(2)}, u32[]{:S(2)}) collective-permute-start(bf16[4,64,128]{2,1,0:T(8,128)(2,1)S(1)} %get-tuple-element.39), channel_id=1, source_target_pairs={{8,0},{16,8},{24,16},{32,24},{40,32},{48,40},{56,48},{64,56},{72,6... | collective-permute-start | bytes 196616 | tf_op jit(solution)/shard_map/ppermute | solution.py:55
  14.2 0.7 copy-start.7
  14.4 1.0 copy-start.3
  16.6 1.0 copy-start.1
  19.2 26.5 %all-to-all-start = ((f32[64,8,128]{2,1,0:T(8,128)}), f32[64,8,128]{2,1,0:T(8,128)S(1)}, u32[]{:S(2)}, u32[]{:S(2)}) async-start(f32[64,8,128]{2,1,0:T(8,128)} %pad_maximum_fusion.2), calls=%async_computation | async-start | bytes 524288 | tf_op jit(solution)/shard_map/all_to_all | solution.py:11
  89.4 11.6 %all-to-all-start.3 = ((f32[8,32,128]{2,1,0:T(8,128)}), f32[8,32,128]{2,1,0:T(8,128)S(1)}, u32[]{:S(2)}, u32[]{:S(2)}) async-start(f32[8,32,128]{2,1,0:T(8,128)} %bitcast.31), calls=%async_computation.3 | async-start | bytes 262144 | tf_op jit(solution)/shard_map/all_to_all | solution.py:11
  101.8 10.7 %all-to-all-start.4 = ((bf16[8,35,128]{2,1,0:T(8,128)(2,1)}), bf16[8,35,128]{2,1,0:T(8,128)(2,1)S(1)}, u32[]{:S(2)}, u32[]{:S(2)}) async-start(bf16[8,35,128]{2,1,0:T(8,128)(2,1)} %broadcast_in_dim.68), calls=%async_computation.4 | async-start | bytes 163840 | tf_op jit(solution)/shard_map/all_to_all | solution.py:11
  132.6 4.4 %collective-permute-start.2 = (f32[4,64,128]{2,1,0:T(8,128)S(1)}, f32[4,64,128]{2,1,0:T(8,128)S(1)}, u32[]{:S(2)}, u32[]{:S(2)}) collective-permute-start(f32[4,64,128]{2,1,0:T(8,128)S(1)} %get-tuple-element.25), channel_id=1, source_target_pairs={{0,8},{8,16},{16,24},{24,32},{32,40},{40,48},{48,56},{56,64},{64,7... | collective-permute-start | bytes 393224 | tf_op jit(solution)/shard_map/ppermute | solution.py:54
  135.0 6.6 %collective-permute-start.3 = (f32[4,64,128]{2,1,0:T(8,128)S(1)}, f32[4,64,128]{2,1,0:T(8,128)S(1)}, u32[]{:S(2)}, u32[]{:S(2)}) collective-permute-start(f32[4,64,128]{2,1,0:T(8,128)S(1)} %get-tuple-element.26), channel_id=1, source_target_pairs={{8,0},{16,8},{24,16},{32,24},{40,32},{48,40},{56,48},{64,56},{72,6... | collective-permute-start | bytes 393224 | tf_op jit(solution)/shard_map/ppermute | solution.py:55

commit v2 on v1

v2 whole, which is shorter than its diff:
```python
import jax
import jax.numpy as jnp
from jax import lax
from jax.sharding import PartitionSpec as P

HIGHEST = lax.Precision.HIGHEST
F32, BF16 = jnp.float32, jnp.bfloat16


def exchange(blocks, axis):
    return lax.all_to_all(blocks, axis, split_axis=0, concat_axis=0, tiled=True)


def in_two(value):
    high = lax.reduce_precision(value, 8, 7)
    return jnp.stack([high, value - high]).astype(BF16)


def body(
    load,
    schur,
    coupling,
    coarse_inverse,
    neighbour_sub,
    neighbour_edge,
    primal_owner,
    primal_offset,
):
    _, order, cases = load.shape
    edges = neighbour_sub.shape[1]
    width = order // edges
    half = edges // 2
    rows, block = coarse_inverse.shape
    n_sub, n_coarse = lax.axis_size("sub"), lax.axis_size("coarse")
    piece = block // n_coarse
    capacity = 2
    slots = n_sub * capacity
    sub_index, coarse_index = lax.axis_index("sub"), lax.axis_index("coarse")

    faces_next = (neighbour_sub[0] // n_coarse - sub_index) % n_sub == 1
    edge_at = neighbour_edge[0]
    same_side = faces_next[:, None] == faces_next[None, :]
    ids = jnp.arange(edges, dtype=jnp.int32)
    from_place = jnp.sum((same_side & (edge_at[None, :] < edge_at[:, None])).astype(jnp.int32), axis=1)
    from_place = from_place + jnp.where(faces_next, half, 0)
    to_place = jnp.sum((same_side & (ids[None, :] < ids[:, None])).astype(jnp.int32), axis=1)
    to_place = to_place + jnp.where(faces_next, 0, half)
    send_order = jnp.sum(jnp.where(to_place[None, :] == ids[:, None], ids[None, :], 0), axis=1)

    def facing(field):
        ordered = field.reshape(edges, width, cases)[send_order]
        from_before = lax.ppermute(ordered[:half], "sub", [(i, (i + 1) % n_sub) for i in range(n_sub)])
        from_next = lax.ppermute(ordered[half:], "sub", [((i + 1) % n_sub, i) for i in range(n_sub)])
        both = jnp.concatenate([from_before, from_next], axis=0)
        return both[from_place].reshape(order, cases)

    owners = primal_owner.reshape(-1)
    offsets = primal_offset.reshape(-1)
    prims = owners.shape[0]
    row_ids = jnp.arange(prims, dtype=jnp.int32)
    earlier = (owners[:, None] == owners[None, :]) & (row_ids[None, :] < row_ids[:, None])
    slot_of = owners * capacity + jnp.sum(earlier.astype(jnp.int32), axis=1)
    placed = jnp.arange(slots, dtype=jnp.int32)[:, None] == slot_of[None, :]
    slotted = jnp.dot(placed.astype(BF16), coupling[0], preferred_element_type=F32).astype(BF16)
    slot_offset = jnp.sum(jnp.where(placed, offsets[None, :] + 1, 0), axis=1) - 1

    def contributions(field):
        twice = 2.0 * field
        jumps = twice.astype(BF16)
        rest = (twice - jumps.astype(F32)).astype(BF16)
        local = jnp.dot(schur[0], jumps, preferred_element_type=F32)
        near = jnp.sum(twice * local, axis=0)
        terms = jnp.dot(slotted, jnp.concatenate([jumps, rest], axis=1), preferred_element_type=F32)
        rounded, whole = terms[:, :cases], terms[:, :cases] + terms[:, cases:]
        by_owner = (n_sub, capacity, cases)
        return local, near, rounded.reshape(by_owner), whole.reshape(by_owner)

    chips = n_sub // 2
    same_core = [[2 * chip + core for chip in range(chips)] for core in range(2)]
    other_core = [(i, i ^ 1) for i in range(n_sub)]

    def product(rhs):
        mine = lax.all_to_all(
            jnp.broadcast_to(rhs[None], (chips,) + rhs.shape), "sub", 0, 0, tiled=True, axis_index_groups=same_core
        )
        theirs = lax.ppermute(mine, "sub", other_core)
        both = jnp.where(
            sub_index % 2 == 0, jnp.concatenate([mine, theirs], axis=1), jnp.concatenate([theirs, mine], axis=1)
        )
        return lax.dot_general(
            coarse_inverse, both.reshape(rows, cases), (((0,), (0,)), ((), ())), preferred_element_type=F32
        )

    start = load[0]
    residual = start.astype(F32) - facing(start).astype(F32)
    local, near, rounded, whole = contributions(residual)
    marked = jnp.broadcast_to(slot_offset.astype(F32).reshape(n_sub, capacity, 1), (n_sub, capacity, cases))
    scalars = jnp.stack([near, jnp.sum(residual * residual, axis=0)])
    incoming = exchange(
        jnp.concatenate([rounded, whole, marked, jnp.broadcast_to(scalars[None], (n_sub, 2, cases))], axis=1), "sub"
    )
    named = incoming[:, 2 * capacity : 3 * capacity].reshape(slots, cases)
    lanes = lax.broadcasted_iota(jnp.int32, (slots, block), 1).astype(F32)
    marks = (jnp.tile(named, (1, block // cases)) == lanes).astype(F32)
    given = jnp.concatenate(
        [incoming[:, :capacity].reshape(slots, cases), incoming[:, capacity : 2 * capacity].reshape(slots, cases)], axis=1
    )
    partial = lax.dot_general(marks, given, (((0,), (0,)), ((), ())), precision=HIGHEST)
    sums = jnp.sum(incoming[:, 3 * capacity :], axis=0)
    total = exchange(
        jnp.concatenate(
            [
                partial[:, :cases].reshape(n_coarse, piece, cases),
                partial[:, cases:].reshape(n_coarse, piece, cases),
                jnp.broadcast_to(sums[None], (n_coarse, 2, cases)),
            ],
            axis=1,
        ),
        "coarse",
    )
    total = jnp.sum(total, axis=0)
    weights, near, norm_now = total[piece : 2 * piece], total[2 * piece], total[2 * piece + 1]
    share = product(total[:piece].astype(BF16))
    solved = jnp.sum(exchange(share.reshape(n_coarse, piece, cases), "coarse"), axis=0).astype(BF16)
    far = jnp.sum(weights * solved.astype(F32), axis=0)
    mine = jnp.concatenate([solved, in_two(far)], axis=0)
    owned = exchange(jnp.broadcast_to(mine[None], (n_coarse,) + mine.shape), "coarse")
    far = jnp.sum(owned[:, piece:].astype(F32), axis=(0, 1))
    answers = jnp.dot(
        marks.astype(BF16), owned[:, :piece].reshape(block, cases), preferred_element_type=F32
    ).astype(BF16)
    replies = exchange(
        jnp.concatenate(
            [answers.reshape(n_sub, capacity, cases), jnp.broadcast_to(in_two(far)[None], (n_sub, 2, cases))], axis=1
        ),
        "sub",
    )
    curvature = near + jnp.sum(replies[:, capacity:].astype(F32), axis=(0, 1))
    alpha = norm_now / curvature
    values = replies[:, :capacity].reshape(slots, cases)
    image = local + lax.dot_general(slotted, values, (((0,), (0,)), ((), ())), preferred_element_type=F32)
    image = image - facing(image)
    remainder = residual - alpha * image

    _, near, _, whole = contributions(remainder)
    incoming = exchange(whole, "sub").reshape(slots, cases)
    partial = lax.dot_general(marks, incoming, (((0,), (0,)), ((), ())), precision=HIGHEST).astype(BF16)
    partial = exchange(jnp.broadcast_to(partial[None], (n_coarse, block, cases)), "coarse")
    weights = jnp.sum(partial.astype(F32), axis=0)
    rhs = lax.dynamic_slice_in_dim(weights, coarse_index * piece, piece, axis=0).astype(BF16)
    scalars = jnp.stack([near + jnp.sum(weights * product(rhs), axis=0), jnp.sum(remainder * remainder, axis=0)])
    scalars = jnp.sum(exchange(jnp.broadcast_to(scalars[None], (n_coarse, 2, cases)), "coarse"), axis=0)
    scalars = jnp.sum(exchange(jnp.broadcast_to(scalars[None], (n_sub, 2, cases)), "sub"), axis=0)
    beta = scalars[1] / norm_now
    step = scalars[1] / (scalars[0] - beta * beta * curvature)
    return ((alpha + step * beta) * residual + step * remainder)[None]


def solution(mesh):
    return jax.shard_map(
        body,
        mesh=mesh,
        in_specs=(
            P(("sub", "coarse"), None, None),
            P(("sub", "coarse"), None, None),
            P(("sub", "coarse"), None, None),
            P("coarse", "sub"),
            P(("sub", "coarse"), None),
            P(("sub", "coarse"), None),
            P(("sub", "coarse"), None, None),
            P(("sub", "coarse"), None),
        ),
        out_specs=P(("sub", "coarse"), None, None),
        check_vma=False,
    )
```

time: 243 us -> 228 us (0.938)
  blocking collectives: 157 us -> 108 us
  waiting for transfers between devices: 33.3 us -> 54.1 us
  starting transfers between devices: 35.3 us -> 46.5 us
    all_to_all x9 -> x5, blocking collectives: 157 us -> 79.5 us  [exchange(): return lax.all_to_all(blocks, axis, split_axis=0, concat_axis=0, tiled=True)]
    all_to_all x0 -> x2, blocking collectives: none -> 28.5 us  [product(): lax.all_to_all(jnp.broadcast_to(rhs[None], (chips,) + rhs.shape), 'sub',...]
    all_to_all x3 -> x4, waiting for transfers between devices: 28.7 us -> 46.7 us  [exchange(): return lax.all_to_all(blocks, axis, split_axis=0, concat_axis=0, tiled=True)]
    ppermute x0 -> x2, starting transfers between devices: none -> 9.61 us  [product(): theirs = lax.ppermute(mine, 'sub', other_core)]
    ppermute x2, waiting for transfers between devices: 0.01 us -> 5.01 us  [facing(): lax.ppermute(ordered[:half], 'sub', [(i, (i + 1) % n_sub) for i in range(...]
    ppermute x2, waiting for transfers between devices: 4.61 us -> 0.62 us  [facing(): lax.ppermute(ordered[half:], 'sub', [((i + 1) % n_sub, i) for i in range(...]
    ppermute x2, starting transfers between devices: 8.14 us -> 11.2 us  [facing(): lax.ppermute(ordered[half:], 'sub', [((i + 1) % n_sub, i) for i in range(...]
    all_to_all x3 -> x4, starting transfers between devices: 20.1 us -> 20.5 us  [exchange(): return lax.all_to_all(blocks, axis, split_axis=0, concat_axis=0, tiled=True)]
  transfers between devices with their start and end apart: 7 -> 10, of which waited for: 4 -> 9; matrix products, arithmetic and copies ran while one was open for 0% -> 1% of each run, Pallas kernels for 0% -> 0%
where the time goes in v2:
time: 228 us; the launch traced here: 227 us
  blocking collectives  108 us (47%)
  waiting for transfers between devices  54.1 us (24%)
  starting transfers between devices  46.5 us (20%)
  local copies, waits for them, and re-layouts  11.3 us (5%)
  matrix products  3.2 us (1%)
  other arithmetic  3.14 us (1%)
    all_to_all x5, blocking collectives, exchange(): return lax.all_to_all(blocks, axis, split_axis=0, concat_axis=0, tiled=True)  79.5 us
    all_to_all x4, waiting for transfers between devices, exchange(): return lax.all_to_all(blocks, axis, split_axis=0, concat_axis=0, tiled=True)  46.7 us
    all_to_all x2, blocking collectives, product(): lax.all_to_all(jnp.broadcast_to(rhs[None], (chips,) + rhs.shape), 'sub',...  28.5 us
    all_to_all x4, starting transfers between devices, exchange(): return lax.all_to_all(blocks, axis, split_axis=0, concat_axis=0, tiled=True)  20.5 us
    ppermute x2, starting transfers between devices, facing(): lax.ppermute(ordered[half:], 'sub', [((i + 1) % n_sub, i) for i in range(...  11.2 us
    ppermute x2, starting transfers between devices, product(): theirs = lax.ppermute(mine, 'sub', other_core)  9.61 us
    ppermute x2, starting transfers between devices, facing(): lax.ppermute(ordered[:half], 'sub', [(i, (i + 1) % n_sub) for i in range(...  5.18 us
    ppermute x2, waiting for transfers between devices, facing(): lax.ppermute(ordered[:half], 'sub', [(i, (i + 1) % n_sub) for i in range(...  5.01 us
  transfers between devices with their start and end apart: 10, of which 9 were waited for; matrix products, arithmetic and copies ran while one was open for 1% of the time, Pallas kernels for 0%

profile of v2, /device:TPU:1, one launch (start us, length us, event | category | flops | bytes accessed | tf_op | source)
XLA Modules:
  0.0 226.9 jit_solution(5739971824647497204)
XLA Ops:
  1.8 1.5 gather_fusion
  3.3 8.9 %collective-permute-start.1 = (bf16[4,64,128]{2,1,0:T(8,128)(2,1)S(1)}, bf16[4,64,128]{2,1,0:T(8,128)(2,1)S(1)}, u32[]{:S(2)}, u32[]{:S(2)}) collective-permute-start(bf16[4,64,128]{2,1,0:T(8,128)(2,1)S(1)} %get-tuple-element.33), channel_id=1, source_target_pairs={{8,0},{16,8},{24,16},{32,24},{40,32},{48,40},{56,48},{64,56},{72,6... | collective-permute-start | bytes 196616 | tf_op jit(solution)/shard_map/ppermute | solution.py:53
  12.3 1.9 collective-permute-start
  16.4 3.8 %collective-permute-done = bf16[4,64,128]{2,1,0:T(8,128)(2,1)S(1)} collective-permute-done((bf16[4,64,128]{2,1,0:T(8,128)(2,1)S(1)}, bf16[4,64,128]{2,1,0:T(8,128)(2,1)S(1)}, u32[]{:S(2)}, u32[]{:S(2)}) %collective-permute-start) | collective-permute-done | bytes 65568 | tf_op jit(solution)/shard_map/ppermute | solution.py:52
  23.8 10.3 %all-to-all-start = ((f32[64,8,128]{2,1,0:T(8,128)}), f32[64,8,128]{2,1,0:T(8,128)S(1)}, u32[]{:S(2)}, u32[]{:S(2)}) async-start(f32[64,8,128]{2,1,0:T(8,128)} %pad_maximum_fusion.1), calls=%async_computation | async-start | bytes 524288 | tf_op jit(solution)/shard_map/all_to_all | solution.py:11
  34.1 13.2 %all-to-all-done = f32[64,8,128]{2,1,0:T(8,128)S(1)} async-done(((f32[64,8,128]{2,1,0:T(8,128)}), f32[64,8,128]{2,1,0:T(8,128)S(1)}, u32[]{:S(2)}, u32[]{:S(2)}) %all-to-all-start) | async-done | bytes 262176 | tf_op jit(solution)/shard_map/all_to_all | solution.py:11
  48.0 19.0 %all_to_all.55 = f32[8,66,128]{2,1,0:T(8,128)S(1)} all-to-all(f32[8,66,128]{2,1,0:T(8,128)S(1)} %pad_maximum_fusion), channel_id=1, replica_groups=mesh['sub'=64,'coarse'=8] {'coarse'}, dimensions={0} | all-to-all | bytes 540672 | tf_op jit(solution)/shard_map/all_to_all | solution.py:11
  67.1 13.8 %all_to_all.56 = bf16[32,32,128]{2,1,0:T(8,128)(2,1)S(1)} all-to-all(bf16[32,32,128]{2,1,0:T(8,128)(2,1)S(1)} %broadcast_in_dim.65), channel_id=1, replica_groups={{0,16,32,48,64,80,96,112,128,144,160,176,192,208,224,240,256,272,288,30..., dimensions={0} | all-to-all | bytes 524288 | tf_op jit(solution)/shard_map/all_to_all | solution.py:83
  80.8 5.6 %collective-permute-start.2 = (bf16[32,32,128]{2,1,0:T(8,128)(2,1)S(1)}, bf16[32,32,128]{2,1,0:T(8,128)(2,1)S(1)}, u32[]{:S(2)}, u32[]{:S(2)}) collective-permute-start(bf16[32,32,128]{2,1,0:T(8,128)(2,1)S(1)} %all_to_all.56), channel_id=1, source_target_pairs={{0,8},{8,0},{16,24},{24,16},{32,40},{40,32},{48,56},{56,48},{64,72... | collective-permute-start | bytes 786440 | tf_op jit(solution)/shard_map/ppermute | solution.py:86
  88.8 3.4 %all-to-all-start.3 = ((f32[8,32,128]{2,1,0:T(8,128)}), f32[8,32,128]{2,1,0:T(8,128)S(1)}, u32[]{:S(2)}, u32[]{:S(2)}) async-start(f32[8,32,128]{2,1,0:T(8,128)} %bitcast.33), calls=%async_computation.3 | async-start | bytes 262144 | tf_op jit(solution)/shard_map/all_to_all | solution.py:11
  92.2 8.3 %all-to-all-done.3 = f32[8,32,128]{2,1,0:T(8,128)S(1)} async-done(((f32[8,32,128]{2,1,0:T(8,128)}), f32[8,32,128]{2,1,0:T(8,128)S(1)}, u32[]{:S(2)}, u32[]{:S(2)}) %all-to-all-start.3) | async-done | bytes 131104 | tf_op jit(solution)/shard_map/all_to_all | solution.py:11
  101.2 3.4 %all-to-all-start.4 = ((bf16[8,34,128]{2,1,0:T(8,128)(2,1)}), bf16[8,34,128]{2,1,0:T(8,128)(2,1)S(1)}, u32[]{:S(2)}, u32[]{:S(2)}) async-start(bf16[8,34,128]{2,1,0:T(8,128)(2,1)} %broadcast_in_dim.66), calls=%async_computation.4 | async-start | bytes 163840 | tf_op jit(solution)/shard_map/all_to_all | solution.py:11
  104.7 7.2 %all-to-all-done.4 = bf16[8,34,128]{2,1,0:T(8,128)(2,1)S(1)} async-done(((bf16[8,34,128]{2,1,0:T(8,128)(2,1)}), bf16[8,34,128]{2,1,0:T(8,128)(2,1)S(1)}, u32[]{:S(2)}, u32[]{:S(2)}) %all-to-all-start.4) | async-done | bytes 69664 | tf_op jit(solution)/shard_map/all_to_all | solution.py:11
  112.3 16.5 %all_to_all.57 = bf16[64,4,128]{2,1,0:T(4,128)(2,1)S(1)} all-to-all(bf16[64,4,128]{2,1,0:T(4,128)(2,1)S(1)} %pad_maximum_fusion.4), channel_id=1, replica_groups=mesh['sub'=64,'coarse'=8] {'sub'}, dimensions={0} | all-to-all | bytes 131072 | tf_op jit(solution)/shard_map/all_to_all | solution.py:11
  129.8 2.3 %collective-permute-start.4 = (f32[4,64,128]{2,1,0:T(8,128)S(1)}, f32[4,64,128]{2,1,0:T(8,128)S(1)}, u32[]{:S(2)}, u32[]{:S(2)}) collective-permute-start(f32[4,64,128]{2,1,0:T(8,128)S(1)} %get-tuple-element.22), channel_id=1, source_target_pairs={{8,0},{16,8},{24,16},{32,24},{40,32},{48,40},{56,48},{64,56},{72,6... | collective-permute-start | bytes 393224 | tf_op jit(solution)/shard_map/ppermute | solution.py:53
  132.1 3.3 %collective-permute-start.3 = (f32[4,64,128]{2,1,0:T(8,128)S(1)}, f32[4,64,128]{2,1,0:T(8,128)S(1)}, u32[]{:S(2)}, u32[]{:S(2)}) collective-permute-start(f32[4,64,128]{2,1,0:T(8,128)S(1)} %get-tuple-element.21), channel_id=1, source_target_pairs={{0,8},{8,16},{16,24},{24,32},{32,40},{40,48},{48,56},{56,64},{64,7... | collective-permute-start | bytes 393224 | tf_op jit(solution)/shard_map/ppermute | solution.py:52
  136.0 1.2 collective-permute-done.3
  138.5 19.8 %all_to_all.58 = f32[64,2,128]{2,1,0:T(2,128)S(1)} all-to-all(f32[64,2,128]{2,1,0:T(2,128)S(1)} %bitcast.152), channel_id=1, replica_groups=mesh['sub'=64,'coarse'=8] {'sub'}, dimensions={0} | all-to-all | bytes 131072 | tf_op jit(solution)/shard_map/all_to_all | solution.py:11
  159.3 3.5 %all-to-all-start.7 = ((bf16[8,256,128]{2,1,0:T(8,128)(2,1)}), bf16[8,256,128]{2,1,0:T(8,128)(2,1)S(1)}, u32[]{:S(2)}, u32[]{:S(2)}) async-start(bf16[8,256,128]{2,1,0:T(8,128)(2,1)} %broadcast_in_dim.68), calls=%async_computation.7 | async-start | bytes 1048576 | tf_op jit(solution)/shard_map/all_to_all | solution.py:11
  162.8 17.9 %all-to-all-done.7 = bf16[8,256,128]{2,1,0:T(8,128)(2,1)S(1)} async-done(((bf16[8,256,128]{2,1,0:T(8,128)(2,1)}), bf16[8,256,128]{2,1,0:T(8,128)(2,1)S(1)}, u32[]{:S(2)}, u32[]{:S(2)}) %all-to-all-start.7) | async-done | bytes 524320 | tf_op jit(solution)/shard_map/all_to_all | solution.py:11
  180.9 14.8 %all_to_all.59 = bf16[32,32,128]{2,1,0:T(8,128)(2,1)S(1)} all-to-all(bf16[32,32,128]{2,1,0:T(8,128)(2,1)S(1)} %broadcast_in_dim.69), channel_id=1, replica_groups={{0,16,32,48,64,80,96,112,128,144,160,176,192,208,224,240,256,272,288,30..., dimensions={0} | all-to-all | bytes 524288 | tf_op jit(solution)/shard_map/all_to_all | solution.py:83
  195.6 4.0 %collective-permute-start.5 = (bf16[32,32,128]{2,1,0:T(8,128)(2,1)S(1)}, bf16[32,32,128]{2,1,0:T(8,128)(2,1)S(1)}, u32[]{:S(2)}, u32[]{:S(2)}) collective-permute-start(bf16[32,32,128]{2,1,0:T(8,128)(2,1)S(1)} %all_to_all.59), channel_id=1, source_target_pairs={{0,8},{8,0},{16,24},{24,16},{32,40},{40,32},{48,56},{56,48},{64,72... | collective-permute-start | bytes 786440 | tf_op jit(solution)/shard_map/ppermute | solution.py:86
  201.4 8.9 %all_to_all.60 = f32[8,2,128]{2,1,0:T(2,128)S(1)} all-to-all(f32[8,2,128]{2,1,0:T(2,128)S(1)} %broadcast_in_dim.70), channel_id=1, replica_groups=mesh['sub'=64,'coarse'=8] {'coarse'}, dimensions={0} | all-to-all | bytes 16384 | tf_op jit(solution)/shard_map/all_to_all | solution.py:11
  210.4 15.4 %all_to_all.61 = f32[64,2,128]{2,1,0:T(2,128)S(1)} all-to-all(f32[64,2,128]{2,1,0:T(2,128)S(1)} %broadcast_in_dim.71), channel_id=1, replica_groups=mesh['sub'=64,'coarse'=8] {'sub'}, dimensions={0} | all-to-all | bytes 131072 | tf_op jit(solution)/shard_map/all_to_all | solution.py:11
  (112 shorter events, 18.5 us)
Async XLA Ops:
  0.0 87.7 %copy-start = (bf16[2048,256]{1,0:T(8,128)(2,1)S(1)}, bf16[2048,256]{1,0:T(8,128)(2,1)}, u32[]{:S(2)}) copy-start(bf16[2048,256]{1,0:T(8,128)(2,1)} %param.11) | copy-start | bytes 3145732
  0.0 0.7 copy-start.5
  0.8 0.7 copy-start.4
  3.3 10.9 %copy-start.2 = (bf16[1,512,128]{2,1,0:T(8,128)(2,1)S(1)}, bf16[1,512,128]{2,1,0:T(8,128)(2,1)}, u32[]{:S(2)}) copy-start(bf16[1,512,128]{2,1,0:T(8,128)(2,1)} %param.8) | copy-start | bytes 393220
  3.3 13.1 %collective-permute-start.1 = (bf16[4,64,128]{2,1,0:T(8,128)(2,1)S(1)}, bf16[4,64,128]{2,1,0:T(8,128)(2,1)S(1)}, u32[]{:S(2)}, u32[]{:S(2)}) collective-permute-start(bf16[4,64,128]{2,1,0:T(8,128)(2,1)S(1)} %get-tuple-element.33), channel_id=1, source_target_pairs={{8,0},{16,8},{24,16},{32,24},{40,32},{48,40},{56,48},{64,56},{72,6... | collective-permute-start | bytes 196616 | tf_op jit(solution)/shard_map/ppermute | solution.py:53
  12.3 8.0 %collective-permute-start = (bf16[4,64,128]{2,1,0:T(8,128)(2,1)S(1)}, bf16[4,64,128]{2,1,0:T(8,128)(2,1)S(1)}, u32[]{:S(2)}, u32[]{:S(2)}) collective-permute-start(bf16[4,64,128]{2,1,0:T(8,128)(2,1)S(1)} %get-tuple-element.32), channel_id=1, source_target_pairs={{0,8},{8,16},{16,24},{24,32},{32,40},{40,48},{48,56},{56,64},{64,7... | collective-permute-start | bytes 196616 | tf_op jit(solution)/shard_map/ppermute | solution.py:52
  14.2 1.7 copy-start.3
  14.4 0.7 copy-start.6
  15.2 0.7 copy-start.7
  21.1 1.0 copy-start.1
  23.8 23.6 %all-to-all-start = ((f32[64,8,128]{2,1,0:T(8,128)}), f32[64,8,128]{2,1,0:T(8,128)S(1)}, u32[]{:S(2)}, u32[]{:S(2)}) async-start(f32[64,8,128]{2,1,0:T(8,128)} %pad_maximum_fusion.1), calls=%async_computation | async-start | bytes 524288 | tf_op jit(solution)/shard_map/all_to_all | solution.py:11
  80.8 6.7 %collective-permute-start.2 = (bf16[32,32,128]{2,1,0:T(8,128)(2,1)S(1)}, bf16[32,32,128]{2,1,0:T(8,128)(2,1)S(1)}, u32[]{:S(2)}, u32[]{:S(2)}) collective-permute-start(bf16[32,32,128]{2,1,0:T(8,128)(2,1)S(1)} %all_to_all.56), channel_id=1, source_target_pairs={{0,8},{8,0},{16,24},{24,16},{32,40},{40,32},{48,56},{56,48},{64,72... | collective-permute-start | bytes 786440 | tf_op jit(solution)/shard_map/ppermute | solution.py:86
  88.8 11.7 %all-to-all-start.3 = ((f32[8,32,128]{2,1,0:T(8,128)}), f32[8,32,128]{2,1,0:T(8,128)S(1)}, u32[]{:S(2)}, u32[]{:S(2)}) async-start(f32[8,32,128]{2,1,0:T(8,128)} %bitcast.33), calls=%async_computation.3 | async-start | bytes 262144 | tf_op jit(solution)/shard_map/all_to_all | solution.py:11
  101.2 10.7 %all-to-all-start.4 = ((bf16[8,34,128]{2,1,0:T(8,128)(2,1)}), bf16[8,34,128]{2,1,0:T(8,128)(2,1)S(1)}, u32[]{:S(2)}, u32[]{:S(2)}) async-start(bf16[8,34,128]{2,1,0:T(8,128)(2,1)} %broadcast_in_dim.66), calls=%async_computation.4 | async-start | bytes 163840 | tf_op jit(solution)/shard_map/all_to_all | solution.py:11
  129.8 6.3 %collective-permute-start.4 = (f32[4,64,128]{2,1,0:T(8,128)S(1)}, f32[4,64,128]{2,1,0:T(8,128)S(1)}, u32[]{:S(2)}, u32[]{:S(2)}) collective-permute-start(f32[4,64,128]{2,1,0:T(8,128)S(1)} %get-tuple-element.22), channel_id=1, source_target_pairs={{8,0},{16,8},{24,16},{32,24},{40,32},{48,40},{56,48},{64,56},{72,6... | collective-permute-start | bytes 393224 | tf_op jit(solution)/shard_map/ppermute | solution.py:53
  132.1 5.2 %collective-permute-start.3 = (f32[4,64,128]{2,1,0:T(8,128)S(1)}, f32[4,64,128]{2,1,0:T(8,128)S(1)}, u32[]{:S(2)}, u32[]{:S(2)}) collective-permute-start(f32[4,64,128]{2,1,0:T(8,128)S(1)} %get-tuple-element.21), channel_id=1, source_target_pairs={{0,8},{8,16},{16,24},{24,32},{32,40},{40,48},{48,56},{56,64},{64,7... | collective-permute-start | bytes 393224 | tf_op jit(solution)/shard_map/ppermute | solution.py:52
  159.3 21.4 %all-to-all-start.7 = ((bf16[8,256,128]{2,1,0:T(8,128)(2,1)}), bf16[8,256,128]{2,1,0:T(8,128)(2,1)S(1)}, u32[]{:S(2)}, u32[]{:S(2)}) async-start(bf16[8,256,128]{2,1,0:T(8,128)(2,1)} %broadcast_in_dim.68), calls=%async_computation.7 | async-start | bytes 1048576 | tf_op jit(solution)/shard_map/all_to_all | solution.py:11
  195.6 5.2 %collective-permute-start.5 = (bf16[32,32,128]{2,1,0:T(8,128)(2,1)S(1)}, bf16[32,32,128]{2,1,0:T(8,128)(2,1)S(1)}, u32[]{:S(2)}, u32[]{:S(2)}) collective-permute-start(bf16[32,32,128]{2,1,0:T(8,128)(2,1)S(1)} %all_to_all.59), channel_id=1, source_target_pairs={{0,8},{8,0},{16,24},{24,16},{32,40},{40,32},{48,56},{56,48},{64,72... | collective-permute-start | bytes 786440 | tf_op jit(solution)/shard_map/ppermute | solution.py:86

commit v3 on v2

v3 whole, which is shorter than its diff:
```python
import jax
import jax.numpy as jnp
from jax import lax
from jax.sharding import PartitionSpec as P

F32, BF16 = jnp.float32, jnp.bfloat16


def exchange(blocks, axis):
    return lax.all_to_all(blocks, axis, split_axis=0, concat_axis=0, tiled=True)


def in_two(value):
    high = lax.reduce_precision(value, 8, 7)
    return high.astype(BF16), (value - high).astype(BF16)


def in_parts(marks, value, flip):
    high = lax.reduce_precision(value, 8, 7)
    middle = lax.reduce_precision(value - high, 8, 7)
    parts = jnp.concatenate([high, middle, value - high - middle], axis=1).astype(BF16)
    out = lax.dot_general(marks, parts, (((1 - flip,), (0,)), ((), ())), preferred_element_type=F32)
    wide = value.shape[1]
    return out[:, :wide] + out[:, wide : 2 * wide] + out[:, 2 * wide :]


def body(
    load,
    schur,
    coupling,
    coarse_inverse,
    neighbour_sub,
    neighbour_edge,
    primal_owner,
    primal_offset,
):
    _, order, cases = load.shape
    edges = neighbour_sub.shape[1]
    width = order // edges
    half = edges // 2
    rows, block = coarse_inverse.shape
    n_sub, n_coarse = lax.axis_size("sub"), lax.axis_size("coarse")
    piece = block // n_coarse
    capacity = 2
    slots = n_sub * capacity
    sub_index, coarse_index = lax.axis_index("sub"), lax.axis_index("coarse")

    faces_next = (neighbour_sub[0] // n_coarse - sub_index) % n_sub == 1
    edge_at = neighbour_edge[0]
    same_side = faces_next[:, None] == faces_next[None, :]
    ids = jnp.arange(edges, dtype=jnp.int32)
    from_place = jnp.sum((same_side & (edge_at[None, :] < edge_at[:, None])).astype(jnp.int32), axis=1)
    from_place = from_place + jnp.where(faces_next, half, 0)
    to_place = jnp.sum((same_side & (ids[None, :] < ids[:, None])).astype(jnp.int32), axis=1)
    to_place = to_place + jnp.where(faces_next, 0, half)
    send_order = jnp.sum(jnp.where(to_place[None, :] == ids[:, None], ids[None, :], 0), axis=1)

    def facing(field):
        ordered = field.reshape(edges, width, cases)[send_order]
        from_before = lax.ppermute(ordered[:half], "sub", [(i, (i + 1) % n_sub) for i in range(n_sub)])
        from_next = lax.ppermute(ordered[half:], "sub", [((i + 1) % n_sub, i) for i in range(n_sub)])
        both = jnp.concatenate([from_before, from_next], axis=0)
        return both[from_place].reshape(order, cases)

    owners = primal_owner.reshape(-1)
    offsets = primal_offset.reshape(-1)
    prims = owners.shape[0]
    row_ids = jnp.arange(prims, dtype=jnp.int32)
    earlier = (owners[:, None] == owners[None, :]) & (row_ids[None, :] < row_ids[:, None])
    slot_of = owners * capacity + jnp.sum(earlier.astype(jnp.int32), axis=1)
    placed = jnp.arange(slots, dtype=jnp.int32)[:, None] == slot_of[None, :]
    slotted = jnp.dot(placed.astype(BF16), coupling[0], preferred_element_type=F32).astype(BF16)
    slot_offset = jnp.sum(jnp.where(placed, offsets[None, :] + 1, 0), axis=1).reshape(n_sub, capacity, 1)
    lane = jnp.arange(slots, dtype=jnp.int32).reshape(1, capacity, n_sub)
    asked = jnp.where(lane == sub_index + n_sub * jnp.arange(capacity).reshape(1, capacity, 1), slot_offset, 0)
    asked = asked.astype(F32).reshape(n_sub, 1, slots)
    codes = jnp.pad(slot_of, (0, cases - prims), constant_values=-1).astype(F32)

    chips = n_sub // 2
    same_core = [[2 * chip + core for chip in range(chips)] for core in range(2)]
    other_core = [(i, i ^ 1) for i in range(n_sub)]
    devices = n_sub * n_coarse
    near_by = 2 * n_coarse
    columns = [[start + k for k in range(near_by)] for start in range(0, devices, near_by)]
    planes = [[start + k for k in range(0, devices, near_by)] for start in range(near_by)]

    def product(rhs):
        mine = lax.all_to_all(
            jnp.broadcast_to(rhs[None], (chips,) + rhs.shape), "sub", 0, 0, tiled=True, axis_index_groups=same_core
        )
        theirs = lax.ppermute(mine, "sub", other_core)
        both = jnp.where(
            sub_index % 2 == 0, jnp.concatenate([mine, theirs], axis=1), jnp.concatenate([theirs, mine], axis=1)
        )
        return lax.dot_general(
            coarse_inverse, both.reshape(rows, cases), (((0,), (0,)), ((), ())), preferred_element_type=F32
        )

    def added(scalars, groups):
        wide = jnp.broadcast_to(scalars[None], (len(groups[0]),) + scalars.shape)
        wide = lax.all_to_all(wide, ("sub", "coarse"), 0, 0, tiled=True, axis_index_groups=groups)
        return jnp.sum(wide, axis=0)

    start = load[0]
    residual = start.astype(F32) - facing(start).astype(F32)
    jumps, rest = in_two(2.0 * residual)
    local = jnp.dot(schur[0], jumps, preferred_element_type=F32)
    near = jnp.sum(2.0 * residual * local, axis=0)
    terms = jnp.dot(slotted, jumps, preferred_element_type=F32).reshape(n_sub, capacity, cases)
    squares = jnp.broadcast_to(jnp.sum(residual * residual, axis=0), (n_sub, 1, cases))
    incoming = exchange(jnp.concatenate([terms, asked, squares], axis=1), "sub")
    given = jnp.concatenate([incoming[:, k] for k in range(capacity)], axis=0)
    asked = jnp.sum(incoming[:, capacity], axis=0)
    norm_now = jnp.sum(incoming[:, capacity + 1], axis=0)
    ids = lax.broadcasted_iota(jnp.int32, (block, slots), 0).astype(F32) + 1.0
    partial = in_parts((ids == asked[None]).astype(BF16), given, 0)
    sides = jnp.broadcast_to(jnp.stack([asked, codes])[None], (n_coarse, 2, cases))
    incoming = exchange(jnp.concatenate([partial.reshape(n_coarse, piece, cases), sides], axis=1), "coarse")
    asked_all = incoming[:, piece].reshape(1, n_coarse * slots)
    codes_all = incoming[:, piece + 1]
    ids = lax.broadcasted_iota(jnp.int32, (block, n_coarse * slots), 0).astype(F32) + 1.0
    marks = (ids == asked_all).astype(BF16)
    share = product(jnp.sum(incoming[:, :piece], axis=0).astype(BF16))
    answers = in_parts(marks, share, 1).reshape(n_coarse, slots, cases)
    solved = jnp.sum(exchange(answers, "coarse"), axis=0).astype(BF16)
    far = in_two(near + jnp.sum(given * solved.astype(F32), axis=0))
    out = [solved[k * n_sub : (k + 1) * n_sub, None] for k in range(capacity)]
    out = out + [jnp.broadcast_to(part, (n_sub, 1, cases)) for part in far]
    replies = exchange(jnp.concatenate(out, axis=1), "sub")
    curvature = jnp.sum(replies[:, capacity:].astype(F32), axis=(0, 1))
    values = replies[:, :capacity].reshape(slots, cases)
    image = local + lax.dot_general(slotted, values, (((0,), (0,)), ((), ())), preferred_element_type=F32)
    image = image - facing(image)

    old = jnp.dot(coupling[0], jnp.concatenate([jumps, rest], axis=1), preferred_element_type=F32)
    new = jnp.dot(coupling[0], jnp.concatenate(in_two(2.0 * image), axis=1), preferred_element_type=F32)
    sent = jnp.concatenate(
        [old[:, :cases] + old[:, cases:], new[:, :cases] + new[:, cases:], curvature[None], norm_now[None]], axis=0
    )
    incoming = exchange(jnp.broadcast_to(sent[None], (n_coarse,) + sent.shape), "coarse")
    curvature = jnp.sum(incoming[:, 2 * prims], axis=0)
    norm_now = jnp.sum(incoming[:, 2 * prims + 1], axis=0)
    alpha = norm_now / curvature
    coupled = (incoming[:, :prims] - alpha * incoming[:, prims : 2 * prims]).astype(BF16)
    room = 32
    coupled = jnp.pad(coupled, ((0, 0), (0, room - prims), (0, 0))).reshape(n_coarse * room, cases)
    codes_all = codes_all[:, :room].reshape(1, n_coarse * room)
    place = lax.broadcasted_iota(jnp.int32, (n_sub * n_coarse * capacity, n_coarse * room), 0)
    plane = lax.broadcasted_iota(jnp.int32, (n_sub * n_coarse * capacity, n_coarse * room), 1) // room
    here = place // (n_coarse * capacity) * capacity + place % capacity
    spread = (place // capacity % n_coarse == plane) & (here.astype(F32) == codes_all)
    outgoing = jnp.dot(spread.astype(BF16), coupled, preferred_element_type=F32).astype(BF16)
    incoming = exchange(outgoing.reshape(n_sub, n_coarse * capacity, cases), "sub")
    incoming = incoming.transpose(1, 0, 2).reshape(n_coarse * slots, cases)
    weights = jnp.dot(marks, incoming, preferred_element_type=F32)
    rhs = lax.dynamic_slice_in_dim(weights, coarse_index * piece, piece, axis=0).astype(BF16)
    far = jnp.sum(weights * product(rhs), axis=0)
    remainder = residual - alpha * image
    twice = 2.0 * remainder
    near = jnp.sum(twice * jnp.dot(schur[0], twice.astype(BF16), preferred_element_type=F32), axis=0)
    scalars = jnp.stack([near + far, jnp.sum(remainder * remainder, axis=0)])
    scalars = added(added(scalars, columns), planes)
    beta = scalars[1] / norm_now
    step = scalars[1] / (scalars[0] - beta * beta * curvature)
    return ((alpha + step * beta) * residual + step * remainder)[None]


def solution(mesh):
    return jax.shard_map(
        body,
        mesh=mesh,
        in_specs=(
            P(("sub", "coarse"), None, None),
            P(("sub", "coarse"), None, None),
            P(("sub", "coarse"), None, None),
            P("coarse", "sub"),
            P(("sub", "coarse"), None),
            P(("sub", "coarse"), None),
            P(("sub", "coarse"), None, None),
            P(("sub", "coarse"), None),
        ),
        out_specs=P(("sub", "coarse"), None, None),
        check_vma=False,
    )
```

time: 228 us -> 217 us (0.952)
  blocking collectives: 108 us -> 65.8 us
  waiting for transfers between devices: 54.1 us -> 67.1 us
  starting transfers between devices: 46.5 us -> 56.5 us
  matrix products: 3.2 us -> 9.09 us
  other arithmetic: 3.14 us -> 7.86 us
  local copies, waits for them, and re-layouts: 11.3 us -> 8.68 us
    all_to_all x5 -> x1, blocking collectives: 79.5 us -> 15.2 us  [exchange(): return lax.all_to_all(blocks, axis, split_axis=0, concat_axis=0, tiled=True)]
    all_to_all x0 -> x2, blocking collectives: none -> 22.1 us  [added(): lax.all_to_all(wide, ('sub', 'coarse'), 0, 0, tiled=True, axis_index_grou...]
    all_to_all x4 -> x5, waiting for transfers between devices: 46.7 us -> 60.9 us  [exchange(): return lax.all_to_all(blocks, axis, split_axis=0, concat_axis=0, tiled=True)]
    all_to_all x4 -> x5, starting transfers between devices: 20.5 us -> 31.8 us  [exchange(): return lax.all_to_all(blocks, axis, split_axis=0, concat_axis=0, tiled=True)]
    dot_general x7 -> x9, matrix products: 1.88 us -> 6.92 us  [the longest x1 4.46 us: body(): jnp.dot(spread.astype(BF16), coupled, preferred_element_type=F32)]
    ppermute x2, waiting for transfers between devices: 5.01 us -> 0.01 us  [facing(): lax.ppermute(ordered[:half], 'sub', [(i, (i + 1) % n_sub) for i in range(...]
    ppermute x2, waiting for transfers between devices: 0.62 us -> 4.55 us  [facing(): lax.ppermute(ordered[half:], 'sub', [((i + 1) % n_sub, i) for i in range(...]
    ppermute x2, starting transfers between devices: 11.2 us -> 8.12 us  [facing(): lax.ppermute(ordered[half:], 'sub', [((i + 1) % n_sub, i) for i in range(...]
  transfers between devices with their start and end apart: 10 -> 11, of which waited for: 9 -> 8; matrix products, arithmetic and copies ran while one was open for 1% -> 3% of each run, Pallas kernels for 0% -> 0%
where the time goes in v3:
time: 217 us; the launch traced here: 216 us
  waiting for transfers between devices  67.1 us (31%)
  blocking collectives  65.8 us (30%)
  starting transfers between devices  56.5 us (26%)
  matrix products  9.09 us (4%)
  local copies, waits for them, and re-layouts  8.68 us (4%)
  other arithmetic  7.86 us (4%)
    all_to_all x5, waiting for transfers between devices, exchange(): return lax.all_to_all(blocks, axis, split_axis=0, concat_axis=0, tiled=True)  60.9 us
    all_to_all x5, starting transfers between devices, exchange(): return lax.all_to_all(blocks, axis, split_axis=0, concat_axis=0, tiled=True)  31.8 us
    all_to_all x2, blocking collectives, product(): lax.all_to_all(jnp.broadcast_to(rhs[None], (chips,) + rhs.shape), 'sub',...  28.5 us
    all_to_all x2, blocking collectives, added(): lax.all_to_all(wide, ('sub', 'coarse'), 0, 0, tiled=True, axis_index_grou...  22.1 us
    all_to_all x1, blocking collectives, exchange(): return lax.all_to_all(blocks, axis, split_axis=0, concat_axis=0, tiled=True)  15.2 us
    ppermute x2, starting transfers between devices, product(): theirs = lax.ppermute(mine, 'sub', other_core)  9.66 us
    ppermute x2, starting transfers between devices, facing(): lax.ppermute(ordered[half:], 'sub', [((i + 1) % n_sub, i) for i in range(...  8.12 us
    ppermute x2, starting transfers between devices, facing(): lax.ppermute(ordered[:half], 'sub', [(i, (i + 1) % n_sub) for i in range(...  6.95 us
  transfers between devices with their start and end apart: 11, of which 8 were waited for; matrix products, arithmetic and copies ran while one was open for 3% of the time, Pallas kernels for 0%

profile of v3, /device:TPU:1, one launch (start us, length us, event | category | flops | bytes accessed | tf_op | source)
XLA Modules:
  0.0 215.8 jit_solution(9432563726261511227)
XLA Ops:
  2.5 1.5 gather_fusion
  4.0 4.5 %collective-permute-start = (bf16[4,64,128]{2,1,0:T(8,128)(2,1)S(1)}, bf16[4,64,128]{2,1,0:T(8,128)(2,1)S(1)}, u32[]{:S(2)}, u32[]{:S(2)}) collective-permute-start(bf16[4,64,128]{2,1,0:T(8,128)(2,1)S(1)} %get-tuple-element.33), channel_id=1, source_target_pairs={{0,8},{8,16},{16,24},{24,32},{32,40},{40,48},{48,56},{56,64},{64,7... | collective-permute-start | bytes 196616 | tf_op jit(solution)/shard_map/ppermute | solution.py:60
  8.6 6.2 %collective-permute-start.1 = (bf16[4,64,128]{2,1,0:T(8,128)(2,1)S(1)}, bf16[4,64,128]{2,1,0:T(8,128)(2,1)S(1)}, u32[]{:S(2)}, u32[]{:S(2)}) collective-permute-start(bf16[4,64,128]{2,1,0:T(8,128)(2,1)S(1)} %get-tuple-element.34), channel_id=1, source_target_pairs={{8,0},{16,8},{24,16},{32,24},{40,32},{48,40},{56,48},{64,56},{72,6... | collective-permute-start | bytes 196616 | tf_op jit(solution)/shard_map/ppermute | solution.py:61
  22.9 10.5 %all-to-all-start = ((f32[64,4,128]{2,1,0:T(4,128)}), f32[64,4,128]{2,1,0:T(4,128)S(1)}, u32[]{:S(2)}, u32[]{:S(2)}) async-start(f32[64,4,128]{2,1,0:T(4,128)} %copy.76), calls=%async_computation | async-start | bytes 262144 | tf_op jit(solution)/shard_map/all_to_all | solution.py:10
  33.5 11.1 %all-to-all-done = f32[64,4,128]{2,1,0:T(4,128)S(1)} async-done(((f32[64,4,128]{2,1,0:T(4,128)}), f32[64,4,128]{2,1,0:T(4,128)S(1)}, u32[]{:S(2)}, u32[]{:S(2)}) %all-to-all-start) | async-done | bytes 131104 | tf_op jit(solution)/shard_map/all_to_all | solution.py:10
  45.0 15.2 %all_to_all.50 = f32[8,34,128]{2,1,0:T(8,128)S(1)} all-to-all(f32[8,34,128]{2,1,0:T(8,128)S(1)} %pad_maximum_fusion.1), channel_id=1, replica_groups=mesh['sub'=64,'coarse'=8] {'coarse'}, dimensions={0} | all-to-all | bytes 278528 | tf_op jit(solution)/shard_map/all_to_all | solution.py:10
  60.3 13.6 %all_to_all.51 = bf16[32,32,128]{2,1,0:T(8,128)(2,1)S(1)} all-to-all(bf16[32,32,128]{2,1,0:T(8,128)(2,1)S(1)} %broadcast_in_dim.154), channel_id=1, replica_groups={{0,16,32,48,64,80,96,112,128,144,160,176,192,208,224,240,256,272,288,30..., dimensions={0} | all-to-all | bytes 524288 | tf_op jit(solution)/shard_map/all_to_all | solution.py:88
  73.8 5.6 %collective-permute-start.2 = (bf16[32,32,128]{2,1,0:T(8,128)(2,1)S(1)}, bf16[32,32,128]{2,1,0:T(8,128)(2,1)S(1)}, u32[]{:S(2)}, u32[]{:S(2)}) collective-permute-start(bf16[32,32,128]{2,1,0:T(8,128)(2,1)S(1)} %all_to_all.51), channel_id=1, source_target_pairs={{0,8},{8,0},{16,24},{24,16},{32,40},{40,32},{48,56},{56,48},{64,72... | collective-permute-start | bytes 786440 | tf_op jit(solution)/shard_map/ppermute | solution.py:91
  82.5 3.6 %all-to-all-start.3 = ((f32[8,128,128]{2,1,0:T(8,128)}), f32[8,128,128]{2,1,0:T(8,128)S(1)}, u32[]{:S(2)}, u32[]{:S(2)}) async-start(f32[8,128,128]{2,1,0:T(8,128)} %bitcast.30), calls=%async_computation.3 | async-start | bytes 1048576 | tf_op jit(solution)/shard_map/all_to_all | solution.py:10
  86.2 17.9 %all-to-all-done.3 = f32[8,128,128]{2,1,0:T(8,128)S(1)} async-done(((f32[8,128,128]{2,1,0:T(8,128)}), f32[8,128,128]{2,1,0:T(8,128)S(1)}, u32[]{:S(2)}, u32[]{:S(2)}) %all-to-all-start.3) | async-done | bytes 524320 | tf_op jit(solution)/shard_map/all_to_all | solution.py:10
  104.9 4.5 %all-to-all-start.4 = ((bf16[64,4,128]{2,1,0:T(4,128)(2,1)}), bf16[64,4,128]{2,1,0:T(4,128)(2,1)S(1)}, u32[]{:S(2)}, u32[]{:S(2)}) async-start(bf16[64,4,128]{2,1,0:T(4,128)(2,1)} %copy.78), calls=%async_computation.4 | async-start | bytes 131072 | tf_op jit(solution)/shard_map/all_to_all | solution.py:10
  109.6 10.0 %all-to-all-done.4 = bf16[64,4,128]{2,1,0:T(4,128)(2,1)S(1)} async-done(((bf16[64,4,128]{2,1,0:T(4,128)(2,1)}), bf16[64,4,128]{2,1,0:T(4,128)(2,1)S(1)}, u32[]{:S(2)}, u32[]{:S(2)}) %all-to-all-start.4) | async-done | bytes 65568 | tf_op jit(solution)/shard_map/all_to_all | solution.py:10
  120.6 2.4 %collective-permute-start.3 = (f32[4,64,128]{2,1,0:T(8,128)S(1)}, f32[4,64,128]{2,1,0:T(8,128)S(1)}, u32[]{:S(2)}, u32[]{:S(2)}) collective-permute-start(f32[4,64,128]{2,1,0:T(8,128)S(1)} %get-tuple-element.20), channel_id=1, source_target_pairs={{0,8},{8,16},{16,24},{24,32},{32,40},{40,48},{48,56},{56,64},{64,7... | collective-permute-start | bytes 393224 | tf_op jit(solution)/shard_map/ppermute | solution.py:60
  123.0 1.9 collective-permute-start.4
  125.1 4.6 %collective-permute-done.4 = f32[4,64,128]{2,1,0:T(8,128)S(1)} collective-permute-done((f32[4,64,128]{2,1,0:T(8,128)S(1)}, f32[4,64,128]{2,1,0:T(8,128)S(1)}, u32[]{:S(2)}, u32[]{:S(2)}) %collective-permute-start.4) | collective-permute-done | bytes 131104 | tf_op jit(solution)/shard_map/ppermute | solution.py:61
  131.3 3.4 %all-to-all-start.5 = ((f32[8,50,128]{2,1,0:T(8,128)}), f32[8,50,128]{2,1,0:T(8,128)S(1)}, u32[]{:S(2)}, u32[]{:S(2)}) async-start(f32[8,50,128]{2,1,0:T(8,128)} %broadcast_in_dim.161), calls=%async_computation.5 | async-start | bytes 458752 | tf_op jit(solution)/shard_map/all_to_all | solution.py:10
  134.9 8.8 %all-to-all-done.5 = f32[8,50,128]{2,1,0:T(8,128)S(1)} async-done(((f32[8,50,128]{2,1,0:T(8,128)}), f32[8,50,128]{2,1,0:T(8,128)S(1)}, u32[]{:S(2)}, u32[]{:S(2)}) %all-to-all-start.5) | async-done | bytes 204832 | tf_op jit(solution)/shard_map/all_to_all | solution.py:10
  143.8 4.5 %convolution_convert_fusion = bf16[1024,128]{1,0:T(8,128)(2,1)} fusion(bf16[256,128]{1,0:T(8,128)(2,1)S(1)} %bitcast.177, f32[256]{0:T(256)S(1)} %eq.157, s32[1024]{0:T(1024)S(1)} %get-tuple-element.44, s32[1024]{0:T(1024)S(1)} %get-tuple-element.46, s32[1024]{0:T(1024)S(1)} %get-tuple-element.45, s32[1024]{0:T(1024)S(1)} %get-tuple-element.51, ...), kind=kOutput, calls=%fused_computation.12 | convolution fusion | flops 72744960 | bytes 358656 | tf_op jit(solution)/shard_map/dot_general | solution.py:152
  148.2 9.8 %all-to-all-start.6 = ((bf16[64,16,128]{2,1,0:T(8,128)(2,1)}), bf16[64,16,128]{2,1,0:T(8,128)(2,1)S(1)}, u32[]{:S(2)}, u32[]{:S(2)}) async-start(bf16[64,16,128]{2,1,0:T(8,128)(2,1)} %bitcast.46), calls=%async_computation.6 | async-start | bytes 524288 | tf_op jit(solution)/shard_map/all_to_all | solution.py:10
  158.0 13.2 %all-to-all-done.6 = bf16[64,16,128]{2,1,0:T(8,128)(2,1)S(1)} async-done(((bf16[64,16,128]{2,1,0:T(8,128)(2,1)}), bf16[64,16,128]{2,1,0:T(8,128)(2,1)S(1)}, u32[]{:S(2)}, u32[]{:S(2)}) %all-to-all-start.6) | async-done | bytes 262176 | tf_op jit(solution)/shard_map/all_to_all | solution.py:10
  171.7 15.0 %all_to_all.52 = bf16[32,32,128]{2,1,0:T(8,128)(2,1)S(1)} all-to-all(bf16[32,32,128]{2,1,0:T(8,128)(2,1)S(1)} %broadcast_in_dim.162), channel_id=1, replica_groups={{0,16,32,48,64,80,96,112,128,144,160,176,192,208,224,240,256,272,288,30..., dimensions={0} | all-to-all | bytes 524288 | tf_op jit(solution)/shard_map/all_to_all | solution.py:88
  186.6 4.1 %collective-permute-start.5 = (bf16[32,32,128]{2,1,0:T(8,128)(2,1)S(1)}, bf16[32,32,128]{2,1,0:T(8,128)(2,1)S(1)}, u32[]{:S(2)}, u32[]{:S(2)}) collective-permute-start(bf16[32,32,128]{2,1,0:T(8,128)(2,1)S(1)} %all_to_all.52), channel_id=1, source_target_pairs={{0,8},{8,0},{16,24},{24,16},{32,40},{40,32},{48,56},{56,48},{64,72... | collective-permute-start | bytes 786440 | tf_op jit(solution)/shard_map/ppermute | solution.py:91
  192.6 9.8 %all_to_all.53 = f32[16,2,128]{2,1,0:T(2,128)S(1)} all-to-all(f32[16,2,128]{2,1,0:T(2,128)S(1)} %broadcast_in_dim.163), channel_id=1, replica_groups={{0,1,2,3,4,5,6,7,8,9,10,11,12,13,14,15},{16,17,18,19,20,21,22,23,24,25,..., dimensions={0} | all-to-all | bytes 32768 | tf_op jit(solution)/shard_map/all_to_all | solution.py:101
  202.4 12.3 %all_to_all.54 = f32[32,2,128]{2,1,0:T(2,128)S(1)} all-to-all(f32[32,2,128]{2,1,0:T(2,128)S(1)} %broadcast_in_dim.164), channel_id=1, replica_groups={{0,16,32,48,64,80,96,112,128,144,160,176,192,208,224,240,256,272,288,30..., dimensions={0} | all-to-all | bytes 65536 | tf_op jit(solution)/shard_map/all_to_all | solution.py:101
  (121 shorter events, 21.4 us)
Async XLA Ops:
  0.0 80.7 %copy-start = (bf16[2048,256]{1,0:T(8,128)(2,1)S(1)}, bf16[2048,256]{1,0:T(8,128)(2,1)}, u32[]{:S(2)}) copy-start(bf16[2048,256]{1,0:T(8,128)(2,1)} %param.11) | copy-start | bytes 3145732
  4.0 16.5 %collective-permute-start = (bf16[4,64,128]{2,1,0:T(8,128)(2,1)S(1)}, bf16[4,64,128]{2,1,0:T(8,128)(2,1)S(1)}, u32[]{:S(2)}, u32[]{:S(2)}) collective-permute-start(bf16[4,64,128]{2,1,0:T(8,128)(2,1)S(1)} %get-tuple-element.33), channel_id=1, source_target_pairs={{0,8},{8,16},{16,24},{24,32},{32,40},{40,48},{48,56},{56,64},{64,7... | collective-permute-start | bytes 196616 | tf_op jit(solution)/shard_map/ppermute | solution.py:60
  8.6 12.0 %collective-permute-start.1 = (bf16[4,64,128]{2,1,0:T(8,128)(2,1)S(1)}, bf16[4,64,128]{2,1,0:T(8,128)(2,1)S(1)}, u32[]{:S(2)}, u32[]{:S(2)}) collective-permute-start(bf16[4,64,128]{2,1,0:T(8,128)(2,1)S(1)} %get-tuple-element.34), channel_id=1, source_target_pairs={{8,0},{16,8},{24,16},{32,24},{40,32},{48,40},{56,48},{64,56},{72,6... | collective-permute-start | bytes 196616 | tf_op jit(solution)/shard_map/ppermute | solution.py:61
  20.6 1.1 copy-start.1
  22.9 21.6 %all-to-all-start = ((f32[64,4,128]{2,1,0:T(4,128)}), f32[64,4,128]{2,1,0:T(4,128)S(1)}, u32[]{:S(2)}, u32[]{:S(2)}) async-start(f32[64,4,128]{2,1,0:T(4,128)} %copy.76), calls=%async_computation | async-start | bytes 262144 | tf_op jit(solution)/shard_map/all_to_all | solution.py:10
  73.8 6.7 %collective-permute-start.2 = (bf16[32,32,128]{2,1,0:T(8,128)(2,1)S(1)}, bf16[32,32,128]{2,1,0:T(8,128)(2,1)S(1)}, u32[]{:S(2)}, u32[]{:S(2)}) collective-permute-start(bf16[32,32,128]{2,1,0:T(8,128)(2,1)S(1)} %all_to_all.51), channel_id=1, source_target_pairs={{0,8},{8,0},{16,24},{24,16},{32,40},{40,32},{48,56},{56,48},{64,72... | collective-permute-start | bytes 786440 | tf_op jit(solution)/shard_map/ppermute | solution.py:91
  82.5 26.9 %copy-start.2 = (bf16[1,24,512]{2,1,0:T(8,128)(2,1)S(1)}, bf16[1,24,512]{2,1,0:T(8,128)(2,1)}, u32[]{:S(2)}) copy-start(bf16[1,24,512]{2,1,0:T(8,128)(2,1)} %param.10) | copy-start | bytes 73732
  82.5 21.6 %all-to-all-start.3 = ((f32[8,128,128]{2,1,0:T(8,128)}), f32[8,128,128]{2,1,0:T(8,128)S(1)}, u32[]{:S(2)}, u32[]{:S(2)}) async-start(f32[8,128,128]{2,1,0:T(8,128)} %bitcast.30), calls=%async_computation.3 | async-start | bytes 1048576 | tf_op jit(solution)/shard_map/all_to_all | solution.py:10
  104.9 14.7 %all-to-all-start.4 = ((bf16[64,4,128]{2,1,0:T(4,128)(2,1)}), bf16[64,4,128]{2,1,0:T(4,128)(2,1)S(1)}, u32[]{:S(2)}, u32[]{:S(2)}) async-start(bf16[64,4,128]{2,1,0:T(4,128)(2,1)} %copy.78), calls=%async_computation.4 | async-start | bytes 131072 | tf_op jit(solution)/shard_map/all_to_all | solution.py:10
  120.6 4.5 %collective-permute-start.3 = (f32[4,64,128]{2,1,0:T(8,128)S(1)}, f32[4,64,128]{2,1,0:T(8,128)S(1)}, u32[]{:S(2)}, u32[]{:S(2)}) collective-permute-start(f32[4,64,128]{2,1,0:T(8,128)S(1)} %get-tuple-element.20), channel_id=1, source_target_pairs={{0,8},{8,16},{16,24},{24,32},{32,40},{40,48},{48,56},{56,64},{64,7... | collective-permute-start | bytes 393224 | tf_op jit(solution)/shard_map/ppermute | solution.py:60
  123.0 6.6 %collective-permute-start.4 = (f32[4,64,128]{2,1,0:T(8,128)S(1)}, f32[4,64,128]{2,1,0:T(8,128)S(1)}, u32[]{:S(2)}, u32[]{:S(2)}) collective-permute-start(f32[4,64,128]{2,1,0:T(8,128)S(1)} %get-tuple-element.21), channel_id=1, source_target_pairs={{8,0},{16,8},{24,16},{32,24},{40,32},{48,40},{56,48},{64,56},{72,6... | collective-permute-start | bytes 393224 | tf_op jit(solution)/shard_map/ppermute | solution.py:61
  131.3 12.3 %all-to-all-start.5 = ((f32[8,50,128]{2,1,0:T(8,128)}), f32[8,50,128]{2,1,0:T(8,128)S(1)}, u32[]{:S(2)}, u32[]{:S(2)}) async-start(f32[8,50,128]{2,1,0:T(8,128)} %broadcast_in_dim.161), calls=%async_computation.5 | async-start | bytes 458752 | tf_op jit(solution)/shard_map/all_to_all | solution.py:10
  148.2 22.9 %all-to-all-start.6 = ((bf16[64,16,128]{2,1,0:T(8,128)(2,1)}), bf16[64,16,128]{2,1,0:T(8,128)(2,1)S(1)}, u32[]{:S(2)}, u32[]{:S(2)}) async-start(bf16[64,16,128]{2,1,0:T(8,128)(2,1)} %bitcast.46), calls=%async_computation.6 | async-start | bytes 524288 | tf_op jit(solution)/shard_map/all_to_all | solution.py:10
  186.6 5.2 %collective-permute-start.5 = (bf16[32,32,128]{2,1,0:T(8,128)(2,1)S(1)}, bf16[32,32,128]{2,1,0:T(8,128)(2,1)S(1)}, u32[]{:S(2)}, u32[]{:S(2)}) collective-permute-start(bf16[32,32,128]{2,1,0:T(8,128)(2,1)S(1)} %all_to_all.52), channel_id=1, source_target_pairs={{0,8},{8,0},{16,24},{24,16},{32,40},{40,32},{48,56},{56,48},{64,72... | collective-permute-start | bytes 786440 | tf_op jit(solution)/shard_map/ppermute | solution.py:91

commit v4 on v0

v4 whole, which is shorter than its diff:
```python
import jax
import jax.numpy as jnp
from jax import lax
from jax.experimental import pallas as pl
from jax.experimental.pallas import tpu as pltpu
from jax.sharding import PartitionSpec as P

F32, BF16, I32 = jnp.float32, jnp.bfloat16, jnp.int32
CAPACITY = 2
LINES = 4
ROOM = 32
SIDES = 8


def dot(a, b):
    return jnp.dot(a, b, preferred_element_type=F32)


def dot_t(a, b):
    return lax.dot_general(a, b, (((0,), (0,)), ((), ())), preferred_element_type=F32)


def iota(shape, dim):
    return lax.broadcasted_iota(I32, shape, dim)


def ones_where(mask):
    return jnp.where(mask, 1.0, 0.0).astype(BF16)


def in_two(value):
    high = value.astype(BF16)
    return high, (value - high.astype(F32)).astype(BF16)


def in_three(value):
    high = value.astype(BF16)
    rest = value - high.astype(F32)
    middle = rest.astype(BF16)
    return jnp.concatenate([high, middle, (rest - middle.astype(F32)).astype(BF16)], axis=1)


def joined(parts, count):
    wide = parts.shape[1] // count
    out = parts[:, :wide]
    for k in range(1, count):
        out = out + parts[:, k * wide : (k + 1) * wide]
    return out


def run(kernel, outs, *args):
    def spec(x):
        small = jnp.issubdtype(x.dtype, jnp.integer) and x.size <= 8
        return pl.BlockSpec(memory_space=pltpu.SMEM if small else pltpu.VMEM)

    return pl.pallas_call(
        kernel,
        out_shape=[jax.ShapeDtypeStruct(shape, dtype) for shape, dtype in outs],
        in_specs=[spec(x) for x in args],
        out_specs=[pl.BlockSpec(memory_space=pltpu.VMEM)] * len(outs),
        compiler_params=pltpu.CompilerParams(vmem_limit_bytes=32 * 1024 * 1024),
    )(*args)


def body(
    load,
    schur,
    coupling,
    coarse_inverse,
    neighbour_sub,
    neighbour_edge,
    primal_owner,
    primal_offset,
):
    _, order, cases = load.shape
    edges = neighbour_sub.shape[1]
    width = order // edges
    half = edges // 2
    rows, block = coarse_inverse.shape
    prims = primal_offset.shape[1]
    n_sub, n_coarse = lax.axis_size("sub"), lax.axis_size("coarse")
    piece = block // n_coarse
    slots = n_sub * CAPACITY
    lines = n_sub * LINES
    chips = n_sub // 2
    sub_index, coarse_index = lax.axis_index("sub"), lax.axis_index("coarse")
    here = jnp.stack([sub_index, coarse_index])[None].astype(I32)

    to_next = [(i, (i + 1) % n_sub) for i in range(n_sub)]
    to_before = [((i + 1) % n_sub, i) for i in range(n_sub)]
    other_core = [(i, i ^ 1) for i in range(n_sub)]
    same_core = [[2 * chip + core for chip in range(chips)] for core in range(2)]
    near_by = 2 * n_coarse
    devices = n_sub * n_coarse
    columns = [[start + k for k in range(near_by)] for start in range(0, devices, near_by)]
    planes = [[start + k for k in range(0, devices, near_by)] for start in range(near_by)]

    def exchange(blocks, axis, groups=None):
        return lax.all_to_all(blocks, axis, 0, 0, tiled=True, axis_index_groups=groups)

    def faces_next(here_ref, sub_ref, e):
        return lax.rem(lax.div(sub_ref[0, e], n_coarse) - here_ref[0, 0] + n_sub, n_sub) == 1

    def edge(e):
        return slice(e * width, (e + 1) * width)

    def set_up(here_ref, owner_ref, offset_ref, coupling_ref, slotted_ref, asked_ref, codes_ref):
        same = iota((prims, prims), 0) == iota((prims, prims), 1)
        owner_row = jnp.sum(jnp.where(same, owner_ref[...], 0), axis=0, keepdims=True)
        before = (owner_ref[...] == owner_row) & (iota((prims, prims), 0) < iota((prims, prims), 1))
        second = jnp.sum(jnp.where(before, 1, 0), axis=0, keepdims=True)
        line = iota((lines, prims), 0)
        placed = line == owner_row * LINES + second
        slotted_ref[...] = dot(ones_where(placed), coupling_ref[...]).astype(BF16)
        lane = iota((lines, slots), 1)
        asked = jnp.zeros((lines, slots), I32)
        for k in range(CAPACITY):
            named = (line >> 2 == owner_row) & (second == k)
            offset = jnp.sum(jnp.where(named, offset_ref[...] + 1, 0), axis=1, keepdims=True)
            asked = jnp.where(lane == k * n_sub + here_ref[0, 0], offset, asked)
        asked_ref[...] = jnp.where((iota((lines, slots), 0) & (LINES - 1)) == CAPACITY, asked, 0).astype(F32)
        target = owner_row * (n_coarse * CAPACITY) + second + CAPACITY * here_ref[0, 1] + 1
        far_lane = iota((prims, n_coarse * ROOM), 1) == iota((prims, n_coarse * ROOM), 0) + ROOM * here_ref[0, 1]
        target_col = jnp.sum(jnp.where(same, target, 0), axis=1, keepdims=True)
        codes = jnp.sum(jnp.where(far_lane, target_col, 0), axis=0, keepdims=True).astype(F32)
        codes_ref[...] = jnp.zeros((SIDES, cases), F32)
        for k in range(n_coarse * ROOM // cases):
            codes_ref[k + 1 : k + 2, :] = codes[:, k * cases : (k + 1) * cases]

    def first(
        here_ref, sub_ref, edge_ref, load_ref, before_ref, next_ref, schur_ref, slotted_ref, asked_ref, coupling_ref,
        residual_ref, local_ref, out_ref, near_ref, old_ref,
    ):
        for e in range(edges):
            start = pl.multiple_of(edge_ref[0, e] * width, width)
            ahead = next_ref[pl.ds(start, width), :].astype(F32)
            behind = before_ref[pl.ds(start, width), :].astype(F32)
            facing = jnp.where(faces_next(here_ref, sub_ref, e), ahead, behind)
            residual_ref[edge(e), :] = load_ref[edge(e), :].astype(F32) - facing
        twice = 2.0 * residual_ref[...]
        jumps, rest = in_two(twice)
        terms = dot(slotted_ref[...], jumps)
        squares = jnp.sum(twice * twice, axis=0, keepdims=True) * 0.25
        line = iota((lines, cases), 0) & (LINES - 1)
        out_ref[...] = terms + asked_ref[...] + jnp.where(line == LINES - 1, squares, 0.0)
        local = dot(schur_ref[...], jumps)
        local_ref[...] = local
        near_ref[...] = jnp.sum(twice * local, axis=0, keepdims=True)
        old_ref[...] = joined(dot(coupling_ref[...], jnp.concatenate([jumps, rest], axis=1)), 2)

    def line_of(shape, dim):
        return (iota(shape, dim) & (LINES - 1)) * n_sub + (iota(shape, dim) >> 2)

    def owner_sums(in_ref, codes_ref, out_ref, norm_ref):
        given = in_ref[...]
        line = iota((lines, cases), 0) & (LINES - 1)
        asked = jnp.sum(jnp.where(line == CAPACITY, given, 0.0), axis=0, keepdims=True)
        norm_ref[...] = jnp.sum(jnp.where(line == LINES - 1, given, 0.0), axis=0, keepdims=True)
        expand = ones_where(iota((slots, lines), 0) == line_of((slots, lines), 1))
        wide = dot(jnp.broadcast_to(asked, (SIDES, slots)).astype(BF16), expand)[:1]
        marks = ones_where((iota((block, lines), 0) + 1).astype(F32) == wide)
        partial = joined(dot(marks, in_three(given)), 3)
        sides = codes_ref[...] + jnp.where(iota((SIDES, cases), 0) == 0, asked, 0.0)
        for c in range(n_coarse):
            out_ref[c, :piece] = partial[c * piece : (c + 1) * piece]
            out_ref[c, piece:] = sides

    def coarse_sums(in_ref, rhs_ref, marks_ref, codes_ref):
        total = in_ref[0]
        for c in range(1, n_coarse):
            total = total + in_ref[c]
        rhs = total[:piece].astype(BF16)
        for k in range(chips):
            rhs_ref[k] = rhs
        ids = (iota((block, slots), 0) + 1).astype(F32)
        for c in range(n_coarse):
            marks_ref[:, c * slots : (c + 1) * slots] = ones_where(ids == in_ref[c, piece : piece + 1])
        codes_ref[...] = total[piece:]

    def product(here_ref, mine_ref, theirs_ref, inverse_ref, both_ref):
        core = lax.rem(here_ref[0, 0], 2)
        for k in range(chips):
            both_ref[pl.ds(pl.multiple_of((2 * k + core) * piece, piece), piece), :] = mine_ref[k]
            both_ref[pl.ds(pl.multiple_of((2 * k + 1 - core) * piece, piece), piece), :] = theirs_ref[k]
        return dot_t(inverse_ref[...], both_ref[...])

    def answer(here_ref, mine_ref, theirs_ref, inverse_ref, marks_ref, both_ref, out_ref):
        share = in_three(product(here_ref, mine_ref, theirs_ref, inverse_ref, both_ref))
        for c in range(n_coarse):
            out_ref[c] = joined(dot_t(marks_ref[:, c * slots : (c + 1) * slots], share), 3)

    def reply(in_ref, given_ref, near_ref, out_ref):
        solved = in_ref[0]
        for c in range(1, n_coarse):
            solved = solved + in_ref[c]
        expand = ones_where(line_of((lines, slots), 0) == iota((lines, slots), 1))
        wide = dot(expand, solved.astype(BF16))
        line = iota((lines, cases), 0) & (LINES - 1)
        far = near_ref[...] + jnp.sum(jnp.where(line < CAPACITY, given_ref[...] * wide, 0.0), axis=0, keepdims=True)
        high, low = in_two(far)
        wide = jnp.where(line == CAPACITY, high.astype(F32), wide)
        out_ref[...] = jnp.where(line == CAPACITY + 1, low.astype(F32), wide).astype(BF16)

    def back(here_ref, sub_ref, in_ref, slotted_ref, local_ref, image_ref, ahead_ref, behind_ref, curvature_ref):
        replies = in_ref[...]
        image_ref[...] = local_ref[...] + dot_t(slotted_ref[...], replies)
        line = iota((lines, cases), 0) & (LINES - 1)
        curvature_ref[...] = jnp.sum(jnp.where(line >= CAPACITY, replies.astype(F32), 0.0), axis=0, keepdims=True)
        ahead = jnp.int32(0)
        for e in range(edges):
            faces = faces_next(here_ref, sub_ref, e)

            @pl.when(faces)
            def _():
                ahead_ref[pl.ds(pl.multiple_of(ahead * width, width), width), :] = image_ref[edge(e), :]

            @pl.when(jnp.logical_not(faces))
            def _():
                behind_ref[pl.ds(pl.multiple_of((e - ahead) * width, width), width), :] = image_ref[edge(e), :]

            ahead = ahead + faces.astype(I32)

    def coupled_rows(
        here_ref, sub_ref, edge_ref, image_ref, before_ref, next_ref, coupling_ref, old_ref, curvature_ref, norm_ref,
        jump_ref, out_ref,
    ):
        for e in range(edges):
            faces = faces_next(here_ref, sub_ref, e)
            place = jnp.int32(0)
            for other in range(edges):
                alike = faces_next(here_ref, sub_ref, other) == faces
                place = place + (alike & (edge_ref[0, other] < edge_ref[0, e])).astype(I32)
            start = pl.multiple_of(place * width, width)
            facing = jnp.where(faces, next_ref[pl.ds(start, width), :], before_ref[pl.ds(start, width), :])
            jump_ref[edge(e), :] = image_ref[edge(e), :] - facing
        pair = jnp.concatenate(in_two(2.0 * jump_ref[...]), axis=1)
        new = joined(dot(coupling_ref[...], pair), 2)
        line = iota((SIDES, cases), 0)
        tail = jnp.where(line == 0, curvature_ref[...], jnp.where(line == 1, norm_ref[...], 0.0))
        for c in range(n_coarse):
            out_ref[c, :prims] = old_ref[...]
            out_ref[c, prims : 2 * prims] = new
            out_ref[c, 2 * prims :] = tail

    def spread(in_ref, codes_ref, out_ref, scalars_ref):
        tail = in_ref[0, 2 * prims :]
        for c in range(1, n_coarse):
            tail = tail + in_ref[c, 2 * prims :]
        curvature, norm = tail[0:1], tail[1:2]
        alpha = norm / curvature
        line = iota((SIDES, cases), 0)
        scalars_ref[...] = jnp.where(line == 0, alpha, jnp.where(line == 1, curvature, norm))
        empty = jnp.zeros((ROOM - prims, cases), F32)
        parts = []
        for c in range(n_coarse):
            parts += [in_ref[c, :prims] - alpha * in_ref[c, prims : 2 * prims], empty]
        coupled = jnp.concatenate(parts, axis=0).astype(BF16)
        target = jnp.concatenate([codes_ref[k + 1 : k + 2, :] for k in range(n_coarse * ROOM // cases)], axis=1)
        total = n_coarse * slots
        marks = ones_where((iota((total, n_coarse * ROOM), 0) + 1).astype(F32) == target)
        out_ref[...] = dot(marks, coupled).astype(BF16)

    def owner_rows(here_ref, in_ref, marks_ref, weights_ref, rhs_ref):
        weights_ref[...] = dot(marks_ref[...], in_ref[...])
        start = pl.multiple_of(here_ref[0, 1] * piece, piece)
        rhs = weights_ref[pl.ds(start, piece), :].astype(BF16)
        for k in range(chips):
            rhs_ref[k] = rhs

    def second(residual_ref, jump_ref, scalars_ref, schur_ref, remainder_ref, sums_ref):
        remainder = residual_ref[...] - scalars_ref[0:1] * jump_ref[...]
        remainder_ref[...] = remainder
        twice = 2.0 * remainder
        near = jnp.sum(twice * dot(schur_ref[...], twice.astype(BF16)), axis=0, keepdims=True)
        line = iota((SIDES, cases), 0)
        norm = jnp.sum(remainder * remainder, axis=0, keepdims=True)
        sums_ref[...] = jnp.where(line == 0, near, jnp.where(line == 1, norm, 0.0))

    def energy(here_ref, mine_ref, theirs_ref, inverse_ref, weights_ref, sums_ref, both_ref, out_ref):
        share = product(here_ref, mine_ref, theirs_ref, inverse_ref, both_ref)
        far = jnp.sum(weights_ref[...] * share, axis=0, keepdims=True)
        out_ref[...] = sums_ref[...] + jnp.where(iota((SIDES, cases), 0) == 0, far, 0.0)

    field = ((order, cases), F32)
    row = ((1, cases), F32)
    gathered = ((chips, piece, cases), BF16)
    owners = primal_owner.reshape(prims, 1)
    offsets = primal_offset.reshape(1, prims)
    start = load[0]
    from_before = lax.ppermute(start, "sub", to_next)
    from_next = lax.ppermute(start, "sub", to_before)
    slotted, asked, codes = run(
        set_up,
        [((lines, order), BF16), ((lines, slots), F32), ((SIDES, cases), F32)],
        here,
        owners,
        offsets,
        coupling[0],
    )
    residual, local, outgoing, near, old = run(
        first,
        [field, field, ((lines, cases), F32), row, ((prims, cases), F32)],
        here, neighbour_sub, neighbour_edge, start, from_before, from_next, schur[0], slotted, asked, coupling[0],
    )
    given = exchange(outgoing.reshape(n_sub, LINES, cases), "sub").reshape(lines, cases)
    outgoing, norm = run(owner_sums, [((n_coarse, piece + SIDES, cases), F32), row], given, codes)
    incoming = exchange(outgoing, "coarse")
    rhs, marks, codes = run(
        coarse_sums, [gathered, ((block, n_coarse * slots), BF16), ((SIDES, cases), F32)], incoming
    )
    mine = exchange(rhs, "sub", same_core)
    theirs = lax.ppermute(mine, "sub", other_core)
    both = ((rows, cases), BF16)
    _, outgoing = run(answer, [both, ((n_coarse, slots, cases), F32)], here, mine, theirs, coarse_inverse, marks)
    incoming = exchange(outgoing, "coarse")
    (outgoing,) = run(reply, [((lines, cases), BF16)], incoming, given, near)
    replies = exchange(outgoing.reshape(n_sub, LINES, cases), "sub").reshape(lines, cases)
    side = ((half * width, cases), F32)
    image, ahead, behind, curvature = run(
        back, [field, side, side, row], here, neighbour_sub, replies, slotted, local
    )
    from_before = lax.ppermute(ahead, "sub", to_next)
    from_next = lax.ppermute(behind, "sub", to_before)
    image, outgoing = run(
        coupled_rows,
        [field, ((n_coarse, 2 * prims + SIDES, cases), F32)],
        here, neighbour_sub, neighbour_edge, image, from_before, from_next, coupling[0], old, curvature, norm,
    )
    incoming = exchange(outgoing, "coarse")
    outgoing, scalars = run(
        spread, [((n_coarse * slots, cases), BF16), ((SIDES, cases), F32)], incoming, codes
    )
    incoming = exchange(outgoing.reshape(n_sub, n_coarse * CAPACITY, cases), "sub")
    incoming = incoming.transpose(1, 0, 2).reshape(n_coarse * slots, cases)
    weights, rhs = run(owner_rows, [((block, cases), F32), gathered], here, incoming, marks)
    mine = exchange(rhs, "sub", same_core)
    theirs = lax.ppermute(mine, "sub", other_core)
    remainder, sums = run(second, [field, ((SIDES, cases), F32)], residual, image, scalars, schur[0])
    _, sums = run(
        energy, [both, ((SIDES, cases), F32)], here, mine, theirs, coarse_inverse, weights, sums
    )
    sums = sums[:2]
    for groups in (columns, planes):
        wide = jnp.broadcast_to(sums[None], (len(groups[0]),) + sums.shape)
        sums = jnp.sum(exchange(wide, ("sub", "coarse"), groups), axis=0)
    alpha, curvature, norm = scalars[0], scalars[1], scalars[2]
    beta = sums[1] / norm
    step = sums[1] / (sums[0] - beta * beta * curvature)
    return ((alpha + step * beta) * residual + step * remainder)[None]


def solution(mesh):
    return jax.shard_map(
        body,
        mesh=mesh,
        in_specs=(
            P(("sub", "coarse"), None, None),
            P(("sub", "coarse"), None, None),
            P(("sub", "coarse"), None, None),
            P("coarse", "sub"),
            P(("sub", "coarse"), None),
            P(("sub", "coarse"), None),
            P(("sub", "coarse"), None, None),
            P(("sub", "coarse"), None),
        ),
        out_specs=P(("sub", "coarse"), None, None),
        check_vma=False,
    )
```

time: 861 us -> 207 us (0.24)
  waiting for transfers between devices: 325 us -> 10.5 us
  blocking collectives: 425 us -> 156 us
  starting transfers between devices: 69.9 us -> 24.7 us
  between operations: 14 us -> 0.17 us
  local copies, waits for them, and re-layouts: 17.4 us -> 4.11 us
  Pallas kernels: 0 us -> 9.74 us
    psum x5 -> x0, blocking collectives: 337 us -> none  [the longest x2 193 us: squares(): return lax.psum(jnp.sum(vector * vector, axis=(0, 1)), ('sub', 'coarse'))]
    reduce_scatter x2 -> x0, waiting for transfers between devices: 285 us -> none  [body(): lax.psum_scatter(jnp.dot(coarse_inverse, coarse_rhs, preferred_element_ty...]
    all_to_all x2 -> x10, blocking collectives: 49.7 us -> 156 us  [exchange(): lax.all_to_all(blocks, axis, 0, 0, tiled=True, axis_index_groups=groups)]
    all_gather x2 -> x0, blocking collectives: 38.4 us -> none  [body(): lax.all_gather(share.astype(jnp.bfloat16), 'coarse', axis=0, tiled=True)]
    all_to_all x3 -> x0, starting transfers between devices: 30.5 us -> none  [the longest x1 18.9 us: body(): lax.all_to_all(owned[recv_offsets], 'sub', split_axis=0, concat_axis=0, t...]
    all_to_all x3 -> x0, waiting for transfers between devices: 24.1 us -> none  [the longest x1 9.24 us: body(): lax.all_to_all(owned[recv_offsets], 'sub', split_axis=0, concat_axis=0, t...]
    ppermute x10 -> x6, starting transfers between devices: 39.3 us -> 24.7 us  [the longest x2 9.58 us: body(): theirs = lax.ppermute(mine, 'sub', other_core)]
    pallas_call x0 -> x12, Pallas kernels: none -> 9.74 us  [run(): pl.pallas_call(kernel, out_shape=[jax.ShapeDtypeStruct(shape, dtype) for...]
  transfers between devices with their start and end apart: 15 -> 6, of which waited for: 12 -> 4; matrix products, arithmetic and copies ran while one was open for 1% -> 0% of each run, Pallas kernels for 0% -> 1%
where the time goes in v4:
time: 207 us; the launch traced here: 206 us
  blocking collectives  156 us (75%)
  starting transfers between devices  24.7 us (12%)
  waiting for transfers between devices  10.5 us (5%)
  Pallas kernels  9.74 us (5%)
  local copies, waits for them, and re-layouts  4.11 us (2%)
    all_to_all x10, blocking collectives, exchange(): lax.all_to_all(blocks, axis, 0, 0, tiled=True, axis_index_groups=groups)  156 us
    pallas_call x12, Pallas kernels, run(): pl.pallas_call(kernel, out_shape=[jax.ShapeDtypeStruct(shape, dtype) for...  9.74 us
    ppermute x2, starting transfers between devices, body(): theirs = lax.ppermute(mine, 'sub', other_core)  9.58 us
    ppermute x1, starting transfers between devices, body(): from_next = lax.ppermute(start, 'sub', to_before)  8.91 us
    ppermute x1, waiting for transfers between devices, body(): from_next = lax.ppermute(behind, 'sub', to_before)  4.61 us
  transfers between devices with their start and end apart: 6, of which 4 were waited for; matrix products, arithmetic and copies ran while one was open for 0% of the time, Pallas kernels for 1%

profile of v4, /device:TPU:1, one launch (start us, length us, event | category | flops | bytes accessed | tf_op | source)
XLA Modules:
  0.0 206.1 jit_solution(14729288088178801403)
XLA Ops:
  0.0 8.9 %collective-permute-start.1 = (bf16[512,128]{1,0:T(8,128)(2,1)}, bf16[512,128]{1,0:T(8,128)(2,1)S(1)}, u32[]{:S(2)}, u32[]{:S(2)}) collective-permute-start(bf16[512,128]{1,0:T(8,128)(2,1)} %bitcast.32), channel_id=1, source_target_pairs={{8,0},{16,8},{24,16},{32,24},{40,32},{48,40},{56,48},{64,56},{72,6... | collective-permute-start | bytes 393224 | tf_op jit(solution)/shard_map/ppermute | solution.py:291
  8.9 1.9 collective-permute-start
  13.2 4.0 %collective-permute-done.before_ref = bf16[512,128]{1,0:T(8,128)(2,1)S(1)} collective-permute-done((bf16[512,128]{1,0:T(8,128)(2,1)}, bf16[512,128]{1,0:T(8,128)(2,1)S(1)}, u32[]{:S(2)}, u32[]{:S(2)}) %collective-permute-start) | collective-permute-done | bytes 131104 | tf_op jit(solution)/shard_map/ppermute | solution.py:290
  17.9 1.0 copy-done.1
  19.8 1.0 shard_map.83
  20.8 21.4 %all_to_all.50 = f32[64,4,128]{2,1,0:T(4,128)S(1)} all-to-all(f32[64,4,128]{2,1,0:T(4,128)S(1)} %bitcast.31), channel_id=1, replica_groups=mesh['sub'=64,'coarse'=8] {'sub'}, dimensions={0} | all-to-all | bytes 262144 | tf_op jit(solution)/shard_map/all_to_all | solution.py:99
  42.7 15.2 %all_to_all.51.in_ref = f32[8,40,128]{2,1,0:T(8,128)S(1)} all-to-all(f32[8,40,128]{2,1,0:T(8,128)S(1)} %get-tuple-element.36), channel_id=1, replica_groups=mesh['sub'=64,'coarse'=8] {'coarse'}, dimensions={0} | all-to-all | bytes 327680 | tf_op jit(solution)/shard_map/all_to_all | solution.py:99
  58.0 13.6 %all_to_all.52.mine_ref = bf16[32,32,128]{2,1,0:T(8,128)(2,1)S(1)} all-to-all(bf16[32,32,128]{2,1,0:T(8,128)(2,1)S(1)} %get-tuple-element.37), channel_id=1, replica_groups={{0,16,32,48,64,80,96,112,128,144,160,176,192,208,224,240,256,272,288,30..., dimensions={0} | all-to-all | bytes 524288 | tf_op jit(solution)/shard_map/all_to_all | solution.py:99
  71.6 5.5 %collective-permute-start.2 = (bf16[32,32,128]{2,1,0:T(8,128)(2,1)S(1)}, bf16[32,32,128]{2,1,0:T(8,128)(2,1)S(1)}, u32[]{:S(2)}, u32[]{:S(2)}) collective-permute-start(bf16[32,32,128]{2,1,0:T(8,128)(2,1)S(1)} %all_to_all.52.mine_ref), channel_id=1, source_target_pairs={{0,8},{8,0},{16,24},{24,16},{32,40},{40,32},{48,56},{56,48},{64,72... | collective-permute-start | bytes 786440 | tf_op jit(solution)/shard_map/ppermute | solution.py:312
  77.1 1.1 collective-permute-done.2.theirs_ref
  78.2 2.0 shard_map.86
  80.2 19.8 %all_to_all.53.in_ref = f32[8,128,128]{2,1,0:T(8,128)S(1)} all-to-all(f32[8,128,128]{2,1,0:T(8,128)S(1)} %get-tuple-element.39), channel_id=1, replica_groups=mesh['sub'=64,'coarse'=8] {'coarse'}, dimensions={0} | all-to-all | bytes 1048576 | tf_op jit(solution)/shard_map/all_to_all | solution.py:99
  100.2 14.7 %all_to_all.54 = bf16[64,4,128]{2,1,0:T(4,128)(2,1)S(1)} all-to-all(bf16[64,4,128]{2,1,0:T(4,128)(2,1)S(1)} %bitcast.26), channel_id=1, replica_groups=mesh['sub'=64,'coarse'=8] {'sub'}, dimensions={0} | all-to-all | bytes 131072 | tf_op jit(solution)/shard_map/all_to_all | solution.py:99
  115.8 2.4 %collective-permute-start.3 = (f32[256,128]{1,0:T(8,128)S(1)}, f32[256,128]{1,0:T(8,128)S(1)}, u32[]{:S(2)}, u32[]{:S(2)}) collective-permute-start(f32[256,128]{1,0:T(8,128)S(1)} %get-tuple-element.43), channel_id=1, source_target_pairs={{0,8},{8,16},{16,24},{24,32},{32,40},{40,48},{48,56},{56,64},{64,7... | collective-permute-start | bytes 393224 | tf_op jit(solution)/shard_map/ppermute | solution.py:322
  118.2 2.0 collective-permute-start.4
  120.2 4.6 %collective-permute-done.4.next_ref = f32[256,128]{1,0:T(8,128)S(1)} collective-permute-done((f32[256,128]{1,0:T(8,128)S(1)}, f32[256,128]{1,0:T(8,128)S(1)}, u32[]{:S(2)}, u32[]{:S(2)}) %collective-permute-start.4) | collective-permute-done | bytes 131104 | tf_op jit(solution)/shard_map/ppermute | solution.py:323
  124.8 1.0 shard_map.89
  125.9 11.4 %all_to_all.55.in_ref = f32[8,56,128]{2,1,0:T(8,128)S(1)} all-to-all(f32[8,56,128]{2,1,0:T(8,128)S(1)} %get-tuple-element.48), channel_id=1, replica_groups=mesh['sub'=64,'coarse'=8] {'coarse'}, dimensions={0} | all-to-all | bytes 458752 | tf_op jit(solution)/shard_map/all_to_all | solution.py:99
  137.6 22.8 %all_to_all.56 = bf16[64,16,128]{2,1,0:T(8,128)(2,1)S(1)} all-to-all(bf16[64,16,128]{2,1,0:T(8,128)(2,1)S(1)} %bitcast.27), channel_id=1, replica_groups=mesh['sub'=64,'coarse'=8] {'sub'}, dimensions={0} | all-to-all | bytes 524288 | tf_op jit(solution)/shard_map/all_to_all | solution.py:99
  161.3 15.0 %all_to_all.57.mine_ref = bf16[32,32,128]{2,1,0:T(8,128)(2,1)S(1)} all-to-all(bf16[32,32,128]{2,1,0:T(8,128)(2,1)S(1)} %get-tuple-element.52), channel_id=1, replica_groups={{0,16,32,48,64,80,96,112,128,144,160,176,192,208,224,240,256,272,288,30..., dimensions={0} | all-to-all | bytes 524288 | tf_op jit(solution)/shard_map/all_to_all | solution.py:99
  176.3 4.1 %collective-permute-start.5 = (bf16[32,32,128]{2,1,0:T(8,128)(2,1)S(1)}, bf16[32,32,128]{2,1,0:T(8,128)(2,1)S(1)}, u32[]{:S(2)}, u32[]{:S(2)}) collective-permute-start(bf16[32,32,128]{2,1,0:T(8,128)(2,1)S(1)} %all_to_all.57.mine_ref), channel_id=1, source_target_pairs={{0,8},{8,0},{16,24},{24,16},{32,40},{40,32},{48,56},{56,48},{64,72... | collective-permute-start | bytes 786440 | tf_op jit(solution)/shard_map/ppermute | solution.py:337
  181.5 1.6 shard_map.93
  183.1 9.8 %all_to_all.58 = f32[16,2,128]{2,1,0:T(2,128)S(1)} all-to-all(f32[16,2,128]{2,1,0:T(2,128)S(1)} %broadcast_in_dim.9), channel_id=1, replica_groups={{0,1,2,3,4,5,6,7,8,9,10,11,12,13,14,15},{16,17,18,19,20,21,22,23,24,25,..., dimensions={0} | all-to-all | bytes 32768 | tf_op jit(solution)/shard_map/all_to_all | solution.py:99
  193.0 12.3 %all_to_all.59 = f32[32,2,128]{2,1,0:T(2,128)S(1)} all-to-all(f32[32,2,128]{2,1,0:T(2,128)S(1)} %broadcast_in_dim.10), channel_id=1, replica_groups={{0,16,32,48,64,80,96,112,128,144,160,176,192,208,224,240,256,272,288,30..., dimensions={0} | all-to-all | bytes 65536 | tf_op jit(solution)/shard_map/all_to_all | solution.py:99
  (36 shorter events, 8.8 us)
Async XLA Ops:
  0.0 11.7 %copy-start.3 = (bf16[1,24,512]{2,1,0:T(8,128)(2,1)S(1)}, bf16[1,24,512]{2,1,0:T(8,128)(2,1)}, u32[]{:S(2)}) copy-start(bf16[1,24,512]{2,1,0:T(8,128)(2,1)} %param.10) | copy-start | bytes 73732
  0.0 13.2 %collective-permute-start.1 = (bf16[512,128]{1,0:T(8,128)(2,1)}, bf16[512,128]{1,0:T(8,128)(2,1)S(1)}, u32[]{:S(2)}, u32[]{:S(2)}) collective-permute-start(bf16[512,128]{1,0:T(8,128)(2,1)} %bitcast.32), channel_id=1, source_target_pairs={{8,0},{16,8},{24,16},{32,24},{40,32},{48,40},{56,48},{64,56},{72,6... | collective-permute-start | bytes 393224 | tf_op jit(solution)/shard_map/ppermute | solution.py:291
  8.9 8.3 %collective-permute-start = (bf16[512,128]{1,0:T(8,128)(2,1)}, bf16[512,128]{1,0:T(8,128)(2,1)S(1)}, u32[]{:S(2)}, u32[]{:S(2)}) collective-permute-start(bf16[512,128]{1,0:T(8,128)(2,1)} %bitcast.33), channel_id=1, source_target_pairs={{0,8},{8,16},{16,24},{24,32},{32,40},{40,48},{48,56},{56,64},{64,7... | collective-permute-start | bytes 393224 | tf_op jit(solution)/shard_map/ppermute | solution.py:290
  11.7 0.7 copy-start.7
  17.2 0.7 copy-start.5
  17.2 0.7 copy-start.6
  17.8 1.0 copy-start.1
  18.9 0.9 copy-start.4
  19.8 58.4 %copy-start = (bf16[2048,256]{1,0:T(8,128)(2,1)S(1)}, bf16[2048,256]{1,0:T(8,128)(2,1)}, u32[]{:S(2)}) copy-start(bf16[2048,256]{1,0:T(8,128)(2,1)} %inverse_ref.3) | copy-start | bytes 3145732
  71.6 6.6 %collective-permute-start.2 = (bf16[32,32,128]{2,1,0:T(8,128)(2,1)S(1)}, bf16[32,32,128]{2,1,0:T(8,128)(2,1)S(1)}, u32[]{:S(2)}, u32[]{:S(2)}) collective-permute-start(bf16[32,32,128]{2,1,0:T(8,128)(2,1)S(1)} %all_to_all.52.mine_ref), channel_id=1, source_target_pairs={{0,8},{8,0},{16,24},{24,16},{32,40},{40,32},{48,56},{56,48},{64,72... | collective-permute-start | bytes 786440 | tf_op jit(solution)/shard_map/ppermute | solution.py:312
  115.8 4.3 %collective-permute-start.3 = (f32[256,128]{1,0:T(8,128)S(1)}, f32[256,128]{1,0:T(8,128)S(1)}, u32[]{:S(2)}, u32[]{:S(2)}) collective-permute-start(f32[256,128]{1,0:T(8,128)S(1)} %get-tuple-element.43), channel_id=1, source_target_pairs={{0,8},{8,16},{16,24},{24,32},{32,40},{40,48},{48,56},{56,64},{64,7... | collective-permute-start | bytes 393224 | tf_op jit(solution)/shard_map/ppermute | solution.py:322
  118.2 6.6 %collective-permute-start.4 = (f32[256,128]{1,0:T(8,128)S(1)}, f32[256,128]{1,0:T(8,128)S(1)}, u32[]{:S(2)}, u32[]{:S(2)}) collective-permute-start(f32[256,128]{1,0:T(8,128)S(1)} %get-tuple-element.44), channel_id=1, source_target_pairs={{8,0},{16,8},{24,16},{32,24},{40,32},{48,40},{56,48},{64,56},{72,6... | collective-permute-start | bytes 393224 | tf_op jit(solution)/shard_map/ppermute | solution.py:323
  160.4 19.9 %copy-start.2 = (bf16[1,512,512]{2,1,0:T(8,128)(2,1)S(1)}, bf16[1,512,512]{2,1,0:T(8,128)(2,1)}, u32[]{:S(2)}) copy-start(bf16[1,512,512]{2,1,0:T(8,128)(2,1)} %param.9) | copy-start | bytes 1572868
  176.3 5.2 %collective-permute-start.5 = (bf16[32,32,128]{2,1,0:T(8,128)(2,1)S(1)}, bf16[32,32,128]{2,1,0:T(8,128)(2,1)S(1)}, u32[]{:S(2)}, u32[]{:S(2)}) collective-permute-start(bf16[32,32,128]{2,1,0:T(8,128)(2,1)S(1)} %all_to_all.57.mine_ref), channel_id=1, source_target_pairs={{0,8},{8,0},{16,24},{24,16},{32,40},{40,32},{48,56},{56,48},{64,72... | collective-permute-start | bytes 786440 | tf_op jit(solution)/shard_map/ppermute | solution.py:337

commit v5 on v4

--- a/solution.py
+++ b/solution.py
@@ -48,16 +48,21 @@
     return out
 
 
-def run(kernel, outs, *args):
+ANY = pl.BlockSpec(memory_space=pl.ANY)
+SMEM = pl.BlockSpec(memory_space=pltpu.SMEM)
+VMEM = pl.BlockSpec(memory_space=pltpu.VMEM)
+
+
+def run(kernel, outs, *args, specs=None, scratch=()):
     def spec(x):
-        small = jnp.issubdtype(x.dtype, jnp.integer) and x.size <= 8
-        return pl.BlockSpec(memory_space=pltpu.SMEM if small else pltpu.VMEM)
+        return SMEM if jnp.issubdtype(x.dtype, jnp.integer) and x.size <= 32 and x.shape[1] <= 8 else VMEM
 
     return pl.pallas_call(
         kernel,
         out_shape=[jax.ShapeDtypeStruct(shape, dtype) for shape, dtype in outs],
-        in_specs=[spec(x) for x in args],
-        out_specs=[pl.BlockSpec(memory_space=pltpu.VMEM)] * len(outs),
+        in_specs=specs or [spec(x) for x in args],
+        out_specs=[SMEM if dtype == I32 else VMEM for _, dtype in outs],
+        scratch_shapes=scratch,
         compiler_params=pltpu.CompilerParams(vmem_limit_bytes=32 * 1024 * 1024),
     )(*args)
 
@@ -98,20 +103,39 @@
     def exchange(blocks, axis, groups=None):
         return lax.all_to_all(blocks, axis, 0, 0, tiled=True, axis_index_groups=groups)
 
-    def faces_next(here_ref, sub_ref, e):
-        return lax.rem(lax.div(sub_ref[0, e], n_coarse) - here_ref[0, 0] + n_sub, n_sub) == 1
-
     def edge(e):
         return slice(e * width, (e + 1) * width)
 
-    def set_up(here_ref, owner_ref, offset_ref, coupling_ref, slotted_ref, asked_ref, codes_ref):
+    def set_up(
+        here_ref, sub_ref, edge_ref, owner_ref, offset_ref, coupling_hbm, schur_hbm, load_hbm,
+        slotted_ref, turned_ref, asked_ref, codes_ref, table_ref, coupling_ref, schur_ref, load_ref, sems,
+    ):
+        moves = [(coupling_hbm, coupling_ref), (load_hbm, load_ref), (schur_hbm, schur_ref)]
+        moves = [pltpu.make_async_copy(a, b, sems.at[k]) for k, (a, b) in enumerate(moves)]
+        for move in moves:
+            move.start()
+        faces = []
+        for e in range(edges):
+            side = lax.rem(lax.div(sub_ref[0, e], n_coarse) - here_ref[0, 0] + n_sub, n_sub) == 1
+            faces.append(side.astype(I32))
+        ahead = jnp.int32(0)
+        for e in range(edges):
+            place = jnp.int32(0)
+            for other in range(edges):
+                if other != e:
+                    lower = (faces[other] == faces[e]) & (edge_ref[0, other] < edge_ref[0, e])
+                    place = place + lower.astype(I32)
+            table_ref[0, e] = faces[e]
+            table_ref[1, e] = place
+            table_ref[2, e] = faces[e] * ahead + (1 - faces[e]) * (e - ahead)
+            ahead = ahead + faces[e]
         same = iota((prims, prims), 0) == iota((prims, prims), 1)
-        owner_row = jnp.sum(jnp.where(same, owner_ref[...], 0), axis=0, keepdims=True)
-        before = (owner_ref[...] == owner_row) & (iota((prims, prims), 0) < iota((prims, prims), 1))
+        owner_row = owner_ref[...]
+        owner_col = jnp.sum(jnp.where(same, owner_row, 0), axis=1, keepdims=True)
+        before = (owner_col == owner_row) & (iota((prims, prims), 0) < iota((prims, prims), 1))
         second = jnp.sum(jnp.where(before, 1, 0), axis=0, keepdims=True)
         line = iota((lines, prims), 0)
-        placed = line == owner_row * LINES + second
-        slotted_ref[...] = dot(ones_where(placed), coupling_ref[...]).astype(BF16)
+        placed = ones_where(line == owner_row * LINES + second)
         lane = iota((lines, slots), 1)
         asked = jnp.zeros((lines, slots), I32)
         for k in range(CAPACITY):
@@ -126,16 +150,23 @@
         codes_ref[...] = jnp.zeros((SIDES, cases), F32)
         for k in range(n_coarse * ROOM // cases):
             codes_ref[k + 1 : k + 2, :] = codes[:, k * cases : (k + 1) * cases]
+        moves[0].wait()
+        slotted_ref[...] = dot(placed, coupling_ref[...]).astype(BF16)
+        turned_ref[...] = lax.dot_general(
+            coupling_ref[...], placed, (((0,), (1,)), ((), ())), preferred_element_type=F32
+        ).astype(BF16)
+        moves[1].wait()
+        moves[2].wait()
 
     def first(
-        here_ref, sub_ref, edge_ref, load_ref, before_ref, next_ref, schur_ref, slotted_ref, asked_ref, coupling_ref,
+        table_ref, edge_ref, load_ref, before_ref, next_ref, schur_ref, slotted_ref, asked_ref, coupling_ref,
         residual_ref, local_ref, out_ref, near_ref, old_ref,
     ):
         for e in range(edges):
             start = pl.multiple_of(edge_ref[0, e] * width, width)
             ahead = next_ref[pl.ds(start, width), :].astype(F32)
             behind = before_ref[pl.ds(start, width), :].astype(F32)
-            facing = jnp.where(faces_next(here_ref, sub_ref, e), ahead, behind)
+            facing = jnp.where(table_ref[0, e] == 1, ahead, behind)
             residual_ref[edge(e), :] = load_ref[edge(e), :].astype(F32) - facing
         twice = 2.0 * residual_ref[...]
         jumps, rest = in_two(twice)
@@ -165,29 +196,32 @@
             out_ref[c, :piece] = partial[c * piece : (c + 1) * piece]
             out_ref[c, piece:] = sides
 
-    def coarse_sums(in_ref, rhs_ref, marks_ref, codes_ref):
+    def coarse_sums(in_ref, rhs_ref, marks_ref, turned_ref, codes_ref):
         total = in_ref[0]
         for c in range(1, n_coarse):
             total = total + in_ref[c]
         rhs = total[:piece].astype(BF16)
         for k in range(chips):
             rhs_ref[k] = rhs
-        ids = (iota((block, slots), 0) + 1).astype(F32)
-        for c in range(n_coarse):
-            marks_ref[:, c * slots : (c + 1) * slots] = ones_where(ids == in_ref[c, piece : piece + 1])
         codes_ref[...] = total[piece:]
-
-    def product(here_ref, mine_ref, theirs_ref, inverse_ref, both_ref):
-        core = lax.rem(here_ref[0, 0], 2)
-        for k in range(chips):
-            both_ref[pl.ds(pl.multiple_of((2 * k + core) * piece, piece), piece), :] = mine_ref[k]
-            both_ref[pl.ds(pl.multiple_of((2 * k + 1 - core) * piece, piece), piece), :] = theirs_ref[k]
-        return dot_t(inverse_ref[...], both_ref[...])
-
-    def answer(here_ref, mine_ref, theirs_ref, inverse_ref, marks_ref, both_ref, out_ref):
-        share = in_three(product(here_ref, mine_ref, theirs_ref, inverse_ref, both_ref))
-        for c in range(n_coarse):
-            out_ref[c] = joined(dot_t(marks_ref[:, c * slots : (c + 1) * slots], share), 3)
+        down = (iota((block, slots), 0) + 1).astype(F32)
+        across = (iota((slots, block), 1) + 1).astype(F32)
+        asked = jnp.concatenate([in_ref[c, piece : piece + 1] for c in range(n_coarse)], axis=0)
+        turned = jnp.transpose(asked)
+        for c in range(n_coarse):
+            marks_ref[:, c * slots : (c + 1) * slots] = ones_where(down == asked[c : c + 1])
+            turned_ref[c * slots : (c + 1) * slots] = ones_where(across == turned[:, c : c + 1])
+
+    def product(mine, theirs):
+        both = jnp.where(
+            sub_index % 2 == 0, jnp.concatenate([mine, theirs], axis=1), jnp.concatenate([theirs, mine], axis=1)
+        )
+        return dot_t(coarse_inverse, both.reshape(rows, cases))
+
+    def answer(share_ref, turned_ref, out_ref):
+        out = joined(dot(turned_ref[...], in_three(share_ref[...])), 3)
+        for c in range(n_coarse):
+            out_ref[c] = out[c * slots : (c + 1) * slots]
 
     def reply(in_ref, given_ref, near_ref, out_ref):
         solved = in_ref[0]
@@ -201,37 +235,28 @@
         wide = jnp.where(line == CAPACITY, high.astype(F32), wide)
         out_ref[...] = jnp.where(line == CAPACITY + 1, low.astype(F32), wide).astype(BF16)
 
-    def back(here_ref, sub_ref, in_ref, slotted_ref, local_ref, image_ref, ahead_ref, behind_ref, curvature_ref):
+    def back(table_ref, in_ref, turned_ref, local_ref, image_ref, ahead_ref, behind_ref, curvature_ref):
         replies = in_ref[...]
-        image_ref[...] = local_ref[...] + dot_t(slotted_ref[...], replies)
+        image_ref[...] = local_ref[...] + dot(turned_ref[...], replies)
         line = iota((lines, cases), 0) & (LINES - 1)
         curvature_ref[...] = jnp.sum(jnp.where(line >= CAPACITY, replies.astype(F32), 0.0), axis=0, keepdims=True)
-        ahead = jnp.int32(0)
-        for e in range(edges):
-            faces = faces_next(here_ref, sub_ref, e)
-
-            @pl.when(faces)
+        for e in range(edges):
+            place = pl.ds(pl.multiple_of(table_ref[2, e] * width, width), width)
+
+            @pl.when(table_ref[0, e] == 1)
             def _():
-                ahead_ref[pl.ds(pl.multiple_of(ahead * width, width), width), :] = image_ref[edge(e), :]
-
-            @pl.when(jnp.logical_not(faces))
+                ahead_ref[place, :] = image_ref[edge(e), :]
+
+            @pl.when(table_ref[0, e] == 0)
             def _():
-                behind_ref[pl.ds(pl.multiple_of((e - ahead) * width, width), width), :] = image_ref[edge(e), :]
-
-            ahead = ahead + faces.astype(I32)
+                behind_ref[place, :] = image_ref[edge(e), :]
 
     def coupled_rows(
-        here_ref, sub_ref, edge_ref, image_ref, before_ref, next_ref, coupling_ref, old_ref, curvature_ref, norm_ref,
-        jump_ref, out_ref,
+        table_ref, image_ref, before_ref, next_ref, coupling_ref, old_ref, curvature_ref, norm_ref, jump_ref, out_ref
     ):
         for e in range(edges):
-            faces = faces_next(here_ref, sub_ref, e)
-            place = jnp.int32(0)
-            for other in range(edges):
-                alike = faces_next(here_ref, sub_ref, other) == faces
-                place = place + (alike & (edge_ref[0, other] < edge_ref[0, e])).astype(I32)
-            start = pl.multiple_of(place * width, width)
-            facing = jnp.where(faces, next_ref[pl.ds(start, width), :], before_ref[pl.ds(start, width), :])
+            place = pl.ds(pl.multiple_of(table_ref[1, e] * width, width), width)
+            facing = jnp.where(table_ref[0, e] == 1, next_ref[place, :], before_ref[place, :])
             jump_ref[edge(e), :] = image_ref[edge(e), :] - facing
         pair = jnp.concatenate(in_two(2.0 * jump_ref[...]), axis=1)
         new = joined(dot(coupling_ref[...], pair), 2)
@@ -276,70 +301,68 @@
         norm = jnp.sum(remainder * remainder, axis=0, keepdims=True)
         sums_ref[...] = jnp.where(line == 0, near, jnp.where(line == 1, norm, 0.0))
 
-    def energy(here_ref, mine_ref, theirs_ref, inverse_ref, weights_ref, sums_ref, both_ref, out_ref):
-        share = product(here_ref, mine_ref, theirs_ref, inverse_ref, both_ref)
-        far = jnp.sum(weights_ref[...] * share, axis=0, keepdims=True)
-        out_ref[...] = sums_ref[...] + jnp.where(iota((SIDES, cases), 0) == 0, far, 0.0)
-
     field = ((order, cases), F32)
     row = ((1, cases), F32)
     gathered = ((chips, piece, cases), BF16)
-    owners = primal_owner.reshape(prims, 1)
-    offsets = primal_offset.reshape(1, prims)
+    scalars_shape = ((SIDES, cases), F32)
+    owners = primal_owner.reshape(1, prims)
     start = load[0]
     from_before = lax.ppermute(start, "sub", to_next)
     from_next = lax.ppermute(start, "sub", to_before)
-    slotted, asked, codes = run(
+    slotted, turned, asked, codes, table, coupling_here, schur_here, load_here = run(
         set_up,
-        [((lines, order), BF16), ((lines, slots), F32), ((SIDES, cases), F32)],
-        here,
-        owners,
-        offsets,
-        coupling[0],
+        [
+            ((lines, order), BF16),
+            ((order, lines), BF16),
+            ((lines, slots), F32),
+            scalars_shape,
+            ((3, edges), I32),
+            ((prims, order), BF16),
+            ((order, order), BF16),
+            ((order, cases), BF16),
+        ],
+        here, neighbour_sub, neighbour_edge, owners, primal_offset, coupling[0], schur[0], start,
+        specs=[SMEM] * 3 + [VMEM] * 2 + [ANY] * 3,
+        scratch=[pltpu.SemaphoreType.DMA((3,))],
     )
     residual, local, outgoing, near, old = run(
         first,
         [field, field, ((lines, cases), F32), row, ((prims, cases), F32)],
-        here, neighbour_sub, neighbour_edge, start, from_before, from_next, schur[0], slotted, asked, coupling[0],
+        table, neighbour_edge, load_here, from_before, from_next, schur_here, slotted, asked, coupling_here,
     )
     given = exchange(outgoing.reshape(n_sub, LINES, cases), "sub").reshape(lines, cases)
     outgoing, norm = run(owner_sums, [((n_coarse, piece + SIDES, cases), F32), row], given, codes)
     incoming = exchange(outgoing, "coarse")
-    rhs, marks, codes = run(
-        coarse_sums, [gathered, ((block, n_coarse * slots), BF16), ((SIDES, cases), F32)], incoming
+    rhs, marks, marks_turned, codes = run(
+        coarse_sums,
+        [gathered, ((block, n_coarse * slots), BF16), ((n_coarse * slots, block), BF16), scalars_shape],
+        incoming,
     )
     mine = exchange(rhs, "sub", same_core)
     theirs = lax.ppermute(mine, "sub", other_core)
-    both = ((rows, cases), BF16)
-    _, outgoing = run(answer, [both, ((n_coarse, slots, cases), F32)], here, mine, theirs, coarse_inverse, marks)
+    (outgoing,) = run(answer, [((n_coarse, slots, cases), F32)], product(mine, theirs), marks_turned)
     incoming = exchange(outgoing, "coarse")
     (outgoing,) = run(reply, [((lines, cases), BF16)], incoming, given, near)
     replies = exchange(outgoing.reshape(n_sub, LINES, cases), "sub").reshape(lines, cases)
     side = ((half * width, cases), F32)
-    image, ahead, behind, curvature = run(
-        back, [field, side, side, row], here, neighbour_sub, replies, slotted, local
-    )
+    image, ahead, behind, curvature = run(back, [field, side, side, row], table, replies, turned, local)
     from_before = lax.ppermute(ahead, "sub", to_next)
     from_next = lax.ppermute(behind, "sub", to_before)
     image, outgoing = run(
         coupled_rows,
         [field, ((n_coarse, 2 * prims + SIDES, cases), F32)],
-        here, neighbour_sub, neighbour_edge, image, from_before, from_next, coupling[0], old, curvature, norm,
+        table, image, from_before, from_next, coupling_here, old, curvature, norm,
     )
     incoming = exchange(outgoing, "coarse")
-    outgoing, scalars = run(
-        spread, [((n_coarse * slots, cases), BF16), ((SIDES, cases), F32)], incoming, codes
-    )
+    outgoing, scalars = run(spread, [((n_coarse * slots, cases), BF16), scalars_shape], incoming, codes)
     incoming = exchange(outgoing.reshape(n_sub, n_coarse * CAPACITY, cases), "sub")
     incoming = incoming.transpose(1, 0, 2).reshape(n_coarse * slots, cases)
     weights, rhs = run(owner_rows, [((block, cases), F32), gathered], here, incoming, marks)
     mine = exchange(rhs, "sub", same_core)
     theirs = lax.ppermute(mine, "sub", other_core)
-    remainder, sums = run(second, [field, ((SIDES, cases), F32)], residual, image, scalars, schur[0])
-    _, sums = run(
-        energy, [both, ((SIDES, cases), F32)], here, mine, theirs, coarse_inverse, weights, sums
-    )
-    sums = sums[:2]
+    remainder, sums = run(second, [field, scalars_shape], residual, image, scalars, schur_here)
+    far = jnp.sum(weights * product(mine, theirs), axis=0)
+    sums = jnp.stack([sums[0] + far, sums[1]])
     for groups in (columns, planes):
         wide = jnp.broadcast_to(sums[None], (len(groups[0]),) + sums.shape)
         sums = jnp.sum(exchange(wide, ("sub", "coarse"), groups), axis=0)

time: 207 us -> 210 us (1.014)
  waiting for transfers between devices: 10.5 us -> 6.91 us
  local copies, waits for them, and re-layouts: 4.11 us -> 7.49 us
    unnamed x16 -> x36, local copies, waits for them, and re-layouts: 3.28 us -> 7.4 us
    ppermute x1, waiting for transfers between devices: 3.96 us -> 0.01 us  [body(): from_before = lax.ppermute(start, 'sub', to_next)]
    all_to_all x10, blocking collectives: 156 us -> 158 us  [exchange(): lax.all_to_all(blocks, axis, 0, 0, tiled=True, axis_index_groups=groups)]
    pallas_call x12 -> x11, Pallas kernels: 9.74 us -> 7.74 us  [run(): pl.pallas_call(kernel, out_shape=[jax.ShapeDtypeStruct(shape, dtype) for...]
  transfers between devices with their start and end apart: 6 -> 6, of which waited for: 4 -> 3; matrix products, arithmetic and copies ran while one was open for 0% -> 0% of each run, Pallas kernels for 1% -> 1%
where the time goes in v5:
time: 210 us; the launch traced here: 209 us
  blocking collectives  158 us (75%)
  starting transfers between devices  24.7 us (12%)
  Pallas kernels  7.74 us (4%)
  local copies, waits for them, and re-layouts  7.49 us (4%)
  waiting for transfers between devices  6.91 us (3%)
  other arithmetic  2.43 us (1%)
    all_to_all x10, blocking collectives, exchange(): lax.all_to_all(blocks, axis, 0, 0, tiled=True, axis_index_groups=groups)  158 us
    ppermute x2, starting transfers between devices, body(): theirs = lax.ppermute(mine, 'sub', other_core)  9.52 us
    ppermute x1, starting transfers between devices, body(): from_next = lax.ppermute(start, 'sub', to_before)  8.91 us
    pallas_call x11, Pallas kernels, run(): pl.pallas_call(kernel, out_shape=[jax.ShapeDtypeStruct(shape, dtype) for...  7.74 us
    unnamed x36, local copies, waits for them, and re-layouts  7.4 us
    ppermute x1, waiting for transfers between devices, body(): from_next = lax.ppermute(behind, 'sub', to_before)  4.62 us
  transfers between devices with their start and end apart: 6, of which 3 were waited for; matrix products, arithmetic and copies ran while one was open for 0% of the time, Pallas kernels for 1%

profile of v5, /device:TPU:1, one launch (start us, length us, event | category | flops | bytes accessed | tf_op | source)
XLA Modules:
  0.0 208.9 jit_solution(6918657184006354056)
XLA Ops:
  0.0 8.9 %collective-permute-start.1 = (bf16[512,128]{1,0:T(8,128)(2,1)}, bf16[512,128]{1,0:T(8,128)(2,1)S(1)}, u32[]{:S(2)}, u32[]{:S(2)}) collective-permute-start(bf16[512,128]{1,0:T(8,128)(2,1)} %bitcast.44), channel_id=1, source_target_pairs={{8,0},{16,8},{24,16},{32,24},{40,32},{48,40},{56,48},{64,56},{72,6... | collective-permute-start | bytes 393224 | tf_op jit(solution)/shard_map/ppermute | solution.py:311
  8.9 1.9 collective-permute-start
  11.6 1.0 copy-done.1
  12.6 0.9 copy-done.2
  15.5 2.1 shard_map.82
  17.6 1.1 shard_map.83
  19.2 23.1 %all_to_all.50 = f32[64,4,128]{2,1,0:T(4,128)S(1)} all-to-all(f32[64,4,128]{2,1,0:T(4,128)S(1)} %bitcast.43), channel_id=1, replica_groups=mesh['sub'=64,'coarse'=8] {'sub'}, dimensions={0} | all-to-all | bytes 262144 | tf_op jit(solution)/shard_map/all_to_all | solution.py:104
  43.2 15.2 %all_to_all.51.in_ref = f32[8,40,128]{2,1,0:T(8,128)S(1)} all-to-all(f32[8,40,128]{2,1,0:T(8,128)S(1)} %get-tuple-element.44), channel_id=1, replica_groups=mesh['sub'=64,'coarse'=8] {'coarse'}, dimensions={0} | all-to-all | bytes 327680 | tf_op jit(solution)/shard_map/all_to_all | solution.py:104
  58.8 14.2 %all_to_all.52 = bf16[32,32,128]{2,1,0:T(8,128)(2,1)} all-to-all(bf16[32,32,128]{2,1,0:T(8,128)(2,1)S(1)} %get-tuple-element.45), channel_id=1, replica_groups={{0,16,32,48,64,80,96,112,128,144,160,176,192,208,224,240,256,272,288,30..., dimensions={0} | all-to-all | bytes 524288 | tf_op jit(solution)/shard_map/all_to_all | solution.py:104
  73.1 5.4 %collective-permute-start.2 = (bf16[32,32,128]{2,1,0:T(8,128)(2,1)}, bf16[32,32,128]{2,1,0:T(8,128)(2,1)}, u32[]{:S(2)}, u32[]{:S(2)}) collective-permute-start(bf16[32,32,128]{2,1,0:T(8,128)(2,1)} %all_to_all.52), channel_id=1, source_target_pairs={{0,8},{8,0},{16,24},{24,16},{32,40},{40,32},{48,56},{56,48},{64,72... | collective-permute-start | bytes 786440 | tf_op jit(solution)/shard_map/ppermute | solution.py:342
  78.5 1.5 collective-permute-done.2
  80.0 1.3 maximum_select_fusion
  82.3 19.2 %all_to_all.53.in_ref = f32[8,128,128]{2,1,0:T(8,128)S(1)} all-to-all(f32[8,128,128]{2,1,0:T(8,128)S(1)} %shard_map.86), channel_id=1, replica_groups=mesh['sub'=64,'coarse'=8] {'coarse'}, dimensions={0} | all-to-all | bytes 1048576 | tf_op jit(solution)/shard_map/all_to_all | solution.py:104
  102.3 15.4 %all_to_all.54 = bf16[64,4,128]{2,1,0:T(4,128)(2,1)S(1)} all-to-all(bf16[64,4,128]{2,1,0:T(4,128)(2,1)S(1)} %bitcast.41), channel_id=1, replica_groups=mesh['sub'=64,'coarse'=8] {'sub'}, dimensions={0} | all-to-all | bytes 131072 | tf_op jit(solution)/shard_map/all_to_all | solution.py:104
  117.6 0.9 shard_map.88
  118.6 2.4 %collective-permute-start.3 = (f32[256,128]{1,0:T(8,128)S(1)}, f32[256,128]{1,0:T(8,128)S(1)}, u32[]{:S(2)}, u32[]{:S(2)}) collective-permute-start(f32[256,128]{1,0:T(8,128)S(1)} %get-tuple-element.51), channel_id=1, source_target_pairs={{0,8},{8,16},{16,24},{24,32},{32,40},{40,48},{48,56},{56,64},{64,7... | collective-permute-start | bytes 393224 | tf_op jit(solution)/shard_map/ppermute | solution.py:349
  120.9 1.9 collective-permute-start.4
  122.9 4.6 %collective-permute-done.4.next_ref = f32[256,128]{1,0:T(8,128)S(1)} collective-permute-done((f32[256,128]{1,0:T(8,128)S(1)}, f32[256,128]{1,0:T(8,128)S(1)}, u32[]{:S(2)}, u32[]{:S(2)}) %collective-permute-start.4) | collective-permute-done | bytes 131104 | tf_op jit(solution)/shard_map/ppermute | solution.py:350
  128.9 11.4 %all_to_all.55.in_ref = f32[8,56,128]{2,1,0:T(8,128)S(1)} all-to-all(f32[8,56,128]{2,1,0:T(8,128)S(1)} %get-tuple-element.56), channel_id=1, replica_groups=mesh['sub'=64,'coarse'=8] {'coarse'}, dimensions={0} | all-to-all | bytes 458752 | tf_op jit(solution)/shard_map/all_to_all | solution.py:104
  140.6 22.8 %all_to_all.56 = bf16[64,16,128]{2,1,0:T(8,128)(2,1)S(1)} all-to-all(bf16[64,16,128]{2,1,0:T(8,128)(2,1)S(1)} %bitcast.42), channel_id=1, replica_groups=mesh['sub'=64,'coarse'=8] {'sub'}, dimensions={0} | all-to-all | bytes 524288 | tf_op jit(solution)/shard_map/all_to_all | solution.py:104
  165.0 15.0 %all_to_all.57 = bf16[32,32,128]{2,1,0:T(8,128)(2,1)S(1)} all-to-all(bf16[32,32,128]{2,1,0:T(8,128)(2,1)S(1)} %get-tuple-element.65), channel_id=1, replica_groups={{0,16,32,48,64,80,96,112,128,144,160,176,192,208,224,240,256,272,288,30..., dimensions={0} | all-to-all | bytes 524288 | tf_op jit(solution)/shard_map/all_to_all | solution.py:104
  180.0 4.1 %collective-permute-start.5 = (bf16[32,32,128]{2,1,0:T(8,128)(2,1)S(1)}, bf16[32,32,128]{2,1,0:T(8,128)(2,1)S(1)}, u32[]{:S(2)}, u32[]{:S(2)}) collective-permute-start(bf16[32,32,128]{2,1,0:T(8,128)(2,1)S(1)} %all_to_all.57), channel_id=1, source_target_pairs={{0,8},{8,0},{16,24},{24,16},{32,40},{40,32},{48,56},{56,48},{64,72... | collective-permute-start | bytes 786440 | tf_op jit(solution)/shard_map/ppermute | solution.py:362
  186.0 9.8 %all_to_all.58 = f32[16,2,128]{2,1,0:T(2,128)S(1)} all-to-all(f32[16,2,128]{2,1,0:T(2,128)S(1)} %broadcast_in_dim.9), channel_id=1, replica_groups={{0,1,2,3,4,5,6,7,8,9,10,11,12,13,14,15},{16,17,18,19,20,21,22,23,24,25,..., dimensions={0} | all-to-all | bytes 32768 | tf_op jit(solution)/shard_map/all_to_all | solution.py:104
  195.8 12.3 %all_to_all.59 = f32[32,2,128]{2,1,0:T(2,128)S(1)} all-to-all(f32[32,2,128]{2,1,0:T(2,128)S(1)} %broadcast_in_dim.10), channel_id=1, replica_groups={{0,16,32,48,64,80,96,112,128,144,160,176,192,208,224,240,256,272,288,30..., dimensions={0} | all-to-all | bytes 65536 | tf_op jit(solution)/shard_map/all_to_all | solution.py:104
  (59 shorter events, 12.2 us)
Async XLA Ops:
  0.0 81.3 %copy-start = (bf16[2048,256]{1,0:T(8,128)(2,1)S(1)}, bf16[2048,256]{1,0:T(8,128)(2,1)}, u32[]{:S(2)}) copy-start(bf16[2048,256]{1,0:T(8,128)(2,1)} %param.11) | copy-start | bytes 3145732
  0.0 11.5 %copy-start.5 = (bf16[1,24,512]{2,1,0:T(8,128)(2,1)S(1)}, bf16[1,24,512]{2,1,0:T(8,128)(2,1)}, u32[]{:S(2)}) copy-start(bf16[1,24,512]{2,1,0:T(8,128)(2,1)} %param.10) | copy-start | bytes 73732
  0.0 17.6 %collective-permute-start.1 = (bf16[512,128]{1,0:T(8,128)(2,1)}, bf16[512,128]{1,0:T(8,128)(2,1)S(1)}, u32[]{:S(2)}, u32[]{:S(2)}) collective-permute-start(bf16[512,128]{1,0:T(8,128)(2,1)} %bitcast.44), channel_id=1, source_target_pairs={{8,0},{16,8},{24,16},{32,24},{40,32},{48,40},{56,48},{64,56},{72,6... | collective-permute-start | bytes 393224 | tf_op jit(solution)/shard_map/ppermute | solution.py:311
  8.9 8.7 %collective-permute-start = (bf16[512,128]{1,0:T(8,128)(2,1)}, bf16[512,128]{1,0:T(8,128)(2,1)S(1)}, u32[]{:S(2)}, u32[]{:S(2)}) collective-permute-start(bf16[512,128]{1,0:T(8,128)(2,1)} %bitcast.45), channel_id=1, source_target_pairs={{0,8},{8,16},{16,24},{24,32},{32,40},{40,48},{48,56},{56,64},{64,7... | collective-permute-start | bytes 393224 | tf_op jit(solution)/shard_map/ppermute | solution.py:310
  10.9 0.6 copy-start.9
  10.9 0.7 copy-start.8
  11.6 1.0 copy-start.1
  12.6 0.9 copy-start.2
  13.5 0.7 copy-start.11
  14.2 0.7 copy-start.12
  14.9 0.7 copy-start.13
  17.6 1.1 copy-start.3
  18.7 0.5 copy-start.14
  42.6 0.5 copy-start.16
  58.8 14.3 %copy-start.6 = (f32[8,128]{1,0:T(8,128)}, f32[8,128]{1,0:T(8,128)S(1)}, u32[]{:S(2)}) copy-start(f32[8,128]{1,0:T(8,128)S(1)} %get-tuple-element.57.codes_ref) | copy-start | bytes 12292
  73.1 6.9 %collective-permute-start.2 = (bf16[32,32,128]{2,1,0:T(8,128)(2,1)}, bf16[32,32,128]{2,1,0:T(8,128)(2,1)}, u32[]{:S(2)}, u32[]{:S(2)}) collective-permute-start(bf16[32,32,128]{2,1,0:T(8,128)(2,1)} %all_to_all.52), channel_id=1, source_target_pairs={{0,8},{8,0},{16,24},{24,16},{32,40},{40,32},{48,56},{56,48},{64,72... | collective-permute-start | bytes 786440 | tf_op jit(solution)/shard_map/ppermute | solution.py:342
  101.5 0.6 copy-start.15
  117.6 9.9 %copy-start.4 = (bf16[24,512]{1,0:T(8,128)(2,1)S(1)}, bf16[24,512]{1,0:T(8,128)(2,1)}, u32[]{:S(2)}) copy-start(bf16[24,512]{1,0:T(8,128)(2,1)} %copy-done.3) | copy-start | bytes 73732
  118.6 4.3 %collective-permute-start.3 = (f32[256,128]{1,0:T(8,128)S(1)}, f32[256,128]{1,0:T(8,128)S(1)}, u32[]{:S(2)}, u32[]{:S(2)}) collective-permute-start(f32[256,128]{1,0:T(8,128)S(1)} %get-tuple-element.51), channel_id=1, source_target_pairs={{0,8},{8,16},{16,24},{24,32},{32,40},{40,48},{48,56},{56,64},{64,7... | collective-permute-start | bytes 393224 | tf_op jit(solution)/shard_map/ppermute | solution.py:349
  120.9 6.6 %collective-permute-start.4 = (f32[256,128]{1,0:T(8,128)S(1)}, f32[256,128]{1,0:T(8,128)S(1)}, u32[]{:S(2)}, u32[]{:S(2)}) collective-permute-start(f32[256,128]{1,0:T(8,128)S(1)} %get-tuple-element.52), channel_id=1, source_target_pairs={{8,0},{16,8},{24,16},{32,24},{40,32},{48,40},{56,48},{64,56},{72,6... | collective-permute-start | bytes 393224 | tf_op jit(solution)/shard_map/ppermute | solution.py:350
  127.5 0.6 copy-start.17
  128.9 11.4 %copy-start.7 = (f32[8,128]{1,0:T(8,128)S(1)}, f32[8,128]{1,0:T(8,128)}, u32[]{:S(2)}) copy-start(f32[8,128]{1,0:T(8,128)} %copy-done.6) | copy-start | bytes 12292
  163.5 0.7 copy-start.10
  180.0 5.2 %collective-permute-start.5 = (bf16[32,32,128]{2,1,0:T(8,128)(2,1)S(1)}, bf16[32,32,128]{2,1,0:T(8,128)(2,1)S(1)}, u32[]{:S(2)}, u32[]{:S(2)}) collective-permute-start(bf16[32,32,128]{2,1,0:T(8,128)(2,1)S(1)} %all_to_all.57), channel_id=1, source_target_pairs={{0,8},{8,0},{16,24},{24,16},{32,40},{40,32},{48,56},{56,48},{64,72... | collective-permute-start | bytes 786440 | tf_op jit(solution)/shard_map/ppermute | solution.py:362

commit v6 on v5

--- a/solution.py
+++ b/solution.py
@@ -48,7 +48,7 @@
     return out
 
 
-ANY = pl.BlockSpec(memory_space=pl.ANY)
+HBM = pl.BlockSpec(memory_space=pltpu.HBM)
 SMEM = pl.BlockSpec(memory_space=pltpu.SMEM)
 VMEM = pl.BlockSpec(memory_space=pltpu.VMEM)
 
@@ -107,13 +107,24 @@
         return slice(e * width, (e + 1) * width)
 
     def set_up(
-        here_ref, sub_ref, edge_ref, owner_ref, offset_ref, coupling_hbm, schur_hbm, load_hbm,
-        slotted_ref, turned_ref, asked_ref, codes_ref, table_ref, coupling_ref, schur_ref, load_ref, sems,
+        here_ref, sub_hbm, edge_hbm, owner_hbm, offset_hbm, coupling_hbm, load_hbm, schur_hbm,
+        slotted_ref, turned_ref, asked_ref, codes_ref, table_ref, coupling_ref, load_ref, schur_ref,
+        sub_ref, edge_ref, owner_ref, offset_ref, sems,
     ):
-        moves = [(coupling_hbm, coupling_ref), (load_hbm, load_ref), (schur_hbm, schur_ref)]
+        moves = [
+            (sub_hbm, sub_ref),
+            (edge_hbm, edge_ref),
+            (owner_hbm, owner_ref),
+            (offset_hbm, offset_ref),
+            (coupling_hbm, coupling_ref),
+            (load_hbm, load_ref),
+            (schur_hbm, schur_ref),
+        ]
         moves = [pltpu.make_async_copy(a, b, sems.at[k]) for k, (a, b) in enumerate(moves)]
         for move in moves:
             move.start()
+        for move in moves[:4]:
+            move.wait()
         faces = []
         for e in range(edges):
             side = lax.rem(lax.div(sub_ref[0, e], n_coarse) - here_ref[0, 0] + n_sub, n_sub) == 1
@@ -128,6 +139,7 @@
             table_ref[0, e] = faces[e]
             table_ref[1, e] = place
             table_ref[2, e] = faces[e] * ahead + (1 - faces[e]) * (e - ahead)
+            table_ref[3, e] = edge_ref[0, e]
             ahead = ahead + faces[e]
         same = iota((prims, prims), 0) == iota((prims, prims), 1)
         owner_row = owner_ref[...]
@@ -150,20 +162,20 @@
         codes_ref[...] = jnp.zeros((SIDES, cases), F32)
         for k in range(n_coarse * ROOM // cases):
             codes_ref[k + 1 : k + 2, :] = codes[:, k * cases : (k + 1) * cases]
-        moves[0].wait()
+        moves[4].wait()
         slotted_ref[...] = dot(placed, coupling_ref[...]).astype(BF16)
         turned_ref[...] = lax.dot_general(
             coupling_ref[...], placed, (((0,), (1,)), ((), ())), preferred_element_type=F32
         ).astype(BF16)
-        moves[1].wait()
-        moves[2].wait()
+        moves[5].wait()
+        moves[6].wait()
 
     def first(
-        table_ref, edge_ref, load_ref, before_ref, next_ref, schur_ref, slotted_ref, asked_ref, coupling_ref,
+        table_ref, load_ref, before_ref, next_ref, schur_ref, slotted_ref, asked_ref, coupling_ref,
         residual_ref, local_ref, out_ref, near_ref, old_ref,
     ):
         for e in range(edges):
-            start = pl.multiple_of(edge_ref[0, e] * width, width)
+            start = pl.multiple_of(table_ref[3, e] * width, width)
             ahead = next_ref[pl.ds(start, width), :].astype(F32)
             behind = before_ref[pl.ds(start, width), :].astype(F32)
             facing = jnp.where(table_ref[0, e] == 1, ahead, behind)
@@ -196,21 +208,16 @@
             out_ref[c, :piece] = partial[c * piece : (c + 1) * piece]
             out_ref[c, piece:] = sides
 
-    def coarse_sums(in_ref, rhs_ref, marks_ref, turned_ref, codes_ref):
+    def coarse_sums(in_ref, rhs_ref, sides_ref):
         total = in_ref[0]
         for c in range(1, n_coarse):
             total = total + in_ref[c]
         rhs = total[:piece].astype(BF16)
         for k in range(chips):
             rhs_ref[k] = rhs
-        codes_ref[...] = total[piece:]
-        down = (iota((block, slots), 0) + 1).astype(F32)
-        across = (iota((slots, block), 1) + 1).astype(F32)
-        asked = jnp.concatenate([in_ref[c, piece : piece + 1] for c in range(n_coarse)], axis=0)
-        turned = jnp.transpose(asked)
         for c in range(n_coarse):
-            marks_ref[:, c * slots : (c + 1) * slots] = ones_where(down == asked[c : c + 1])
-            turned_ref[c * slots : (c + 1) * slots] = ones_where(across == turned[:, c : c + 1])
+            sides_ref[c : c + 1] = in_ref[c, piece : piece + 1]
+        sides_ref[n_coarse:] = total[piece:]
 
     def product(mine, theirs):
         both = jnp.where(
@@ -218,10 +225,12 @@
         )
         return dot_t(coarse_inverse, both.reshape(rows, cases))
 
-    def answer(share_ref, turned_ref, out_ref):
-        out = joined(dot(turned_ref[...], in_three(share_ref[...])), 3)
+    def answer(share_ref, sides_ref, out_ref):
+        asked = jnp.transpose(sides_ref[:n_coarse])
+        across = (iota((slots, block), 1) + 1).astype(F32)
+        share = in_three(share_ref[...])
         for c in range(n_coarse):
-            out_ref[c] = out[c * slots : (c + 1) * slots]
+            out_ref[c] = joined(dot(ones_where(across == asked[:, c : c + 1]), share), 3)
 
     def reply(in_ref, given_ref, near_ref, out_ref):
         solved = in_ref[0]
@@ -267,7 +276,7 @@
             out_ref[c, prims : 2 * prims] = new
             out_ref[c, 2 * prims :] = tail
 
-    def spread(in_ref, codes_ref, out_ref, scalars_ref):
+    def spread(in_ref, sides_ref, out_ref, scalars_ref):
         tail = in_ref[0, 2 * prims :]
         for c in range(1, n_coarse):
             tail = tail + in_ref[c, 2 * prims :]
@@ -280,13 +289,15 @@
         for c in range(n_coarse):
             parts += [in_ref[c, :prims] - alpha * in_ref[c, prims : 2 * prims], empty]
         coupled = jnp.concatenate(parts, axis=0).astype(BF16)
-        target = jnp.concatenate([codes_ref[k + 1 : k + 2, :] for k in range(n_coarse * ROOM // cases)], axis=1)
+        target = jnp.concatenate([sides_ref[n_coarse + k + 1 : n_coarse + k + 2, :] for k in range(n_coarse * ROOM // cases)], axis=1)
         total = n_coarse * slots
         marks = ones_where((iota((total, n_coarse * ROOM), 0) + 1).astype(F32) == target)
         out_ref[...] = dot(marks, coupled).astype(BF16)
 
-    def owner_rows(here_ref, in_ref, marks_ref, weights_ref, rhs_ref):
-        weights_ref[...] = dot(marks_ref[...], in_ref[...])
+    def owner_rows(here_ref, in_ref, sides_ref, weights_ref, rhs_ref):
+        down = (iota((block, slots), 0) + 1).astype(F32)
+        marks = jnp.concatenate([ones_where(down == sides_ref[c : c + 1]) for c in range(n_coarse)], axis=1)
+        weights_ref[...] = dot(marks, in_ref[...])
         start = pl.multiple_of(here_ref[0, 1] * piece, piece)
         rhs = weights_ref[pl.ds(start, piece), :].astype(BF16)
         for k in range(chips):
@@ -309,38 +320,40 @@
     start = load[0]
     from_before = lax.ppermute(start, "sub", to_next)
     from_next = lax.ppermute(start, "sub", to_before)
-    slotted, turned, asked, codes, table, coupling_here, schur_here, load_here = run(
+    slotted, turned, asked, codes, table, coupling_here, load_here, schur_here = run(
         set_up,
         [
             ((lines, order), BF16),
             ((order, lines), BF16),
             ((lines, slots), F32),
             scalars_shape,
-            ((3, edges), I32),
+            ((4, edges), I32),
             ((prims, order), BF16),
+            ((order, cases), BF16),
             ((order, order), BF16),
-            ((order, cases), BF16),
         ],
-        here, neighbour_sub, neighbour_edge, owners, primal_offset, coupling[0], schur[0], start,
-        specs=[SMEM] * 3 + [VMEM] * 2 + [ANY] * 3,
-        scratch=[pltpu.SemaphoreType.DMA((3,))],
+        here, neighbour_sub, neighbour_edge, owners, primal_offset, coupling[0], start, schur[0],
+        specs=[SMEM] + [HBM] * 7,
+        scratch=[
+            pltpu.SMEM((1, edges), I32),
+            pltpu.SMEM((1, edges), I32),
+            pltpu.VMEM((1, prims), I32),
+            pltpu.VMEM((1, prims), I32),
+            pltpu.SemaphoreType.DMA((7,)),
+        ],
     )
     residual, local, outgoing, near, old = run(
         first,
         [field, field, ((lines, cases), F32), row, ((prims, cases), F32)],
-        table, neighbour_edge, load_here, from_before, from_next, schur_here, slotted, asked, coupling_here,
+        table, load_here, from_before, from_next, schur_here, slotted, asked, coupling_here,
     )
     given = exchange(outgoing.reshape(n_sub, LINES, cases), "sub").reshape(lines, cases)
     outgoing, norm = run(owner_sums, [((n_coarse, piece + SIDES, cases), F32), row], given, codes)
     incoming = exchange(outgoing, "coarse")
-    rhs, marks, marks_turned, codes = run(
-        coarse_sums,
-        [gathered, ((block, n_coarse * slots), BF16), ((n_coarse * slots, block), BF16), scalars_shape],
-        incoming,
-    )
+    rhs, sides = run(coarse_sums, [gathered, ((2 * SIDES, cases), F32)], incoming)
     mine = exchange(rhs, "sub", same_core)
     theirs = lax.ppermute(mine, "sub", other_core)
-    (outgoing,) = run(answer, [((n_coarse, slots, cases), F32)], product(mine, theirs), marks_turned)
+    (outgoing,) = run(answer, [((n_coarse, slots, cases), F32)], product(mine, theirs), sides)
     incoming = exchange(outgoing, "coarse")
     (outgoing,) = run(reply, [((lines, cases), BF16)], incoming, given, near)
     replies = exchange(outgoing.reshape(n_sub, LINES, cases), "sub").reshape(lines, cases)
@@ -354,13 +367,13 @@
         table, image, from_before, from_next, coupling_here, old, curvature, norm,
     )
     incoming = exchange(outgoing, "coarse")
-    outgoing, scalars = run(spread, [((n_coarse * slots, cases), BF16), scalars_shape], incoming, codes)
+    outgoing, scalars = run(spread, [((n_coarse * slots, cases), BF16), scalars_shape], incoming, sides)
     incoming = exchange(outgoing.reshape(n_sub, n_coarse * CAPACITY, cases), "sub")
     incoming = incoming.transpose(1, 0, 2).reshape(n_coarse * slots, cases)
-    weights, rhs = run(owner_rows, [((block, cases), F32), gathered], here, incoming, marks)
+    weights, rhs = run(owner_rows, [((block, cases), F32), gathered], here, incoming, sides)
     mine = exchange(rhs, "sub", same_core)
     theirs = lax.ppermute(mine, "sub", other_core)
-    remainder, sums = run(second, [field, scalars_shape], residual, image, scalars, schur_here)
+    remainder, sums = run(second, [field, scalars_shape], residual, image, scalars, schur[0])
     far = jnp.sum(weights * product(mine, theirs), axis=0)
     sums = jnp.stack([sums[0] + far, sums[1]])
     for groups in (columns, planes):

time: 210 us -> 205 us (0.976)
  local copies, waits for them, and re-layouts: 7.49 us -> 4.66 us
    unnamed x36 -> x18, local copies, waits for them, and re-layouts: 7.4 us -> 4.58 us
where the time goes in v6:
time: 205 us; the launch traced here: 204 us
  blocking collectives  157 us (77%)
  starting transfers between devices  24.8 us (12%)
  Pallas kernels  7.77 us (4%)
  waiting for transfers between devices  6.56 us (3%)
  local copies, waits for them, and re-layouts  4.66 us (2%)
    all_to_all x10, blocking collectives, exchange(): lax.all_to_all(blocks, axis, 0, 0, tiled=True, axis_index_groups=groups)  157 us
    ppermute x2, starting transfers between devices, body(): theirs = lax.ppermute(mine, 'sub', other_core)  9.66 us
    ppermute x1, starting transfers between devices, body(): from_next = lax.ppermute(start, 'sub', to_before)  8.91 us
    pallas_call x11, Pallas kernels, run(): pl.pallas_call(kernel, out_shape=[jax.ShapeDtypeStruct(shape, dtype) for...  7.77 us
    ppermute x1, waiting for transfers between devices, body(): from_next = lax.ppermute(behind, 'sub', to_before)  4.62 us
    unnamed x18, local copies, waits for them, and re-layouts  4.58 us
  transfers between devices with their start and end apart: 6, of which 3 were waited for; matrix products, arithmetic and copies ran while one was open for 0% of the time, Pallas kernels for 1%

profile of v6, /device:TPU:1, one launch (start us, length us, event | category | flops | bytes accessed | tf_op | source)
XLA Modules:
  0.0 203.8 jit_solution(587048593959444592)
XLA Ops:
  0.0 8.9 %collective-permute-start.1 = (bf16[512,128]{1,0:T(8,128)(2,1)}, bf16[512,128]{1,0:T(8,128)(2,1)S(1)}, u32[]{:S(2)}, u32[]{:S(2)}) collective-permute-start(bf16[512,128]{1,0:T(8,128)(2,1)} %bitcast.45), channel_id=1, source_target_pairs={{8,0},{16,8},{24,16},{32,24},{40,32},{48,40},{56,48},{64,56},{72,6... | collective-permute-start | bytes 393224 | tf_op jit(solution)/shard_map/ppermute | solution.py:322
  8.9 1.9 collective-permute-start
  11.6 1.0 copy-done.1
  12.6 0.9 copy-done.3
  15.5 2.4 %shard_map.82 = (bf16[256,512]{1,0:T(8,128)(2,1)S(1)}, bf16[512,256]{1,0:T(8,128)(2,1)S(1)}, f32[256,128]{1,0:T(8,128)S(1)}, f32[8,128]{1,0:T(8,128)S(1)}, s32[4...) custom-call(s32[1,2]{1,0:T(1,128)S(1)} %add_bitcast_fusion.1.here_ref,, ...), custom_call_target="tpu_custom_call" | custom-call | tf_op jit(solution)/shard_map/pallas_call | solution.py:60
  17.9 1.1 shard_map.83
  19.0 23.1 %all_to_all.50 = f32[64,4,128]{2,1,0:T(4,128)S(1)} all-to-all(f32[64,4,128]{2,1,0:T(4,128)S(1)} %bitcast.44), channel_id=1, replica_groups=mesh['sub'=64,'coarse'=8] {'sub'}, dimensions={0} | all-to-all | bytes 262144 | tf_op jit(solution)/shard_map/all_to_all | solution.py:104
  42.4 15.2 %all_to_all.51.in_ref = f32[8,40,128]{2,1,0:T(8,128)S(1)} all-to-all(f32[8,40,128]{2,1,0:T(8,128)S(1)} %get-tuple-element.42), channel_id=1, replica_groups=mesh['sub'=64,'coarse'=8] {'coarse'}, dimensions={0} | all-to-all | bytes 327680 | tf_op jit(solution)/shard_map/all_to_all | solution.py:104
  57.7 13.6 %all_to_all.52 = bf16[32,32,128]{2,1,0:T(8,128)(2,1)S(1)} all-to-all(bf16[32,32,128]{2,1,0:T(8,128)(2,1)S(1)} %get-tuple-element.43), channel_id=1, replica_groups={{0,16,32,48,64,80,96,112,128,144,160,176,192,208,224,240,256,272,288,30..., dimensions={0} | all-to-all | bytes 524288 | tf_op jit(solution)/shard_map/all_to_all | solution.py:104
  71.2 5.6 %collective-permute-start.2 = (bf16[32,32,128]{2,1,0:T(8,128)(2,1)S(1)}, bf16[32,32,128]{2,1,0:T(8,128)(2,1)S(1)}, u32[]{:S(2)}, u32[]{:S(2)}) collective-permute-start(bf16[32,32,128]{2,1,0:T(8,128)(2,1)S(1)} %all_to_all.52), channel_id=1, source_target_pairs={{0,8},{8,0},{16,24},{24,16},{32,40},{40,32},{48,56},{56,48},{64,72... | collective-permute-start | bytes 786440 | tf_op jit(solution)/shard_map/ppermute | solution.py:355
  76.8 1.1 collective-permute-done.2
  79.2 20.2 %all_to_all.53.in_ref = f32[8,128,128]{2,1,0:T(8,128)S(1)} all-to-all(f32[8,128,128]{2,1,0:T(8,128)S(1)} %shard_map.86), channel_id=1, replica_groups=mesh['sub'=64,'coarse'=8] {'coarse'}, dimensions={0} | all-to-all | bytes 1048576 | tf_op jit(solution)/shard_map/all_to_all | solution.py:104
  99.7 14.2 %all_to_all.54 = bf16[64,4,128]{2,1,0:T(4,128)(2,1)S(1)} all-to-all(bf16[64,4,128]{2,1,0:T(4,128)(2,1)S(1)} %bitcast.42), channel_id=1, replica_groups=mesh['sub'=64,'coarse'=8] {'sub'}, dimensions={0} | all-to-all | bytes 131072 | tf_op jit(solution)/shard_map/all_to_all | solution.py:104
  113.8 0.9 shard_map.88
  114.7 2.4 %collective-permute-start.3 = (f32[256,128]{1,0:T(8,128)S(1)}, f32[256,128]{1,0:T(8,128)S(1)}, u32[]{:S(2)}, u32[]{:S(2)}) collective-permute-start(f32[256,128]{1,0:T(8,128)S(1)} %get-tuple-element.49), channel_id=1, source_target_pairs={{0,8},{8,16},{16,24},{24,32},{32,40},{40,48},{48,56},{56,64},{64,7... | collective-permute-start | bytes 393224 | tf_op jit(solution)/shard_map/ppermute | solution.py:362
  117.1 1.9 collective-permute-start.4
  119.1 4.6 %collective-permute-done.4.next_ref = f32[256,128]{1,0:T(8,128)S(1)} collective-permute-done((f32[256,128]{1,0:T(8,128)S(1)}, f32[256,128]{1,0:T(8,128)S(1)}, u32[]{:S(2)}, u32[]{:S(2)}) %collective-permute-start.4) | collective-permute-done | bytes 131104 | tf_op jit(solution)/shard_map/ppermute | solution.py:363
  124.5 11.4 %all_to_all.55.in_ref = f32[8,56,128]{2,1,0:T(8,128)S(1)} all-to-all(f32[8,56,128]{2,1,0:T(8,128)S(1)} %get-tuple-element.54), channel_id=1, replica_groups=mesh['sub'=64,'coarse'=8] {'coarse'}, dimensions={0} | all-to-all | bytes 458752 | tf_op jit(solution)/shard_map/all_to_all | solution.py:104
  136.2 22.8 %all_to_all.56 = bf16[64,16,128]{2,1,0:T(8,128)(2,1)S(1)} all-to-all(bf16[64,16,128]{2,1,0:T(8,128)(2,1)S(1)} %bitcast.43), channel_id=1, replica_groups=mesh['sub'=64,'coarse'=8] {'sub'}, dimensions={0} | all-to-all | bytes 524288 | tf_op jit(solution)/shard_map/all_to_all | solution.py:104
  159.1 0.9 shard_map.92
  159.9 15.0 %all_to_all.57 = bf16[32,32,128]{2,1,0:T(8,128)(2,1)S(1)} all-to-all(bf16[32,32,128]{2,1,0:T(8,128)(2,1)S(1)} %get-tuple-element.61), channel_id=1, replica_groups={{0,16,32,48,64,80,96,112,128,144,160,176,192,208,224,240,256,272,288,30..., dimensions={0} | all-to-all | bytes 524288 | tf_op jit(solution)/shard_map/all_to_all | solution.py:104
  174.9 4.1 %collective-permute-start.5 = (bf16[32,32,128]{2,1,0:T(8,128)(2,1)S(1)}, bf16[32,32,128]{2,1,0:T(8,128)(2,1)S(1)}, u32[]{:S(2)}, u32[]{:S(2)}) collective-permute-start(bf16[32,32,128]{2,1,0:T(8,128)(2,1)S(1)} %all_to_all.57), channel_id=1, source_target_pairs={{0,8},{8,0},{16,24},{24,16},{32,40},{40,32},{48,56},{56,48},{64,72... | collective-permute-start | bytes 786440 | tf_op jit(solution)/shard_map/ppermute | solution.py:375
  180.9 9.8 %all_to_all.58 = f32[16,2,128]{2,1,0:T(2,128)S(1)} all-to-all(f32[16,2,128]{2,1,0:T(2,128)S(1)} %broadcast_in_dim.9), channel_id=1, replica_groups={{0,1,2,3,4,5,6,7,8,9,10,11,12,13,14,15},{16,17,18,19,20,21,22,23,24,25,..., dimensions={0} | all-to-all | bytes 32768 | tf_op jit(solution)/shard_map/all_to_all | solution.py:104
  190.7 12.3 %all_to_all.59 = f32[32,2,128]{2,1,0:T(2,128)S(1)} all-to-all(f32[32,2,128]{2,1,0:T(2,128)S(1)} %broadcast_in_dim.10), channel_id=1, replica_groups={{0,16,32,48,64,80,96,112,128,144,160,176,192,208,224,240,256,272,288,30..., dimensions={0} | all-to-all | bytes 65536 | tf_op jit(solution)/shard_map/all_to_all | solution.py:104
  (41 shorter events, 8.4 us)
Async XLA Ops:
  0.0 78.1 %copy-start = (bf16[2048,256]{1,0:T(8,128)(2,1)S(1)}, bf16[2048,256]{1,0:T(8,128)(2,1)}, u32[]{:S(2)}) copy-start(bf16[2048,256]{1,0:T(8,128)(2,1)} %param.11) | copy-start | bytes 3145732
  0.0 10.9 %copy-start.4 = (bf16[1,24,512]{2,1,0:T(8,128)(2,1)S(1)}, bf16[1,24,512]{2,1,0:T(8,128)(2,1)}, u32[]{:S(2)}) copy-start(bf16[1,24,512]{2,1,0:T(8,128)(2,1)} %param.10) | copy-start | bytes 73732
  0.0 17.9 %collective-permute-start.1 = (bf16[512,128]{1,0:T(8,128)(2,1)}, bf16[512,128]{1,0:T(8,128)(2,1)S(1)}, u32[]{:S(2)}, u32[]{:S(2)}) collective-permute-start(bf16[512,128]{1,0:T(8,128)(2,1)} %bitcast.45), channel_id=1, source_target_pairs={{8,0},{16,8},{24,16},{32,24},{40,32},{48,40},{56,48},{64,56},{72,6... | collective-permute-start | bytes 393224 | tf_op jit(solution)/shard_map/ppermute | solution.py:322
  8.9 9.0 %collective-permute-start = (bf16[512,128]{1,0:T(8,128)(2,1)}, bf16[512,128]{1,0:T(8,128)(2,1)S(1)}, u32[]{:S(2)}, u32[]{:S(2)}) collective-permute-start(bf16[512,128]{1,0:T(8,128)(2,1)} %bitcast.46), channel_id=1, source_target_pairs={{0,8},{8,16},{16,24},{24,32},{32,40},{40,48},{48,56},{56,64},{64,7... | collective-permute-start | bytes 393224 | tf_op jit(solution)/shard_map/ppermute | solution.py:321
  10.9 0.7 copy-start.5
  11.6 1.0 copy-start.1
  12.6 0.9 copy-start.3
  13.5 0.7 copy-start.6
  14.2 0.7 copy-start.7
  14.8 0.7 copy-start.8
  71.2 6.7 %collective-permute-start.2 = (bf16[32,32,128]{2,1,0:T(8,128)(2,1)S(1)}, bf16[32,32,128]{2,1,0:T(8,128)(2,1)S(1)}, u32[]{:S(2)}, u32[]{:S(2)}) collective-permute-start(bf16[32,32,128]{2,1,0:T(8,128)(2,1)S(1)} %all_to_all.52), channel_id=1, source_target_pairs={{0,8},{8,0},{16,24},{24,16},{32,40},{40,32},{48,56},{56,48},{64,72... | collective-permute-start | bytes 786440 | tf_op jit(solution)/shard_map/ppermute | solution.py:355
  114.7 4.3 %collective-permute-start.3 = (f32[256,128]{1,0:T(8,128)S(1)}, f32[256,128]{1,0:T(8,128)S(1)}, u32[]{:S(2)}, u32[]{:S(2)}) collective-permute-start(f32[256,128]{1,0:T(8,128)S(1)} %get-tuple-element.49), channel_id=1, source_target_pairs={{0,8},{8,16},{16,24},{24,32},{32,40},{40,48},{48,56},{56,64},{64,7... | collective-permute-start | bytes 393224 | tf_op jit(solution)/shard_map/ppermute | solution.py:362
  117.1 6.6 %collective-permute-start.4 = (f32[256,128]{1,0:T(8,128)S(1)}, f32[256,128]{1,0:T(8,128)S(1)}, u32[]{:S(2)}, u32[]{:S(2)}) collective-permute-start(f32[256,128]{1,0:T(8,128)S(1)} %get-tuple-element.50), channel_id=1, source_target_pairs={{8,0},{16,8},{24,16},{32,24},{40,32},{48,40},{56,48},{64,56},{72,6... | collective-permute-start | bytes 393224 | tf_op jit(solution)/shard_map/ppermute | solution.py:363
  159.1 20.0 %copy-start.2 = (bf16[1,512,512]{2,1,0:T(8,128)(2,1)S(1)}, bf16[1,512,512]{2,1,0:T(8,128)(2,1)}, u32[]{:S(2)}) copy-start(bf16[1,512,512]{2,1,0:T(8,128)(2,1)} %param.9) | copy-start | bytes 1572868
  174.9 5.2 %collective-permute-start.5 = (bf16[32,32,128]{2,1,0:T(8,128)(2,1)S(1)}, bf16[32,32,128]{2,1,0:T(8,128)(2,1)S(1)}, u32[]{:S(2)}, u32[]{:S(2)}) collective-permute-start(bf16[32,32,128]{2,1,0:T(8,128)(2,1)S(1)} %all_to_all.57), channel_id=1, source_target_pairs={{0,8},{8,0},{16,24},{24,16},{32,40},{40,32},{48,56},{56,48},{64,72... | collective-permute-start | bytes 786440 | tf_op jit(solution)/shard_map/ppermute | solution.py:375

commit v7 on v6

--- a/solution.py
+++ b/solution.py
@@ -55,7 +55,7 @@
 
 def run(kernel, outs, *args, specs=None, scratch=()):
     def spec(x):
-        return SMEM if jnp.issubdtype(x.dtype, jnp.integer) and x.size <= 32 and x.shape[1] <= 8 else VMEM
+        return SMEM if jnp.issubdtype(x.dtype, jnp.integer) and x.shape[1] <= 8 else VMEM
 
     return pl.pallas_call(
         kernel,
@@ -107,42 +107,32 @@
         return slice(e * width, (e + 1) * width)
 
     def set_up(
-        here_ref, sub_hbm, edge_hbm, owner_hbm, offset_hbm, coupling_hbm, load_hbm, schur_hbm,
-        slotted_ref, turned_ref, asked_ref, codes_ref, table_ref, coupling_ref, load_ref, schur_ref,
-        sub_ref, edge_ref, owner_ref, offset_ref, sems,
+        ints_ref, row_ref, coupling_ref, load_ref, slotted_ref, turned_ref, asked_ref, codes_ref, table_ref, here_ref
     ):
-        moves = [
-            (sub_hbm, sub_ref),
-            (edge_hbm, edge_ref),
-            (owner_hbm, owner_ref),
-            (offset_hbm, offset_ref),
-            (coupling_hbm, coupling_ref),
-            (load_hbm, load_ref),
-            (schur_hbm, schur_ref),
-        ]
-        moves = [pltpu.make_async_copy(a, b, sems.at[k]) for k, (a, b) in enumerate(moves)]
-        for move in moves:
-            move.start()
-        for move in moves[:4]:
-            move.wait()
+        here_ref[...] = load_ref[...]
+        sub_at, coarse_at = ints_ref[0, 0], ints_ref[0, 1]
+        named_sub = [ints_ref[0, 2 + e] for e in range(edges)]
+        named_edge = [ints_ref[0, 2 + edges + e] for e in range(edges)]
+        owner_row = row_ref[:, 2 + 2 * edges : 2 + 2 * edges + prims]
+        offset_row = row_ref[:, 2 + 2 * edges + prims :]
         faces = []
         for e in range(edges):
-            side = lax.rem(lax.div(sub_ref[0, e], n_coarse) - here_ref[0, 0] + n_sub, n_sub) == 1
+            side = lax.rem(lax.div(named_sub[e], n_coarse) - sub_at + n_sub, n_sub) == 1
             faces.append(side.astype(I32))
         ahead = jnp.int32(0)
         for e in range(edges):
             place = jnp.int32(0)
             for other in range(edges):
                 if other != e:
-                    lower = (faces[other] == faces[e]) & (edge_ref[0, other] < edge_ref[0, e])
+                    lower = (faces[other] == faces[e]) & (named_edge[other] < named_edge[e])
                     place = place + lower.astype(I32)
             table_ref[0, e] = faces[e]
             table_ref[1, e] = place
             table_ref[2, e] = faces[e] * ahead + (1 - faces[e]) * (e - ahead)
-            table_ref[3, e] = edge_ref[0, e]
+            table_ref[3, e] = named_edge[e]
+            table_ref[4, e] = coarse_at
             ahead = ahead + faces[e]
         same = iota((prims, prims), 0) == iota((prims, prims), 1)
-        owner_row = owner_ref[...]
         owner_col = jnp.sum(jnp.where(same, owner_row, 0), axis=1, keepdims=True)
         before = (owner_col == owner_row) & (iota((prims, prims), 0) < iota((prims, prims), 1))
         second = jnp.sum(jnp.where(before, 1, 0), axis=0, keepdims=True)
@@ -152,28 +142,22 @@
         asked = jnp.zeros((lines, slots), I32)
         for k in range(CAPACITY):
             named = (line >> 2 == owner_row) & (second == k)
-            offset = jnp.sum(jnp.where(named, offset_ref[...] + 1, 0), axis=1, keepdims=True)
-            asked = jnp.where(lane == k * n_sub + here_ref[0, 0], offset, asked)
+            offset = jnp.sum(jnp.where(named, offset_row + 1, 0), axis=1, keepdims=True)
+            asked = jnp.where(lane == k * n_sub + sub_at, offset, asked)
         asked_ref[...] = jnp.where((iota((lines, slots), 0) & (LINES - 1)) == CAPACITY, asked, 0).astype(F32)
-        target = owner_row * (n_coarse * CAPACITY) + second + CAPACITY * here_ref[0, 1] + 1
-        far_lane = iota((prims, n_coarse * ROOM), 1) == iota((prims, n_coarse * ROOM), 0) + ROOM * here_ref[0, 1]
+        target = owner_row * (n_coarse * CAPACITY) + second + CAPACITY * coarse_at + 1
+        far_lane = iota((prims, n_coarse * ROOM), 1) == iota((prims, n_coarse * ROOM), 0) + ROOM * coarse_at
         target_col = jnp.sum(jnp.where(same, target, 0), axis=1, keepdims=True)
         codes = jnp.sum(jnp.where(far_lane, target_col, 0), axis=0, keepdims=True).astype(F32)
         codes_ref[...] = jnp.zeros((SIDES, cases), F32)
         for k in range(n_coarse * ROOM // cases):
             codes_ref[k + 1 : k + 2, :] = codes[:, k * cases : (k + 1) * cases]
-        moves[4].wait()
         slotted_ref[...] = dot(placed, coupling_ref[...]).astype(BF16)
         turned_ref[...] = lax.dot_general(
             coupling_ref[...], placed, (((0,), (1,)), ((), ())), preferred_element_type=F32
         ).astype(BF16)
-        moves[5].wait()
-        moves[6].wait()
-
-    def first(
-        table_ref, load_ref, before_ref, next_ref, schur_ref, slotted_ref, asked_ref, coupling_ref,
-        residual_ref, local_ref, out_ref, near_ref, old_ref,
-    ):
+
+    def first(table_ref, load_ref, before_ref, next_ref, slotted_ref, asked_ref, residual_ref, out_ref):
         for e in range(edges):
             start = pl.multiple_of(table_ref[3, e] * width, width)
             ahead = next_ref[pl.ds(start, width), :].astype(F32)
@@ -181,15 +165,19 @@
             facing = jnp.where(table_ref[0, e] == 1, ahead, behind)
             residual_ref[edge(e), :] = load_ref[edge(e), :].astype(F32) - facing
         twice = 2.0 * residual_ref[...]
-        jumps, rest = in_two(twice)
-        terms = dot(slotted_ref[...], jumps)
         squares = jnp.sum(twice * twice, axis=0, keepdims=True) * 0.25
         line = iota((lines, cases), 0) & (LINES - 1)
+        terms = dot(slotted_ref[...], twice.astype(BF16))
         out_ref[...] = terms + asked_ref[...] + jnp.where(line == LINES - 1, squares, 0.0)
-        local = dot(schur_ref[...], jumps)
+
+    def springs(residual_ref, schur_ref, after_ref, local_ref, near_ref):
+        twice = 2.0 * residual_ref[...]
+        local = dot(schur_ref[...], twice.astype(BF16))
         local_ref[...] = local
         near_ref[...] = jnp.sum(twice * local, axis=0, keepdims=True)
-        old_ref[...] = joined(dot(coupling_ref[...], jnp.concatenate([jumps, rest], axis=1)), 2)
+
+    def coupled(residual_ref, coupling_ref, after_ref, old_ref):
+        old_ref[...] = joined(dot(coupling_ref[...], jnp.concatenate(in_two(2.0 * residual_ref[...]), axis=1)), 2)
 
     def line_of(shape, dim):
         return (iota(shape, dim) & (LINES - 1)) * n_sub + (iota(shape, dim) >> 2)
@@ -294,11 +282,11 @@
         marks = ones_where((iota((total, n_coarse * ROOM), 0) + 1).astype(F32) == target)
         out_ref[...] = dot(marks, coupled).astype(BF16)
 
-    def owner_rows(here_ref, in_ref, sides_ref, weights_ref, rhs_ref):
+    def owner_rows(table_ref, in_ref, sides_ref, weights_ref, rhs_ref):
         down = (iota((block, slots), 0) + 1).astype(F32)
         marks = jnp.concatenate([ones_where(down == sides_ref[c : c + 1]) for c in range(n_coarse)], axis=1)
         weights_ref[...] = dot(marks, in_ref[...])
-        start = pl.multiple_of(here_ref[0, 1] * piece, piece)
+        start = pl.multiple_of(table_ref[4, 0] * piece, piece)
         rhs = weights_ref[pl.ds(start, piece), :].astype(BF16)
         for k in range(chips):
             rhs_ref[k] = rhs
@@ -316,36 +304,27 @@
     row = ((1, cases), F32)
     gathered = ((chips, piece, cases), BF16)
     scalars_shape = ((SIDES, cases), F32)
-    owners = primal_owner.reshape(1, prims)
+    ints = jnp.concatenate(
+        [here, neighbour_sub, neighbour_edge, primal_owner.reshape(1, prims), primal_offset], axis=1
+    )
     start = load[0]
     from_before = lax.ppermute(start, "sub", to_next)
     from_next = lax.ppermute(start, "sub", to_before)
-    slotted, turned, asked, codes, table, coupling_here, load_here, schur_here = run(
+    slotted, turned, asked, codes, table, start = run(
         set_up,
         [
             ((lines, order), BF16),
             ((order, lines), BF16),
             ((lines, slots), F32),
             scalars_shape,
-            ((4, edges), I32),
-            ((prims, order), BF16),
+            ((5, edges), I32),
             ((order, cases), BF16),
-            ((order, order), BF16),
         ],
-        here, neighbour_sub, neighbour_edge, owners, primal_offset, coupling[0], start, schur[0],
-        specs=[SMEM] + [HBM] * 7,
-        scratch=[
-            pltpu.SMEM((1, edges), I32),
-            pltpu.SMEM((1, edges), I32),
-            pltpu.VMEM((1, prims), I32),
-            pltpu.VMEM((1, prims), I32),
-            pltpu.SemaphoreType.DMA((7,)),
-        ],
-    )
-    residual, local, outgoing, near, old = run(
-        first,
-        [field, field, ((lines, cases), F32), row, ((prims, cases), F32)],
-        table, load_here, from_before, from_next, schur_here, slotted, asked, coupling_here,
+        ints, ints, coupling[0], start,
+        specs=[SMEM, VMEM, VMEM, VMEM],
+    )
+    residual, outgoing = run(
+        first, [field, ((lines, cases), F32)], table, start, from_before, from_next, slotted, asked
     )
     given = exchange(outgoing.reshape(n_sub, LINES, cases), "sub").reshape(lines, cases)
     outgoing, norm = run(owner_sums, [((n_coarse, piece + SIDES, cases), F32), row], given, codes)
@@ -353,6 +332,7 @@
     rhs, sides = run(coarse_sums, [gathered, ((2 * SIDES, cases), F32)], incoming)
     mine = exchange(rhs, "sub", same_core)
     theirs = lax.ppermute(mine, "sub", other_core)
+    local, near = run(springs, [field, row], residual, schur[0], mine, specs=[VMEM, VMEM, HBM])
     (outgoing,) = run(answer, [((n_coarse, slots, cases), F32)], product(mine, theirs), sides)
     incoming = exchange(outgoing, "coarse")
     (outgoing,) = run(reply, [((lines, cases), BF16)], incoming, given, near)
@@ -361,16 +341,17 @@
     image, ahead, behind, curvature = run(back, [field, side, side, row], table, replies, turned, local)
     from_before = lax.ppermute(ahead, "sub", to_next)
     from_next = lax.ppermute(behind, "sub", to_before)
+    (old,) = run(coupled, [((prims, cases), F32)], residual, coupling[0], ahead, specs=[VMEM, VMEM, HBM])
     image, outgoing = run(
         coupled_rows,
         [field, ((n_coarse, 2 * prims + SIDES, cases), F32)],
-        table, image, from_before, from_next, coupling_here, old, curvature, norm,
+        table, image, from_before, from_next, coupling[0], old, curvature, norm,
     )
     incoming = exchange(outgoing, "coarse")
     outgoing, scalars = run(spread, [((n_coarse * slots, cases), BF16), scalars_shape], incoming, sides)
     incoming = exchange(outgoing.reshape(n_sub, n_coarse * CAPACITY, cases), "sub")
     incoming = incoming.transpose(1, 0, 2).reshape(n_coarse * slots, cases)
-    weights, rhs = run(owner_rows, [((block, cases), F32), gathered], here, incoming, sides)
+    weights, rhs = run(owner_rows, [((block, cases), F32), gathered], table, incoming, sides)
     mine = exchange(rhs, "sub", same_core)
     theirs = lax.ppermute(mine, "sub", other_core)
     remainder, sums = run(second, [field, scalars_shape], residual, image, scalars, schur[0])

time: 205 us -> 203 us (level)
  blocking collectives: 157 us -> 137 us
  waiting for transfers between devices: 6.56 us -> 24 us
  starting transfers between devices: 24.8 us -> 28.4 us
  local copies, waits for them, and re-layouts: 4.66 us -> 1.8 us
    all_to_all x10 -> x9, blocking collectives: 157 us -> 137 us  [exchange(): lax.all_to_all(blocks, axis, 0, 0, tiled=True, axis_index_groups=groups)]
    all_to_all x0 -> x1, waiting for transfers between devices: none -> 17.6 us  [exchange(): lax.all_to_all(blocks, axis, 0, 0, tiled=True, axis_index_groups=groups)]
    unnamed x18 -> x8, local copies, waits for them, and re-layouts: 4.58 us -> 0.92 us
    all_to_all x0 -> x1, starting transfers between devices: none -> 3.62 us  [exchange(): lax.all_to_all(blocks, axis, 0, 0, tiled=True, axis_index_groups=groups)]
    ppermute x1, starting transfers between devices: 8.91 us -> 6.2 us  [body(): from_next = lax.ppermute(start, 'sub', to_before)]
    ppermute x1, starting transfers between devices: 1.92 us -> 4.63 us  [body(): from_before = lax.ppermute(start, 'sub', to_next)]
    pallas_call x11 -> x13, Pallas kernels: 7.77 us -> 8.46 us  [run(): pl.pallas_call(kernel, out_shape=[jax.ShapeDtypeStruct(shape, dtype) for...]
  transfers between devices with their start and end apart: 6 -> 7, of which waited for: 3 -> 4; matrix products, arithmetic and copies ran while one was open for 0% -> 0% of each run, Pallas kernels for 1% -> 1%
where the time goes in v7:
time: 203 us; the launch traced here: 202 us
  blocking collectives  137 us (67%)
  starting transfers between devices  28.4 us (14%)
  waiting for transfers between devices  24 us (12%)
  Pallas kernels  8.46 us (4%)
    all_to_all x9, blocking collectives, exchange(): lax.all_to_all(blocks, axis, 0, 0, tiled=True, axis_index_groups=groups)  137 us
    all_to_all x1, waiting for transfers between devices, exchange(): lax.all_to_all(blocks, axis, 0, 0, tiled=True, axis_index_groups=groups)  17.6 us
    ppermute x2, starting transfers between devices, body(): theirs = lax.ppermute(mine, 'sub', other_core)  9.65 us
    pallas_call x13, Pallas kernels, run(): pl.pallas_call(kernel, out_shape=[jax.ShapeDtypeStruct(shape, dtype) for...  8.46 us
    ppermute x1, starting transfers between devices, body(): from_next = lax.ppermute(start, 'sub', to_before)  6.2 us
    ppermute x1, starting transfers between devices, body(): from_before = lax.ppermute(start, 'sub', to_next)  4.63 us
    ppermute x1, waiting for transfers between devices, body(): from_next = lax.ppermute(behind, 'sub', to_before)  4.47 us
  transfers between devices with their start and end apart: 7, of which 4 were waited for; matrix products, arithmetic and copies ran while one was open for 0% of the time, Pallas kernels for 1%

profile of v7, /device:TPU:1, one launch (start us, length us, event | category | flops | bytes accessed | tf_op | source)
XLA Modules:
  0.0 202.2 jit_solution(14689272307719225127)
XLA Ops:
  0.0 4.6 %collective-permute-start = (bf16[512,128]{1,0:T(8,128)(2,1)}, bf16[512,128]{1,0:T(8,128)(2,1)S(1)}, u32[]{:S(2)}, u32[]{:S(2)}) collective-permute-start(bf16[512,128]{1,0:T(8,128)(2,1)} %bitcast.47), channel_id=1, source_target_pairs={{0,8},{8,16},{16,24},{24,32},{32,40},{40,48},{48,56},{56,64},{64,7... | collective-permute-start | bytes 393224 | tf_op jit(solution)/shard_map/ppermute | solution.py:311
  4.6 6.2 %collective-permute-start.1 = (bf16[512,128]{1,0:T(8,128)(2,1)}, bf16[512,128]{1,0:T(8,128)(2,1)S(1)}, u32[]{:S(2)}, u32[]{:S(2)}) collective-permute-start(bf16[512,128]{1,0:T(8,128)(2,1)} %bitcast.48), channel_id=1, source_target_pairs={{8,0},{16,8},{24,16},{32,24},{40,32},{48,40},{56,48},{64,56},{72,6... | collective-permute-start | bytes 393224 | tf_op jit(solution)/shard_map/ppermute | solution.py:312
  11.7 0.9 copy-done.3
  12.6 1.9 shard_map.82
  15.4 23.0 %all_to_all.50 = f32[64,4,128]{2,1,0:T(4,128)S(1)} all-to-all(f32[64,4,128]{2,1,0:T(4,128)S(1)} %bitcast.50), channel_id=1, replica_groups=mesh['sub'=64,'coarse'=8] {'sub'}, dimensions={0} | all-to-all | bytes 262144 | tf_op jit(solution)/shard_map/all_to_all | solution.py:104
  38.8 15.2 %all_to_all.51.in_ref = f32[8,40,128]{2,1,0:T(8,128)S(1)} all-to-all(f32[8,40,128]{2,1,0:T(8,128)S(1)} %get-tuple-element.37), channel_id=1, replica_groups=mesh['sub'=64,'coarse'=8] {'coarse'}, dimensions={0} | all-to-all | bytes 327680 | tf_op jit(solution)/shard_map/all_to_all | solution.py:104
  54.0 13.6 %all_to_all.52.after_ref = bf16[32,32,128]{2,1,0:T(8,128)(2,1)S(1)} all-to-all(bf16[32,32,128]{2,1,0:T(8,128)(2,1)S(1)} %get-tuple-element.38), channel_id=1, replica_groups={{0,16,32,48,64,80,96,112,128,144,160,176,192,208,224,240,256,272,288,30..., dimensions={0} | all-to-all | bytes 524288 | tf_op jit(solution)/shard_map/all_to_all | solution.py:104
  67.6 5.6 %collective-permute-start.2 = (bf16[32,32,128]{2,1,0:T(8,128)(2,1)S(1)}, bf16[32,32,128]{2,1,0:T(8,128)(2,1)S(1)}, u32[]{:S(2)}, u32[]{:S(2)}) collective-permute-start(bf16[32,32,128]{2,1,0:T(8,128)(2,1)S(1)} %all_to_all.52.after_ref), channel_id=1, source_target_pairs={{0,8},{8,0},{16,24},{24,16},{32,40},{40,32},{48,56},{56,48},{64,72... | collective-permute-start | bytes 786440 | tf_op jit(solution)/shard_map/ppermute | solution.py:334
  73.1 1.1 collective-permute-done.2
  75.0 1.4 shard_map.86
  76.3 3.6 %all-to-all-start.3 = ((f32[8,128,128]{2,1,0:T(8,128)}), f32[8,128,128]{2,1,0:T(8,128)S(1)}, u32[]{:S(2)}, u32[]{:S(2)}) async-start(f32[8,128,128]{2,1,0:T(8,128)} %shard_map.86), calls=%async_computation.3 | async-start | bytes 1048576 | tf_op jit(solution)/shard_map/all_to_all | solution.py:104
  80.3 17.6 %all-to-all-done.3.in_ref = f32[8,128,128]{2,1,0:T(8,128)S(1)} async-done(((f32[8,128,128]{2,1,0:T(8,128)}), f32[8,128,128]{2,1,0:T(8,128)S(1)}, u32[]{:S(2)}, u32[]{:S(2)}) %all-to-all-start.3) | async-done | bytes 524320 | tf_op jit(solution)/shard_map/all_to_all | solution.py:104
  98.1 14.0 %all_to_all.53 = bf16[64,4,128]{2,1,0:T(4,128)(2,1)S(1)} all-to-all(bf16[64,4,128]{2,1,0:T(4,128)(2,1)S(1)} %bitcast.42), channel_id=1, replica_groups=mesh['sub'=64,'coarse'=8] {'sub'}, dimensions={0} | all-to-all | bytes 131072 | tf_op jit(solution)/shard_map/all_to_all | solution.py:104
  112.1 0.9 shard_map.89
  113.1 2.4 %collective-permute-start.3 = (f32[256,128]{1,0:T(8,128)S(1)}, f32[256,128]{1,0:T(8,128)S(1)}, u32[]{:S(2)}, u32[]{:S(2)}) collective-permute-start(f32[256,128]{1,0:T(8,128)S(1)} %get-tuple-element.45.after_ref), channel_id=1, source_target_pairs={{0,8},{8,16},{16,24},{24,32},{32,40},{40,48},{48,56},{56,64},{64,7... | collective-permute-start | bytes 393224 | tf_op jit(solution)/shard_map/ppermute | solution.py:342
  115.5 1.9 collective-permute-start.4
  117.6 4.5 %collective-permute-done.4.next_ref = f32[256,128]{1,0:T(8,128)S(1)} collective-permute-done((f32[256,128]{1,0:T(8,128)S(1)}, f32[256,128]{1,0:T(8,128)S(1)}, u32[]{:S(2)}, u32[]{:S(2)}) %collective-permute-start.4) | collective-permute-done | bytes 131104 | tf_op jit(solution)/shard_map/ppermute | solution.py:343
  122.8 11.4 %all_to_all.54.in_ref = f32[8,56,128]{2,1,0:T(8,128)S(1)} all-to-all(f32[8,56,128]{2,1,0:T(8,128)S(1)} %get-tuple-element.49), channel_id=1, replica_groups=mesh['sub'=64,'coarse'=8] {'coarse'}, dimensions={0} | all-to-all | bytes 458752 | tf_op jit(solution)/shard_map/all_to_all | solution.py:104
  134.6 22.8 %all_to_all.55 = bf16[64,16,128]{2,1,0:T(8,128)(2,1)S(1)} all-to-all(bf16[64,16,128]{2,1,0:T(8,128)(2,1)S(1)} %bitcast.43), channel_id=1, replica_groups=mesh['sub'=64,'coarse'=8] {'sub'}, dimensions={0} | all-to-all | bytes 524288 | tf_op jit(solution)/shard_map/all_to_all | solution.py:104
  157.4 0.9 shard_map.94
  158.4 15.0 %all_to_all.56 = bf16[32,32,128]{2,1,0:T(8,128)(2,1)S(1)} all-to-all(bf16[32,32,128]{2,1,0:T(8,128)(2,1)S(1)} %get-tuple-element.55), channel_id=1, replica_groups={{0,16,32,48,64,80,96,112,128,144,160,176,192,208,224,240,256,272,288,30..., dimensions={0} | all-to-all | bytes 524288 | tf_op jit(solution)/shard_map/all_to_all | solution.py:104
  173.3 4.1 %collective-permute-start.5 = (bf16[32,32,128]{2,1,0:T(8,128)(2,1)S(1)}, bf16[32,32,128]{2,1,0:T(8,128)(2,1)S(1)}, u32[]{:S(2)}, u32[]{:S(2)}) collective-permute-start(bf16[32,32,128]{2,1,0:T(8,128)(2,1)S(1)} %all_to_all.56), channel_id=1, source_target_pairs={{0,8},{8,0},{16,24},{24,16},{32,40},{40,32},{48,56},{56,48},{64,72... | collective-permute-start | bytes 786440 | tf_op jit(solution)/shard_map/ppermute | solution.py:356
  179.3 9.8 %all_to_all.57 = f32[16,2,128]{2,1,0:T(2,128)S(1)} all-to-all(f32[16,2,128]{2,1,0:T(2,128)S(1)} %broadcast_in_dim.9), channel_id=1, replica_groups={{0,1,2,3,4,5,6,7,8,9,10,11,12,13,14,15},{16,17,18,19,20,21,22,23,24,25,..., dimensions={0} | all-to-all | bytes 32768 | tf_op jit(solution)/shard_map/all_to_all | solution.py:104
  189.1 12.3 %all_to_all.58 = f32[32,2,128]{2,1,0:T(2,128)S(1)} all-to-all(f32[32,2,128]{2,1,0:T(2,128)S(1)} %broadcast_in_dim.10), channel_id=1, replica_groups={{0,16,32,48,64,80,96,112,128,144,160,176,192,208,224,240,256,272,288,30..., dimensions={0} | all-to-all | bytes 65536 | tf_op jit(solution)/shard_map/all_to_all | solution.py:104
  (35 shorter events, 7.4 us)
Async XLA Ops:
  0.0 74.4 %copy-start = (bf16[2048,256]{1,0:T(8,128)(2,1)S(1)}, bf16[2048,256]{1,0:T(8,128)(2,1)}, u32[]{:S(2)}) copy-start(bf16[2048,256]{1,0:T(8,128)(2,1)} %param.11) | copy-start | bytes 3145732
  0.0 11.7 %copy-start.2 = (bf16[1,24,512]{2,1,0:T(8,128)(2,1)S(1)}, bf16[1,24,512]{2,1,0:T(8,128)(2,1)}, u32[]{:S(2)}) copy-start(bf16[1,24,512]{2,1,0:T(8,128)(2,1)} %param.10) | copy-start | bytes 73732
  0.0 14.5 %collective-permute-start = (bf16[512,128]{1,0:T(8,128)(2,1)}, bf16[512,128]{1,0:T(8,128)(2,1)S(1)}, u32[]{:S(2)}, u32[]{:S(2)}) collective-permute-start(bf16[512,128]{1,0:T(8,128)(2,1)} %bitcast.47), channel_id=1, source_target_pairs={{0,8},{8,16},{16,24},{24,32},{32,40},{40,48},{48,56},{56,64},{64,7... | collective-permute-start | bytes 393224 | tf_op jit(solution)/shard_map/ppermute | solution.py:311
  4.6 9.9 %collective-permute-start.1 = (bf16[512,128]{1,0:T(8,128)(2,1)}, bf16[512,128]{1,0:T(8,128)(2,1)S(1)}, u32[]{:S(2)}, u32[]{:S(2)}) collective-permute-start(bf16[512,128]{1,0:T(8,128)(2,1)} %bitcast.48), channel_id=1, source_target_pairs={{8,0},{16,8},{24,16},{32,24},{40,32},{48,40},{56,48},{64,56},{72,6... | collective-permute-start | bytes 393224 | tf_op jit(solution)/shard_map/ppermute | solution.py:312
  11.7 0.9 copy-start.3
  67.6 6.7 %collective-permute-start.2 = (bf16[32,32,128]{2,1,0:T(8,128)(2,1)S(1)}, bf16[32,32,128]{2,1,0:T(8,128)(2,1)S(1)}, u32[]{:S(2)}, u32[]{:S(2)}) collective-permute-start(bf16[32,32,128]{2,1,0:T(8,128)(2,1)S(1)} %all_to_all.52.after_ref), channel_id=1, source_target_pairs={{0,8},{8,0},{16,24},{24,16},{32,40},{40,32},{48,56},{56,48},{64,72... | collective-permute-start | bytes 786440 | tf_op jit(solution)/shard_map/ppermute | solution.py:334
  76.3 3.6 %copy-start.1 = (bf16[1,512,512]{2,1,0:T(8,128)(2,1)S(1)}, bf16[1,512,512]{2,1,0:T(8,128)(2,1)}, u32[]{:S(2)}) copy-start(bf16[1,512,512]{2,1,0:T(8,128)(2,1)} %param.9) | copy-start | bytes 1572868
  76.3 21.6 %all-to-all-start.3 = ((f32[8,128,128]{2,1,0:T(8,128)}), f32[8,128,128]{2,1,0:T(8,128)S(1)}, u32[]{:S(2)}, u32[]{:S(2)}) async-start(f32[8,128,128]{2,1,0:T(8,128)} %shard_map.86), calls=%async_computation.3 | async-start | bytes 1048576 | tf_op jit(solution)/shard_map/all_to_all | solution.py:104
  113.1 4.5 %collective-permute-start.3 = (f32[256,128]{1,0:T(8,128)S(1)}, f32[256,128]{1,0:T(8,128)S(1)}, u32[]{:S(2)}, u32[]{:S(2)}) collective-permute-start(f32[256,128]{1,0:T(8,128)S(1)} %get-tuple-element.45.after_ref), channel_id=1, source_target_pairs={{0,8},{8,16},{16,24},{24,32},{32,40},{40,48},{48,56},{56,64},{64,7... | collective-permute-start | bytes 393224 | tf_op jit(solution)/shard_map/ppermute | solution.py:342
  115.5 6.6 %collective-permute-start.4 = (f32[256,128]{1,0:T(8,128)S(1)}, f32[256,128]{1,0:T(8,128)S(1)}, u32[]{:S(2)}, u32[]{:S(2)}) collective-permute-start(f32[256,128]{1,0:T(8,128)S(1)} %get-tuple-element.46), channel_id=1, source_target_pairs={{8,0},{16,8},{24,16},{32,24},{40,32},{48,40},{56,48},{64,56},{72,6... | collective-permute-start | bytes 393224 | tf_op jit(solution)/shard_map/ppermute | solution.py:343
  173.3 5.2 %collective-permute-start.5 = (bf16[32,32,128]{2,1,0:T(8,128)(2,1)S(1)}, bf16[32,32,128]{2,1,0:T(8,128)(2,1)S(1)}, u32[]{:S(2)}, u32[]{:S(2)}) collective-permute-start(bf16[32,32,128]{2,1,0:T(8,128)(2,1)S(1)} %all_to_all.56), channel_id=1, source_target_pairs={{0,8},{8,0},{16,24},{24,16},{32,40},{40,32},{48,56},{56,48},{64,72... | collective-permute-start | bytes 786440 | tf_op jit(solution)/shard_map/ppermute | solution.py:356

commit v8 on v7

--- a/solution.py
+++ b/solution.py
@@ -10,6 +10,8 @@
 LINES = 4
 ROOM = 32
 SIDES = 8
+REPLIES = 8
+NOBODY = -1000.0
 
 
 def dot(a, b):
@@ -107,7 +109,8 @@
         return slice(e * width, (e + 1) * width)
 
     def set_up(
-        ints_ref, row_ref, coupling_ref, load_ref, slotted_ref, turned_ref, asked_ref, codes_ref, table_ref, here_ref
+        ints_ref, row_ref, coupling_ref, load_ref,
+        slotted_ref, turned_ref, asked_ref, codes_ref, table_ref, here_ref, ahead_ref, behind_ref,
     ):
         here_ref[...] = load_ref[...]
         sub_at, coarse_at = ints_ref[0, 0], ints_ref[0, 1]
@@ -153,9 +156,24 @@
         for k in range(n_coarse * ROOM // cases):
             codes_ref[k + 1 : k + 2, :] = codes[:, k * cases : (k + 1) * cases]
         slotted_ref[...] = dot(placed, coupling_ref[...]).astype(BF16)
-        turned_ref[...] = lax.dot_general(
-            coupling_ref[...], placed, (((0,), (1,)), ((), ())), preferred_element_type=F32
-        ).astype(BF16)
+        wide_eye = iota((prims, cases), 0) == iota((prims, cases), 1)
+        turned_ref[...] = dot_t(coupling_ref[...], ones_where(wide_eye)).astype(BF16)
+        line_col = jnp.sum(jnp.where(same, owner_row * REPLIES + second, 0), axis=1, keepdims=True)
+        line_row = jnp.sum(jnp.where(wide_eye, line_col, 0), axis=0, keepdims=True).astype(F32)
+        line_row = jnp.where(iota((1, cases), 1) < prims, line_row, NOBODY)
+        lane = iota((1, half * width), 1)
+        for side, ref in ((1, ahead_ref), (0, behind_ref)):
+            target = jnp.zeros((1, half * width), I32)
+            for place in range(half):
+                at = jnp.int32(0)
+                for e in range(edges):
+                    at = at + e * ((faces[e] == side) & (table_ref[2, e] == place)).astype(I32)
+                target = jnp.where(lane // width == place, at * width + lane % width, target)
+            chosen = ones_where(iota((order, half * width), 0) == target)
+            columns_there = dot(coupling_ref[...], chosen)
+            for k in range(half * width // cases):
+                ref[k * prims : (k + 1) * prims] = columns_there[:, k * cases : (k + 1) * cases]
+            ref[half * width // cases * prims :] = jnp.broadcast_to(line_row, (SIDES, cases))
 
     def first(table_ref, load_ref, before_ref, next_ref, slotted_ref, asked_ref, residual_ref, out_ref):
         for e in range(edges):
@@ -170,14 +188,24 @@
         terms = dot(slotted_ref[...], twice.astype(BF16))
         out_ref[...] = terms + asked_ref[...] + jnp.where(line == LINES - 1, squares, 0.0)
 
-    def springs(residual_ref, schur_ref, after_ref, local_ref, near_ref):
+    def springs(
+        table_ref, residual_ref, schur_ref, ahead_in, behind_in, after_ref, local_ref, near_ref, ahead_ref, behind_ref
+    ):
         twice = 2.0 * residual_ref[...]
-        local = dot(schur_ref[...], twice.astype(BF16))
-        local_ref[...] = local
-        near_ref[...] = jnp.sum(twice * local, axis=0, keepdims=True)
-
-    def coupled(residual_ref, coupling_ref, after_ref, old_ref):
-        old_ref[...] = joined(dot(coupling_ref[...], jnp.concatenate(in_two(2.0 * residual_ref[...]), axis=1)), 2)
+        local_ref[...] = dot(schur_ref[...], twice.astype(BF16))
+        near_ref[...] = jnp.sum(twice * local_ref[...], axis=0, keepdims=True)
+        ahead_ref[half * width :] = ahead_in[...]
+        behind_ref[half * width :] = behind_in[...]
+        for e in range(edges):
+            place = pl.ds(pl.multiple_of(table_ref[2, e] * width, width), width)
+
+            @pl.when(table_ref[0, e] == 1)
+            def _():
+                ahead_ref[place, :] = local_ref[edge(e), :]
+
+            @pl.when(table_ref[0, e] == 0)
+            def _():
+                behind_ref[place, :] = local_ref[edge(e), :]
 
     def line_of(shape, dim):
         return (iota(shape, dim) & (LINES - 1)) * n_sub + (iota(shape, dim) >> 2)
@@ -213,7 +241,7 @@
         )
         return dot_t(coarse_inverse, both.reshape(rows, cases))
 
-    def answer(share_ref, sides_ref, out_ref):
+    def answer(share_ref, sides_ref, after_ref, out_ref):
         asked = jnp.transpose(sides_ref[:n_coarse])
         across = (iota((slots, block), 1) + 1).astype(F32)
         share = in_three(share_ref[...])
@@ -224,43 +252,55 @@
         solved = in_ref[0]
         for c in range(1, n_coarse):
             solved = solved + in_ref[c]
-        expand = ones_where(line_of((lines, slots), 0) == iota((lines, slots), 1))
-        wide = dot(expand, solved.astype(BF16))
+        total = n_sub * REPLIES
+        line = iota((total, slots), 0) & (REPLIES - 1)
+        shift = jnp.where(line >> 1 == 1, n_sub - 1, line >> 2)
+        source = ((iota((total, slots), 0) // REPLIES + shift) & (n_sub - 1)) + (line & 1) * n_sub
+        expand = ones_where((source == iota((total, slots), 1)) & (line < 3 * CAPACITY))
+        solved = solved.astype(BF16)
+        wide = dot(expand, solved)
+        given = given_ref[...]
+        own = ones_where(line_of((lines, slots), 0) == iota((lines, slots), 1))
         line = iota((lines, cases), 0) & (LINES - 1)
-        far = near_ref[...] + jnp.sum(jnp.where(line < CAPACITY, given_ref[...] * wide, 0.0), axis=0, keepdims=True)
-        high, low = in_two(far)
-        wide = jnp.where(line == CAPACITY, high.astype(F32), wide)
-        out_ref[...] = jnp.where(line == CAPACITY + 1, low.astype(F32), wide).astype(BF16)
-
-    def back(table_ref, in_ref, turned_ref, local_ref, image_ref, ahead_ref, behind_ref, curvature_ref):
+        terms = jnp.where(line < CAPACITY, given * dot(own, solved), 0.0)
+        high, low = in_two(near_ref[...] + jnp.sum(terms, axis=0, keepdims=True))
+        line = iota((total, cases), 0) & (REPLIES - 1)
+        wide = jnp.where(line == 3 * CAPACITY, high.astype(F32), wide)
+        out_ref[...] = jnp.where(line == 3 * CAPACITY + 1, low.astype(F32), wide).astype(BF16)
+
+    def join(
+        table_ref, in_ref, local_ref, before_ref, next_ref, turned_ref, own_ref, coupling_ref, residual_ref, norm_ref,
+        jump_ref, out_ref, behind_ref, ahead_ref,
+    ):
         replies = in_ref[...]
-        image_ref[...] = local_ref[...] + dot(turned_ref[...], replies)
-        line = iota((lines, cases), 0) & (LINES - 1)
-        curvature_ref[...] = jnp.sum(jnp.where(line >= CAPACITY, replies.astype(F32), 0.0), axis=0, keepdims=True)
-        for e in range(edges):
-            place = pl.ds(pl.multiple_of(table_ref[2, e] * width, width), width)
-
-            @pl.when(table_ref[0, e] == 1)
-            def _():
-                ahead_ref[place, :] = image_ref[edge(e), :]
-
-            @pl.when(table_ref[0, e] == 0)
-            def _():
-                behind_ref[place, :] = image_ref[edge(e), :]
-
-    def coupled_rows(
-        table_ref, image_ref, before_ref, next_ref, coupling_ref, old_ref, curvature_ref, norm_ref, jump_ref, out_ref
-    ):
+        total = n_sub * REPLIES
+        line = iota((total, cases), 0) & (REPLIES - 1)
+        curvature = jnp.sum(jnp.where(line >= 3 * CAPACITY, replies.astype(F32), 0.0), axis=0, keepdims=True)
+        packed = half * width
+        codes_at = packed + packed // cases * prims
+        codes = [own_ref[packed // cases * prims :], before_ref[codes_at:], next_ref[codes_at:]]
+        values = []
+        for k, code in enumerate(codes):
+            column = jnp.transpose(code)[:, :1] + float(k * CAPACITY)
+            chosen = ones_where(iota((cases, total), 1).astype(F32) == column)
+            values.append(dot(chosen, replies).astype(BF16))
+        wide_eye = ones_where(iota((prims, cases), 0) == iota((prims, cases), 1))
+        for side_ref, value, ref in ((before_ref, values[1], behind_ref), (next_ref, values[2], ahead_ref)):
+            there = [side_ref[packed + k * prims : packed + (k + 1) * prims] for k in range(packed // cases)]
+            turned = dot_t(jnp.concatenate(there, axis=1).astype(BF16), wide_eye).astype(BF16)
+            ref[...] = side_ref[:packed] + dot(turned, value)
+        image = local_ref[...] + dot(turned_ref[...], values[0])
         for e in range(edges):
             place = pl.ds(pl.multiple_of(table_ref[1, e] * width, width), width)
-            facing = jnp.where(table_ref[0, e] == 1, next_ref[place, :], before_ref[place, :])
-            jump_ref[edge(e), :] = image_ref[edge(e), :] - facing
-        pair = jnp.concatenate(in_two(2.0 * jump_ref[...]), axis=1)
-        new = joined(dot(coupling_ref[...], pair), 2)
+            facing = jnp.where(table_ref[0, e] == 1, ahead_ref[place, :], behind_ref[place, :])
+            jump_ref[edge(e), :] = image[edge(e), :] - facing
+        pair = jnp.concatenate(in_two(2.0 * residual_ref[...]) + in_two(2.0 * jump_ref[...]), axis=1)
+        rows_there = dot(coupling_ref[...], pair)
+        old, new = joined(rows_there[:, : 2 * cases], 2), joined(rows_there[:, 2 * cases :], 2)
         line = iota((SIDES, cases), 0)
-        tail = jnp.where(line == 0, curvature_ref[...], jnp.where(line == 1, norm_ref[...], 0.0))
+        tail = jnp.where(line == 0, curvature, jnp.where(line == 1, norm_ref[...], 0.0))
         for c in range(n_coarse):
-            out_ref[c, :prims] = old_ref[...]
+            out_ref[c, :prims] = old
             out_ref[c, prims : 2 * prims] = new
             out_ref[c, 2 * prims :] = tail
 
@@ -310,15 +350,18 @@
     start = load[0]
     from_before = lax.ppermute(start, "sub", to_next)
     from_next = lax.ppermute(start, "sub", to_before)
-    slotted, turned, asked, codes, table, start = run(
+    packed = ((half * width // cases * prims + SIDES, cases), F32)
+    slotted, turned, asked, codes, table, start, ahead, behind = run(
         set_up,
         [
             ((lines, order), BF16),
-            ((order, lines), BF16),
+            ((order, cases), BF16),
             ((lines, slots), F32),
             scalars_shape,
             ((5, edges), I32),
             ((order, cases), BF16),
+            packed,
+            packed,
         ],
         ints, ints, coupling[0], start,
         specs=[SMEM, VMEM, VMEM, VMEM],
@@ -332,20 +375,29 @@
     rhs, sides = run(coarse_sums, [gathered, ((2 * SIDES, cases), F32)], incoming)
     mine = exchange(rhs, "sub", same_core)
     theirs = lax.ppermute(mine, "sub", other_core)
-    local, near = run(springs, [field, row], residual, schur[0], mine, specs=[VMEM, VMEM, HBM])
-    (outgoing,) = run(answer, [((n_coarse, slots, cases), F32)], product(mine, theirs), sides)
+    side = ((half * width + packed[0][0], cases), F32)
+    local, near, to_ahead, to_behind = run(
+        springs,
+        [field, row, side, side],
+        table, residual, schur[0], ahead, behind, mine,
+        specs=[SMEM, VMEM, VMEM, VMEM, VMEM, HBM],
+    )
+    from_before = lax.ppermute(to_ahead, "sub", to_next)
+    from_next = lax.ppermute(to_behind, "sub", to_before)
+    (outgoing,) = run(
+        answer,
+        [((n_coarse, slots, cases), F32)],
+        product(mine, theirs), sides, near,
+        specs=[VMEM, VMEM, HBM],
+    )
     incoming = exchange(outgoing, "coarse")
-    (outgoing,) = run(reply, [((lines, cases), BF16)], incoming, given, near)
-    replies = exchange(outgoing.reshape(n_sub, LINES, cases), "sub").reshape(lines, cases)
-    side = ((half * width, cases), F32)
-    image, ahead, behind, curvature = run(back, [field, side, side, row], table, replies, turned, local)
-    from_before = lax.ppermute(ahead, "sub", to_next)
-    from_next = lax.ppermute(behind, "sub", to_before)
-    (old,) = run(coupled, [((prims, cases), F32)], residual, coupling[0], ahead, specs=[VMEM, VMEM, HBM])
+    (outgoing,) = run(reply, [((n_sub * REPLIES, cases), BF16)], incoming, given, near)
+    replies = exchange(outgoing.reshape(n_sub, REPLIES, cases), "sub").reshape(n_sub * REPLIES, cases)
     image, outgoing = run(
-        coupled_rows,
+        join,
         [field, ((n_coarse, 2 * prims + SIDES, cases), F32)],
-        table, image, from_before, from_next, coupling[0], old, curvature, norm,
+        table, replies, local, from_before, from_next, turned, ahead, coupling[0], residual, norm,
+        scratch=[pltpu.VMEM((half * width, cases), F32)] * 2,
     )
     incoming = exchange(outgoing, "coarse")
     outgoing, scalars = run(spread, [((n_coarse * slots, cases), BF16), scalars_shape], incoming, sides)

time: 203 us -> 197 us (0.970)
  waiting for transfers between devices: 24 us -> 9.37 us
  blocking collectives: 137 us -> 142 us
  starting transfers between devices: 28.4 us -> 31 us
    all_to_all x1, waiting for transfers between devices: 17.6 us -> 0.77 us  [exchange(): lax.all_to_all(blocks, axis, 0, 0, tiled=True, axis_index_groups=groups)]
    all_to_all x9, blocking collectives: 137 us -> 142 us  [exchange(): lax.all_to_all(blocks, axis, 0, 0, tiled=True, axis_index_groups=groups)]
    ppermute x1, starting transfers between devices: 6.2 us -> 8.91 us  [body(): from_next = lax.ppermute(start, 'sub', to_before)]
    ppermute x1, starting transfers between devices: 4.63 us -> 1.92 us  [body(): from_before = lax.ppermute(start, 'sub', to_next)]
    ppermute x1, waiting for transfers between devices: 0.01 us -> 2.6 us  [body(): from_before = lax.ppermute(start, 'sub', to_next)]
    pallas_call x13 -> x11, Pallas kernels: 8.46 us -> 8.84 us  [run(): pl.pallas_call(kernel, out_shape=[jax.ShapeDtypeStruct(shape, dtype) for...]
  transfers between devices with their start and end apart: 7 -> 7, of which waited for: 4 -> 6; matrix products, arithmetic and copies ran while one was open for 0% -> 0% of each run, Pallas kernels for 1% -> 2%
where the time goes in v8:
time: 197 us; the launch traced here: 196 us
  blocking collectives  142 us (72%)
  starting transfers between devices  31 us (16%)
  waiting for transfers between devices  9.37 us (5%)
  Pallas kernels  8.84 us (4%)
    all_to_all x9, blocking collectives, exchange(): lax.all_to_all(blocks, axis, 0, 0, tiled=True, axis_index_groups=groups)  142 us
    ppermute x2, starting transfers between devices, body(): theirs = lax.ppermute(mine, 'sub', other_core)  9.58 us
    ppermute x1, starting transfers between devices, body(): from_next = lax.ppermute(start, 'sub', to_before)  8.91 us
    pallas_call x11, Pallas kernels, run(): pl.pallas_call(kernel, out_shape=[jax.ShapeDtypeStruct(shape, dtype) for...  8.84 us
    all_to_all x1, starting transfers between devices, exchange(): lax.all_to_all(blocks, axis, 0, 0, tiled=True, axis_index_groups=groups)  5.11 us
    ppermute x1, waiting for transfers between devices, body(): from_next = lax.ppermute(to_behind, 'sub', to_before)  4.3 us
  transfers between devices with their start and end apart: 7, of which 6 were waited for; matrix products, arithmetic and copies ran while one was open for 0% of the time, Pallas kernels for 2%

profile of v8, /device:TPU:1, one launch (start us, length us, event | category | flops | bytes accessed | tf_op | source)
XLA Modules:
  0.0 195.9 jit_solution(3397023125424523954)
XLA Ops:
  0.0 8.9 %collective-permute-start.1 = (bf16[512,128]{1,0:T(8,128)(2,1)}, bf16[512,128]{1,0:T(8,128)(2,1)S(1)}, u32[]{:S(2)}, u32[]{:S(2)}) collective-permute-start(bf16[512,128]{1,0:T(8,128)(2,1)} %bitcast.43), channel_id=1, source_target_pairs={{8,0},{16,8},{24,16},{32,24},{40,32},{48,40},{56,48},{64,56},{72,6... | collective-permute-start | bytes 393224 | tf_op jit(solution)/shard_map/ppermute | solution.py:352
  8.9 1.9 collective-permute-start
  11.7 0.9 copy-done.2
  12.6 1.9 shard_map.82
  14.6 2.6 %collective-permute-done.before_ref = bf16[512,128]{1,0:T(8,128)(2,1)S(1)} collective-permute-done((bf16[512,128]{1,0:T(8,128)(2,1)}, bf16[512,128]{1,0:T(8,128)(2,1)S(1)}, u32[]{:S(2)}, u32[]{:S(2)}) %collective-permute-start) | collective-permute-done | bytes 131104 | tf_op jit(solution)/shard_map/ppermute | solution.py:351
  18.1 21.4 %all_to_all.50 = f32[64,4,128]{2,1,0:T(4,128)S(1)} all-to-all(f32[64,4,128]{2,1,0:T(4,128)S(1)} %bitcast.46), channel_id=1, replica_groups=mesh['sub'=64,'coarse'=8] {'sub'}, dimensions={0} | all-to-all | bytes 262144 | tf_op jit(solution)/shard_map/all_to_all | solution.py:106
  39.9 15.3 %all_to_all.51.in_ref = f32[8,40,128]{2,1,0:T(8,128)S(1)} all-to-all(f32[8,40,128]{2,1,0:T(8,128)S(1)} %get-tuple-element.37), channel_id=1, replica_groups=mesh['sub'=64,'coarse'=8] {'coarse'}, dimensions={0} | all-to-all | bytes 327680 | tf_op jit(solution)/shard_map/all_to_all | solution.py:106
  55.2 13.6 %all_to_all.52.after_ref = bf16[32,32,128]{2,1,0:T(8,128)(2,1)S(1)} all-to-all(bf16[32,32,128]{2,1,0:T(8,128)(2,1)S(1)} %get-tuple-element.38), channel_id=1, replica_groups={{0,16,32,48,64,80,96,112,128,144,160,176,192,208,224,240,256,272,288,30..., dimensions={0} | all-to-all | bytes 524288 | tf_op jit(solution)/shard_map/all_to_all | solution.py:106
  68.8 5.5 %collective-permute-start.2 = (bf16[32,32,128]{2,1,0:T(8,128)(2,1)S(1)}, bf16[32,32,128]{2,1,0:T(8,128)(2,1)S(1)}, u32[]{:S(2)}, u32[]{:S(2)}) collective-permute-start(bf16[32,32,128]{2,1,0:T(8,128)(2,1)S(1)} %all_to_all.52.after_ref), channel_id=1, source_target_pairs={{0,8},{8,0},{16,24},{24,16},{32,40},{40,32},{48,56},{56,48},{64,72... | collective-permute-start | bytes 786440 | tf_op jit(solution)/shard_map/ppermute | solution.py:377
  74.3 1.0 shard_map.86
  76.7 19.8 %all_to_all.53.in_ref = f32[8,128,128]{2,1,0:T(8,128)S(1)} all-to-all(f32[8,128,128]{2,1,0:T(8,128)S(1)} %shard_map.87), channel_id=1, replica_groups=mesh['sub'=64,'coarse'=8] {'coarse'}, dimensions={0} | all-to-all | bytes 1048576 | tf_op jit(solution)/shard_map/all_to_all | solution.py:106
  96.5 1.0 shard_map.88
  97.5 5.1 %all-to-all-start.4 = ((bf16[64,8,128]{2,1,0:T(8,128)(2,1)}), bf16[64,8,128]{2,1,0:T(8,128)(2,1)S(1)}, u32[]{:S(2)}, u32[]{:S(2)}) async-start(bf16[64,8,128]{2,1,0:T(8,128)(2,1)} %bitcast.11), calls=%async_computation.4 | async-start | bytes 262144 | tf_op jit(solution)/shard_map/all_to_all | solution.py:106
  102.6 3.5 %collective-permute-start.3 = (f32[312,128]{1,0:T(8,128)S(1)}, f32[312,128]{1,0:T(8,128)S(1)}, u32[]{:S(2)}, u32[]{:S(2)}) collective-permute-start(f32[312,128]{1,0:T(8,128)S(1)} %get-tuple-element.45), channel_id=1, source_target_pairs={{0,8},{8,16},{16,24},{24,32},{32,40},{40,48},{48,56},{56,64},{64,7... | collective-permute-start | bytes 479240 | tf_op jit(solution)/shard_map/ppermute | solution.py:385
  106.2 1.9 collective-permute-start.4
  108.9 4.3 %collective-permute-done.4.next_ref = f32[312,128]{1,0:T(8,128)S(1)} collective-permute-done((f32[312,128]{1,0:T(8,128)S(1)}, f32[312,128]{1,0:T(8,128)S(1)}, u32[]{:S(2)}, u32[]{:S(2)}) %collective-permute-start.4) | collective-permute-done | bytes 159776 | tf_op jit(solution)/shard_map/ppermute | solution.py:386
  114.0 1.5 shard_map.89
  115.5 12.2 %all_to_all.54.in_ref = f32[8,56,128]{2,1,0:T(8,128)S(1)} all-to-all(f32[8,56,128]{2,1,0:T(8,128)S(1)} %get-tuple-element.49), channel_id=1, replica_groups=mesh['sub'=64,'coarse'=8] {'coarse'}, dimensions={0} | all-to-all | bytes 458752 | tf_op jit(solution)/shard_map/all_to_all | solution.py:106
  128.0 23.0 %all_to_all.55 = bf16[64,16,128]{2,1,0:T(8,128)(2,1)S(1)} all-to-all(bf16[64,16,128]{2,1,0:T(8,128)(2,1)S(1)} %bitcast.42), channel_id=1, replica_groups=mesh['sub'=64,'coarse'=8] {'sub'}, dimensions={0} | all-to-all | bytes 524288 | tf_op jit(solution)/shard_map/all_to_all | solution.py:106
  151.1 0.9 shard_map.92
  152.0 15.0 %all_to_all.56 = bf16[32,32,128]{2,1,0:T(8,128)(2,1)S(1)} all-to-all(bf16[32,32,128]{2,1,0:T(8,128)(2,1)S(1)} %get-tuple-element.55), channel_id=1, replica_groups={{0,16,32,48,64,80,96,112,128,144,160,176,192,208,224,240,256,272,288,30..., dimensions={0} | all-to-all | bytes 524288 | tf_op jit(solution)/shard_map/all_to_all | solution.py:106
  167.0 4.1 %collective-permute-start.5 = (bf16[32,32,128]{2,1,0:T(8,128)(2,1)S(1)}, bf16[32,32,128]{2,1,0:T(8,128)(2,1)S(1)}, u32[]{:S(2)}, u32[]{:S(2)}) collective-permute-start(bf16[32,32,128]{2,1,0:T(8,128)(2,1)S(1)} %all_to_all.56), channel_id=1, source_target_pairs={{0,8},{8,0},{16,24},{24,16},{32,40},{40,32},{48,56},{56,48},{64,72... | collective-permute-start | bytes 786440 | tf_op jit(solution)/shard_map/ppermute | solution.py:408
  173.0 9.8 %all_to_all.57 = f32[16,2,128]{2,1,0:T(2,128)S(1)} all-to-all(f32[16,2,128]{2,1,0:T(2,128)S(1)} %broadcast_in_dim.9), channel_id=1, replica_groups={{0,1,2,3,4,5,6,7,8,9,10,11,12,13,14,15},{16,17,18,19,20,21,22,23,24,25,..., dimensions={0} | all-to-all | bytes 32768 | tf_op jit(solution)/shard_map/all_to_all | solution.py:106
  182.8 12.3 %all_to_all.58 = f32[32,2,128]{2,1,0:T(2,128)S(1)} all-to-all(f32[32,2,128]{2,1,0:T(2,128)S(1)} %broadcast_in_dim.10), channel_id=1, replica_groups={{0,16,32,48,64,80,96,112,128,144,160,176,192,208,224,240,256,272,288,30..., dimensions={0} | all-to-all | bytes 65536 | tf_op jit(solution)/shard_map/all_to_all | solution.py:106
  (33 shorter events, 8.1 us)
Async XLA Ops:
  0.0 75.6 %copy-start = (bf16[2048,256]{1,0:T(8,128)(2,1)S(1)}, bf16[2048,256]{1,0:T(8,128)(2,1)}, u32[]{:S(2)}) copy-start(bf16[2048,256]{1,0:T(8,128)(2,1)} %param.11) | copy-start | bytes 3145732
  0.0 11.7 %copy-start.3 = (bf16[1,24,512]{2,1,0:T(8,128)(2,1)S(1)}, bf16[1,24,512]{2,1,0:T(8,128)(2,1)}, u32[]{:S(2)}) copy-start(bf16[1,24,512]{2,1,0:T(8,128)(2,1)} %param.10) | copy-start | bytes 73732
  0.0 14.6 %collective-permute-start.1 = (bf16[512,128]{1,0:T(8,128)(2,1)}, bf16[512,128]{1,0:T(8,128)(2,1)S(1)}, u32[]{:S(2)}, u32[]{:S(2)}) collective-permute-start(bf16[512,128]{1,0:T(8,128)(2,1)} %bitcast.43), channel_id=1, source_target_pairs={{8,0},{16,8},{24,16},{32,24},{40,32},{48,40},{56,48},{64,56},{72,6... | collective-permute-start | bytes 393224 | tf_op jit(solution)/shard_map/ppermute | solution.py:352
  8.9 8.3 %collective-permute-start = (bf16[512,128]{1,0:T(8,128)(2,1)}, bf16[512,128]{1,0:T(8,128)(2,1)S(1)}, u32[]{:S(2)}, u32[]{:S(2)}) collective-permute-start(bf16[512,128]{1,0:T(8,128)(2,1)} %bitcast.44), channel_id=1, source_target_pairs={{0,8},{8,16},{16,24},{24,32},{32,40},{40,48},{48,56},{56,64},{64,7... | collective-permute-start | bytes 393224 | tf_op jit(solution)/shard_map/ppermute | solution.py:351
  11.7 0.9 copy-start.2
  39.9 34.4 %copy-start.1 = (bf16[1,512,512]{2,1,0:T(8,128)(2,1)S(1)}, bf16[1,512,512]{2,1,0:T(8,128)(2,1)}, u32[]{:S(2)}) copy-start(bf16[1,512,512]{2,1,0:T(8,128)(2,1)} %param.9) | copy-start | bytes 1572868
  68.8 6.6 %collective-permute-start.2 = (bf16[32,32,128]{2,1,0:T(8,128)(2,1)S(1)}, bf16[32,32,128]{2,1,0:T(8,128)(2,1)S(1)}, u32[]{:S(2)}, u32[]{:S(2)}) collective-permute-start(bf16[32,32,128]{2,1,0:T(8,128)(2,1)S(1)} %all_to_all.52.after_ref), channel_id=1, source_target_pairs={{0,8},{8,0},{16,24},{24,16},{32,40},{40,32},{48,56},{56,48},{64,72... | collective-permute-start | bytes 786440 | tf_op jit(solution)/shard_map/ppermute | solution.py:377
  97.5 16.5 %all-to-all-start.4 = ((bf16[64,8,128]{2,1,0:T(8,128)(2,1)}), bf16[64,8,128]{2,1,0:T(8,128)(2,1)S(1)}, u32[]{:S(2)}, u32[]{:S(2)}) async-start(bf16[64,8,128]{2,1,0:T(8,128)(2,1)} %bitcast.11), calls=%async_computation.4 | async-start | bytes 262144 | tf_op jit(solution)/shard_map/all_to_all | solution.py:106
  102.6 6.3 %collective-permute-start.3 = (f32[312,128]{1,0:T(8,128)S(1)}, f32[312,128]{1,0:T(8,128)S(1)}, u32[]{:S(2)}, u32[]{:S(2)}) collective-permute-start(f32[312,128]{1,0:T(8,128)S(1)} %get-tuple-element.45), channel_id=1, source_target_pairs={{0,8},{8,16},{16,24},{24,32},{32,40},{40,48},{48,56},{56,64},{64,7... | collective-permute-start | bytes 479240 | tf_op jit(solution)/shard_map/ppermute | solution.py:385
  106.2 7.0 %collective-permute-start.4 = (f32[312,128]{1,0:T(8,128)S(1)}, f32[312,128]{1,0:T(8,128)S(1)}, u32[]{:S(2)}, u32[]{:S(2)}) collective-permute-start(f32[312,128]{1,0:T(8,128)S(1)} %get-tuple-element.46), channel_id=1, source_target_pairs={{8,0},{16,8},{24,16},{32,24},{40,32},{48,40},{56,48},{64,56},{72,6... | collective-permute-start | bytes 479240 | tf_op jit(solution)/shard_map/ppermute | solution.py:386
  167.0 5.2 %collective-permute-start.5 = (bf16[32,32,128]{2,1,0:T(8,128)(2,1)S(1)}, bf16[32,32,128]{2,1,0:T(8,128)(2,1)S(1)}, u32[]{:S(2)}, u32[]{:S(2)}) collective-permute-start(bf16[32,32,128]{2,1,0:T(8,128)(2,1)S(1)} %all_to_all.56), channel_id=1, source_target_pairs={{0,8},{8,0},{16,24},{24,16},{32,40},{40,32},{48,56},{56,48},{64,72... | collective-permute-start | bytes 786440 | tf_op jit(solution)/shard_map/ppermute | solution.py:408

commit v9 on v8

--- a/solution.py
+++ b/solution.py
@@ -248,7 +248,7 @@
         for c in range(n_coarse):
             out_ref[c] = joined(dot(ones_where(across == asked[:, c : c + 1]), share), 3)
 
-    def reply(in_ref, given_ref, near_ref, out_ref):
+    def reply(in_ref, given_ref, near_ref, before_ref, next_ref, out_ref):
         solved = in_ref[0]
         for c in range(1, n_coarse):
             solved = solved + in_ref[c]
@@ -391,7 +391,12 @@
         specs=[VMEM, VMEM, HBM],
     )
     incoming = exchange(outgoing, "coarse")
-    (outgoing,) = run(reply, [((n_sub * REPLIES, cases), BF16)], incoming, given, near)
+    (outgoing,) = run(
+        reply,
+        [((n_sub * REPLIES, cases), BF16)],
+        incoming, given, near, from_before, from_next,
+        specs=[VMEM, VMEM, VMEM, HBM, HBM],
+    )
     replies = exchange(outgoing.reshape(n_sub, REPLIES, cases), "sub").reshape(n_sub * REPLIES, cases)
     image, outgoing = run(
         join,

time: 197 us -> 195 us (0.990)
  blocking collectives: 142 us -> 134 us
  waiting for transfers between devices: 9.37 us -> 17 us
  starting transfers between devices: 31 us -> 28.2 us
    all_to_all x1, waiting for transfers between devices: 0.77 us -> 9.15 us  [exchange(): lax.all_to_all(blocks, axis, 0, 0, tiled=True, axis_index_groups=groups)]
    all_to_all x9, blocking collectives: 142 us -> 134 us  [exchange(): lax.all_to_all(blocks, axis, 0, 0, tiled=True, axis_index_groups=groups)]
  transfers between devices with their start and end apart: 7 -> 7, of which waited for: 6 -> 5; matrix products, arithmetic and copies ran while one was open for 0% -> 0% of each run, Pallas kernels for 2% -> 2%
where the time goes in v9:
time: 195 us
  blocking collectives  134 us (69%)
  starting transfers between devices  28.2 us (14%)
  waiting for transfers between devices  17 us (9%)
  Pallas kernels  9.65 us (5%)
  other arithmetic  2.28 us (1%)
    all_to_all x9, blocking collectives, exchange(): lax.all_to_all(blocks, axis, 0, 0, tiled=True, axis_index_groups=groups)  134 us
    pallas_call x11, Pallas kernels, run(): pl.pallas_call(kernel, out_shape=[jax.ShapeDtypeStruct(shape, dtype) for...  9.65 us
    ppermute x2, starting transfers between devices, body(): theirs = lax.ppermute(mine, 'sub', other_core)  9.58 us
    all_to_all x1, waiting for transfers between devices, exchange(): lax.all_to_all(blocks, axis, 0, 0, tiled=True, axis_index_groups=groups)  9.15 us
    ppermute x1, starting transfers between devices, body(): from_next = lax.ppermute(start, 'sub', to_before)  8.91 us
    ppermute x1, waiting for transfers between devices, body(): from_next = lax.ppermute(to_behind, 'sub', to_before)  4.37 us
  transfers between devices with their start and end apart: 7, of which 5 were waited for; matrix products, arithmetic and copies ran while one was open for 0% of the time, Pallas kernels for 2%

profile of v9, /device:TPU:1, one launch (start us, length us, event | category | flops | bytes accessed | tf_op | source)
XLA Modules:
  0.0 194.6 jit_solution(17490720157623101483)
XLA Ops:
  0.0 8.9 %collective-permute-start.1 = (bf16[512,128]{1,0:T(8,128)(2,1)}, bf16[512,128]{1,0:T(8,128)(2,1)S(1)}, u32[]{:S(2)}, u32[]{:S(2)}) collective-permute-start(bf16[512,128]{1,0:T(8,128)(2,1)} %bitcast.44), channel_id=1, source_target_pairs={{8,0},{16,8},{24,16},{32,24},{40,32},{48,40},{56,48},{64,56},{72,6... | collective-permute-start | bytes 393224 | tf_op jit(solution)/shard_map/ppermute | solution.py:352
  8.9 1.9 collective-permute-start
  12.6 1.9 shard_map.82
  14.6 2.6 %collective-permute-done.before_ref = bf16[512,128]{1,0:T(8,128)(2,1)S(1)} collective-permute-done((bf16[512,128]{1,0:T(8,128)(2,1)}, bf16[512,128]{1,0:T(8,128)(2,1)S(1)}, u32[]{:S(2)}, u32[]{:S(2)}) %collective-permute-start) | collective-permute-done | bytes 131104 | tf_op jit(solution)/shard_map/ppermute | solution.py:351
  18.1 21.4 %all_to_all.50 = f32[64,4,128]{2,1,0:T(4,128)S(1)} all-to-all(f32[64,4,128]{2,1,0:T(4,128)S(1)} %bitcast.47), channel_id=1, replica_groups=mesh['sub'=64,'coarse'=8] {'sub'}, dimensions={0} | all-to-all | bytes 262144 | tf_op jit(solution)/shard_map/all_to_all | solution.py:106
  39.9 15.3 %all_to_all.51.in_ref = f32[8,40,128]{2,1,0:T(8,128)S(1)} all-to-all(f32[8,40,128]{2,1,0:T(8,128)S(1)} %get-tuple-element.37), channel_id=1, replica_groups=mesh['sub'=64,'coarse'=8] {'coarse'}, dimensions={0} | all-to-all | bytes 327680 | tf_op jit(solution)/shard_map/all_to_all | solution.py:106
  55.2 13.6 %all_to_all.52.after_ref = bf16[32,32,128]{2,1,0:T(8,128)(2,1)S(1)} all-to-all(bf16[32,32,128]{2,1,0:T(8,128)(2,1)S(1)} %get-tuple-element.38), channel_id=1, replica_groups={{0,16,32,48,64,80,96,112,128,144,160,176,192,208,224,240,256,272,288,30..., dimensions={0} | all-to-all | bytes 524288 | tf_op jit(solution)/shard_map/all_to_all | solution.py:106
  68.8 5.5 %collective-permute-start.2 = (bf16[32,32,128]{2,1,0:T(8,128)(2,1)S(1)}, bf16[32,32,128]{2,1,0:T(8,128)(2,1)}, u32[]{:S(2)}, u32[]{:S(2)}) collective-permute-start(bf16[32,32,128]{2,1,0:T(8,128)(2,1)S(1)} %all_to_all.52.after_ref), channel_id=1, source_target_pairs={{0,8},{8,0},{16,24},{24,16},{32,40},{40,32},{48,56},{56,48},{64,72... | collective-permute-start | bytes 786440 | tf_op jit(solution)/shard_map/ppermute | solution.py:377
  74.3 1.7 shard_map.86
  76.0 1.2 maximum_select_fusion
  77.7 1.4 shard_map.87
  79.1 3.5 %all-to-all-start.3 = ((f32[8,128,128]{2,1,0:T(8,128)}), f32[8,128,128]{2,1,0:T(8,128)S(1)}, u32[]{:S(2)}, u32[]{:S(2)}) async-start(f32[8,128,128]{2,1,0:T(8,128)} %shard_map.87), calls=%async_computation.3 | async-start | bytes 1048576 | tf_op jit(solution)/shard_map/all_to_all | solution.py:106
  82.6 1.9 collective-permute-start.3
  84.5 2.4 %collective-permute-start.4 = (f32[312,128]{1,0:T(8,128)S(1)}, f32[312,128]{1,0:T(8,128)S(1)}, u32[]{:S(2)}, u32[]{:S(2)}) collective-permute-start(f32[312,128]{1,0:T(8,128)S(1)} %get-tuple-element.45), channel_id=1, source_target_pairs={{8,0},{16,8},{24,16},{32,24},{40,32},{48,40},{56,48},{64,56},{72,6... | collective-permute-start | bytes 479240 | tf_op jit(solution)/shard_map/ppermute | solution.py:386
  87.0 4.4 %collective-permute-done.4.next_ref = f32[312,128]{1,0:T(8,128)S(1)} collective-permute-done((f32[312,128]{1,0:T(8,128)S(1)}, f32[312,128]{1,0:T(8,128)S(1)}, u32[]{:S(2)}, u32[]{:S(2)}) %collective-permute-start.4) | collective-permute-done | bytes 159776 | tf_op jit(solution)/shard_map/ppermute | solution.py:386
  91.4 9.2 %all-to-all-done.3.in_ref = f32[8,128,128]{2,1,0:T(8,128)S(1)} async-done(((f32[8,128,128]{2,1,0:T(8,128)}), f32[8,128,128]{2,1,0:T(8,128)S(1)}, u32[]{:S(2)}, u32[]{:S(2)}) %all-to-all-start.3) | async-done | bytes 524320 | tf_op jit(solution)/shard_map/all_to_all | solution.py:106
  100.9 15.1 %all_to_all.53 = bf16[64,8,128]{2,1,0:T(8,128)(2,1)S(1)} all-to-all(bf16[64,8,128]{2,1,0:T(8,128)(2,1)S(1)} %bitcast.42), channel_id=1, replica_groups=mesh['sub'=64,'coarse'=8] {'sub'}, dimensions={0} | all-to-all | bytes 262144 | tf_op jit(solution)/shard_map/all_to_all | solution.py:106
  116.0 1.5 shard_map.89
  117.5 13.4 %all_to_all.54.in_ref = f32[8,56,128]{2,1,0:T(8,128)S(1)} all-to-all(f32[8,56,128]{2,1,0:T(8,128)S(1)} %get-tuple-element.49), channel_id=1, replica_groups=mesh['sub'=64,'coarse'=8] {'coarse'}, dimensions={0} | all-to-all | bytes 458752 | tf_op jit(solution)/shard_map/all_to_all | solution.py:106
  131.2 18.5 %all_to_all.55 = bf16[64,16,128]{2,1,0:T(8,128)(2,1)S(1)} all-to-all(bf16[64,16,128]{2,1,0:T(8,128)(2,1)S(1)} %bitcast.43), channel_id=1, replica_groups=mesh['sub'=64,'coarse'=8] {'sub'}, dimensions={0} | all-to-all | bytes 524288 | tf_op jit(solution)/shard_map/all_to_all | solution.py:106
  150.7 15.0 %all_to_all.56 = bf16[32,32,128]{2,1,0:T(8,128)(2,1)S(1)} all-to-all(bf16[32,32,128]{2,1,0:T(8,128)(2,1)S(1)} %get-tuple-element.55), channel_id=1, replica_groups={{0,16,32,48,64,80,96,112,128,144,160,176,192,208,224,240,256,272,288,30..., dimensions={0} | all-to-all | bytes 524288 | tf_op jit(solution)/shard_map/all_to_all | solution.py:106
  165.7 4.1 %collective-permute-start.5 = (bf16[32,32,128]{2,1,0:T(8,128)(2,1)S(1)}, bf16[32,32,128]{2,1,0:T(8,128)(2,1)S(1)}, u32[]{:S(2)}, u32[]{:S(2)}) collective-permute-start(bf16[32,32,128]{2,1,0:T(8,128)(2,1)S(1)} %all_to_all.56), channel_id=1, source_target_pairs={{0,8},{8,0},{16,24},{24,16},{32,40},{40,32},{48,56},{56,48},{64,72... | collective-permute-start | bytes 786440 | tf_op jit(solution)/shard_map/ppermute | solution.py:413
  171.7 9.8 %all_to_all.57 = f32[16,2,128]{2,1,0:T(2,128)S(1)} all-to-all(f32[16,2,128]{2,1,0:T(2,128)S(1)} %broadcast_in_dim.9), channel_id=1, replica_groups={{0,1,2,3,4,5,6,7,8,9,10,11,12,13,14,15},{16,17,18,19,20,21,22,23,24,25,..., dimensions={0} | all-to-all | bytes 32768 | tf_op jit(solution)/shard_map/all_to_all | solution.py:106
  181.5 12.3 %all_to_all.58 = f32[32,2,128]{2,1,0:T(2,128)S(1)} all-to-all(f32[32,2,128]{2,1,0:T(2,128)S(1)} %broadcast_in_dim.10), channel_id=1, replica_groups={{0,16,32,48,64,80,96,112,128,144,160,176,192,208,224,240,256,272,288,30..., dimensions={0} | all-to-all | bytes 65536 | tf_op jit(solution)/shard_map/all_to_all | solution.py:106
  (33 shorter events, 8.0 us)
Async XLA Ops:
  0.0 77.2 %copy-start = (bf16[2048,256]{1,0:T(8,128)(2,1)S(1)}, bf16[2048,256]{1,0:T(8,128)(2,1)}, u32[]{:S(2)}) copy-start(bf16[2048,256]{1,0:T(8,128)(2,1)} %param.11) | copy-start | bytes 3145732
  0.0 11.7 %copy-start.3 = (bf16[1,24,512]{2,1,0:T(8,128)(2,1)S(1)}, bf16[1,24,512]{2,1,0:T(8,128)(2,1)}, u32[]{:S(2)}) copy-start(bf16[1,24,512]{2,1,0:T(8,128)(2,1)} %param.10) | copy-start | bytes 73732
  0.0 14.6 %collective-permute-start.1 = (bf16[512,128]{1,0:T(8,128)(2,1)}, bf16[512,128]{1,0:T(8,128)(2,1)S(1)}, u32[]{:S(2)}, u32[]{:S(2)}) collective-permute-start(bf16[512,128]{1,0:T(8,128)(2,1)} %bitcast.44), channel_id=1, source_target_pairs={{8,0},{16,8},{24,16},{32,24},{40,32},{48,40},{56,48},{64,56},{72,6... | collective-permute-start | bytes 393224 | tf_op jit(solution)/shard_map/ppermute | solution.py:352
  8.9 8.3 %collective-permute-start = (bf16[512,128]{1,0:T(8,128)(2,1)}, bf16[512,128]{1,0:T(8,128)(2,1)S(1)}, u32[]{:S(2)}, u32[]{:S(2)}) collective-permute-start(bf16[512,128]{1,0:T(8,128)(2,1)} %bitcast.45), channel_id=1, source_target_pairs={{0,8},{8,16},{16,24},{24,32},{32,40},{40,48},{48,56},{56,64},{64,7... | collective-permute-start | bytes 393224 | tf_op jit(solution)/shard_map/ppermute | solution.py:351
  11.7 0.9 copy-start.2
  39.9 34.4 %copy-start.1 = (bf16[1,512,512]{2,1,0:T(8,128)(2,1)S(1)}, bf16[1,512,512]{2,1,0:T(8,128)(2,1)}, u32[]{:S(2)}) copy-start(bf16[1,512,512]{2,1,0:T(8,128)(2,1)} %param.9) | copy-start | bytes 1572868
  68.8 7.2 %collective-permute-start.2 = (bf16[32,32,128]{2,1,0:T(8,128)(2,1)S(1)}, bf16[32,32,128]{2,1,0:T(8,128)(2,1)}, u32[]{:S(2)}, u32[]{:S(2)}) collective-permute-start(bf16[32,32,128]{2,1,0:T(8,128)(2,1)S(1)} %all_to_all.52.after_ref), channel_id=1, source_target_pairs={{0,8},{8,0},{16,24},{24,16},{32,40},{40,32},{48,56},{56,48},{64,72... | collective-permute-start | bytes 786440 | tf_op jit(solution)/shard_map/ppermute | solution.py:377
  79.1 21.5 %all-to-all-start.3 = ((f32[8,128,128]{2,1,0:T(8,128)}), f32[8,128,128]{2,1,0:T(8,128)S(1)}, u32[]{:S(2)}, u32[]{:S(2)}) async-start(f32[8,128,128]{2,1,0:T(8,128)} %shard_map.87), calls=%async_computation.3 | async-start | bytes 1048576 | tf_op jit(solution)/shard_map/all_to_all | solution.py:106
  82.6 4.4 %collective-permute-start.3 = (f32[312,128]{1,0:T(8,128)}, f32[312,128]{1,0:T(8,128)S(1)}, u32[]{:S(2)}, u32[]{:S(2)}) collective-permute-start(f32[312,128]{1,0:T(8,128)} %get-tuple-element.44), channel_id=1, source_target_pairs={{0,8},{8,16},{16,24},{24,32},{32,40},{40,48},{48,56},{56,64},{64,7... | collective-permute-start | bytes 479240 | tf_op jit(solution)/shard_map/ppermute | solution.py:385
  84.5 6.9 %collective-permute-start.4 = (f32[312,128]{1,0:T(8,128)S(1)}, f32[312,128]{1,0:T(8,128)S(1)}, u32[]{:S(2)}, u32[]{:S(2)}) collective-permute-start(f32[312,128]{1,0:T(8,128)S(1)} %get-tuple-element.45), channel_id=1, source_target_pairs={{8,0},{16,8},{24,16},{32,24},{40,32},{48,40},{56,48},{64,56},{72,6... | collective-permute-start | bytes 479240 | tf_op jit(solution)/shard_map/ppermute | solution.py:386
  165.7 5.2 %collective-permute-start.5 = (bf16[32,32,128]{2,1,0:T(8,128)(2,1)S(1)}, bf16[32,32,128]{2,1,0:T(8,128)(2,1)S(1)}, u32[]{:S(2)}, u32[]{:S(2)}) collective-permute-start(bf16[32,32,128]{2,1,0:T(8,128)(2,1)S(1)} %all_to_all.56), channel_id=1, source_target_pairs={{0,8},{8,0},{16,24},{24,16},{32,40},{40,32},{48,56},{56,48},{64,72... | collective-permute-start | bytes 786440 | tf_op jit(solution)/shard_map/ppermute | solution.py:413

commit v10 on v9

--- a/solution.py
+++ b/solution.py
@@ -110,7 +110,7 @@
 
     def set_up(
         ints_ref, row_ref, coupling_ref, load_ref,
-        slotted_ref, turned_ref, asked_ref, codes_ref, table_ref, here_ref, ahead_ref, behind_ref,
+        slotted_ref, asked_ref, codes_ref, table_ref, here_ref, ahead_ref, behind_ref,
     ):
         here_ref[...] = load_ref[...]
         sub_at, coarse_at = ints_ref[0, 0], ints_ref[0, 1]
@@ -157,7 +157,6 @@
             codes_ref[k + 1 : k + 2, :] = codes[:, k * cases : (k + 1) * cases]
         slotted_ref[...] = dot(placed, coupling_ref[...]).astype(BF16)
         wide_eye = iota((prims, cases), 0) == iota((prims, cases), 1)
-        turned_ref[...] = dot_t(coupling_ref[...], ones_where(wide_eye)).astype(BF16)
         line_col = jnp.sum(jnp.where(same, owner_row * REPLIES + second, 0), axis=1, keepdims=True)
         line_row = jnp.sum(jnp.where(wide_eye, line_col, 0), axis=0, keepdims=True).astype(F32)
         line_row = jnp.where(iota((1, cases), 1) < prims, line_row, NOBODY)
@@ -189,11 +188,11 @@
         out_ref[...] = terms + asked_ref[...] + jnp.where(line == LINES - 1, squares, 0.0)
 
     def springs(
-        table_ref, residual_ref, schur_ref, ahead_in, behind_in, after_ref, local_ref, near_ref, ahead_ref, behind_ref
+        table_ref, residual_ref, schur_ref, coupling_ref, ahead_in, behind_in, after_ref,
+        near_ref, old_ref, ahead_ref, behind_ref, local_ref,
     ):
-        twice = 2.0 * residual_ref[...]
-        local_ref[...] = dot(schur_ref[...], twice.astype(BF16))
-        near_ref[...] = jnp.sum(twice * local_ref[...], axis=0, keepdims=True)
+        jumps, rest = in_two(2.0 * residual_ref[...])
+        local_ref[...] = dot(schur_ref[...], jumps)
         ahead_ref[half * width :] = ahead_in[...]
         behind_ref[half * width :] = behind_in[...]
         for e in range(edges):
@@ -207,10 +206,13 @@
             def _():
                 behind_ref[place, :] = local_ref[edge(e), :]
 
+        near_ref[...] = 2.0 * jnp.sum(residual_ref[...] * local_ref[...], axis=0, keepdims=True)
+        old_ref[...] = joined(dot(coupling_ref[...], jnp.concatenate([jumps, rest], axis=1)), 2)
+
     def line_of(shape, dim):
         return (iota(shape, dim) & (LINES - 1)) * n_sub + (iota(shape, dim) >> 2)
 
-    def owner_sums(in_ref, codes_ref, out_ref, norm_ref):
+    def owner_sums(in_ref, codes_ref, out_ref, norm_ref, kept_ref):
         given = in_ref[...]
         line = iota((lines, cases), 0) & (LINES - 1)
         asked = jnp.sum(jnp.where(line == CAPACITY, given, 0.0), axis=0, keepdims=True)
@@ -218,7 +220,9 @@
         expand = ones_where(iota((slots, lines), 0) == line_of((slots, lines), 1))
         wide = dot(jnp.broadcast_to(asked, (SIDES, slots)).astype(BF16), expand)[:1]
         marks = ones_where((iota((block, lines), 0) + 1).astype(F32) == wide)
-        partial = joined(dot(marks, in_three(given)), 3)
+        parts = in_three(given)
+        partial = joined(dot(marks, parts), 3)
+        kept_ref[...] = joined(dot(expand, parts), 3)
         sides = codes_ref[...] + jnp.where(iota((SIDES, cases), 0) == 0, asked, 0.0)
         for c in range(n_coarse):
             out_ref[c, :piece] = partial[c * piece : (c + 1) * piece]
@@ -259,17 +263,14 @@
         expand = ones_where((source == iota((total, slots), 1)) & (line < 3 * CAPACITY))
         solved = solved.astype(BF16)
         wide = dot(expand, solved)
-        given = given_ref[...]
-        own = ones_where(line_of((lines, slots), 0) == iota((lines, slots), 1))
-        line = iota((lines, cases), 0) & (LINES - 1)
-        terms = jnp.where(line < CAPACITY, given * dot(own, solved), 0.0)
-        high, low = in_two(near_ref[...] + jnp.sum(terms, axis=0, keepdims=True))
+        far = jnp.sum(given_ref[...] * solved.astype(F32), axis=0, keepdims=True)
+        high, low = in_two(near_ref[...] + far)
         line = iota((total, cases), 0) & (REPLIES - 1)
         wide = jnp.where(line == 3 * CAPACITY, high.astype(F32), wide)
         out_ref[...] = jnp.where(line == 3 * CAPACITY + 1, low.astype(F32), wide).astype(BF16)
 
     def join(
-        table_ref, in_ref, local_ref, before_ref, next_ref, turned_ref, own_ref, coupling_ref, residual_ref, norm_ref,
+        table_ref, in_ref, own_ahead_ref, own_behind_ref, before_ref, next_ref, coupling_ref, old_ref, norm_ref,
         jump_ref, out_ref, behind_ref, ahead_ref,
     ):
         replies = in_ref[...]
@@ -278,7 +279,7 @@
         curvature = jnp.sum(jnp.where(line >= 3 * CAPACITY, replies.astype(F32), 0.0), axis=0, keepdims=True)
         packed = half * width
         codes_at = packed + packed // cases * prims
-        codes = [own_ref[packed // cases * prims :], before_ref[codes_at:], next_ref[codes_at:]]
+        codes = [own_ahead_ref[codes_at:], before_ref[codes_at:], next_ref[codes_at:]]
         values = []
         for k, code in enumerate(codes):
             column = jnp.transpose(code)[:, :1] + float(k * CAPACITY)
@@ -289,18 +290,18 @@
             there = [side_ref[packed + k * prims : packed + (k + 1) * prims] for k in range(packed // cases)]
             turned = dot_t(jnp.concatenate(there, axis=1).astype(BF16), wide_eye).astype(BF16)
             ref[...] = side_ref[:packed] + dot(turned, value)
-        image = local_ref[...] + dot(turned_ref[...], values[0])
+        back = dot(dot_t(coupling_ref[...], wide_eye).astype(BF16), values[0])
         for e in range(edges):
             place = pl.ds(pl.multiple_of(table_ref[1, e] * width, width), width)
             facing = jnp.where(table_ref[0, e] == 1, ahead_ref[place, :], behind_ref[place, :])
-            jump_ref[edge(e), :] = image[edge(e), :] - facing
-        pair = jnp.concatenate(in_two(2.0 * residual_ref[...]) + in_two(2.0 * jump_ref[...]), axis=1)
-        rows_there = dot(coupling_ref[...], pair)
-        old, new = joined(rows_there[:, : 2 * cases], 2), joined(rows_there[:, 2 * cases :], 2)
+            place = pl.ds(pl.multiple_of(table_ref[2, e] * width, width), width)
+            own = jnp.where(table_ref[0, e] == 1, own_ahead_ref[place, :], own_behind_ref[place, :])
+            jump_ref[edge(e), :] = own + back[edge(e), :] - facing
+        new = joined(dot(coupling_ref[...], jnp.concatenate(in_two(2.0 * jump_ref[...]), axis=1)), 2)
         line = iota((SIDES, cases), 0)
         tail = jnp.where(line == 0, curvature, jnp.where(line == 1, norm_ref[...], 0.0))
         for c in range(n_coarse):
-            out_ref[c, :prims] = old
+            out_ref[c, :prims] = old_ref[...]
             out_ref[c, prims : 2 * prims] = new
             out_ref[c, 2 * prims :] = tail
 
@@ -351,11 +352,10 @@
     from_before = lax.ppermute(start, "sub", to_next)
     from_next = lax.ppermute(start, "sub", to_before)
     packed = ((half * width // cases * prims + SIDES, cases), F32)
-    slotted, turned, asked, codes, table, start, ahead, behind = run(
+    slotted, asked, codes, table, start, ahead, behind = run(
         set_up,
         [
             ((lines, order), BF16),
-            ((order, cases), BF16),
             ((lines, slots), F32),
             scalars_shape,
             ((5, edges), I32),
@@ -370,17 +370,20 @@
         first, [field, ((lines, cases), F32)], table, start, from_before, from_next, slotted, asked
     )
     given = exchange(outgoing.reshape(n_sub, LINES, cases), "sub").reshape(lines, cases)
-    outgoing, norm = run(owner_sums, [((n_coarse, piece + SIDES, cases), F32), row], given, codes)
+    outgoing, norm, kept = run(
+        owner_sums, [((n_coarse, piece + SIDES, cases), F32), row, ((slots, cases), F32)], given, codes
+    )
     incoming = exchange(outgoing, "coarse")
     rhs, sides = run(coarse_sums, [gathered, ((2 * SIDES, cases), F32)], incoming)
     mine = exchange(rhs, "sub", same_core)
     theirs = lax.ppermute(mine, "sub", other_core)
     side = ((half * width + packed[0][0], cases), F32)
-    local, near, to_ahead, to_behind = run(
+    near, old, to_ahead, to_behind = run(
         springs,
-        [field, row, side, side],
-        table, residual, schur[0], ahead, behind, mine,
-        specs=[SMEM, VMEM, VMEM, VMEM, VMEM, HBM],
+        [row, ((prims, cases), F32), side, side],
+        table, residual, schur[0], coupling[0], ahead, behind, mine,
+        specs=[SMEM, VMEM, VMEM, VMEM, VMEM, VMEM, HBM],
+        scratch=[pltpu.VMEM((order, cases), F32)],
     )
     from_before = lax.ppermute(to_ahead, "sub", to_next)
     from_next = lax.ppermute(to_behind, "sub", to_before)
@@ -394,14 +397,14 @@
     (outgoing,) = run(
         reply,
         [((n_sub * REPLIES, cases), BF16)],
-        incoming, given, near, from_before, from_next,
+        incoming, kept, near, from_before, from_next,
         specs=[VMEM, VMEM, VMEM, HBM, HBM],
     )
     replies = exchange(outgoing.reshape(n_sub, REPLIES, cases), "sub").reshape(n_sub * REPLIES, cases)
     image, outgoing = run(
         join,
         [field, ((n_coarse, 2 * prims + SIDES, cases), F32)],
-        table, replies, local, from_before, from_next, turned, ahead, coupling[0], residual, norm,
+        table, replies, to_ahead, to_behind, from_before, from_next, coupling[0], old, norm,
         scratch=[pltpu.VMEM((half * width, cases), F32)] * 2,
     )
     incoming = exchange(outgoing, "coarse")

time: 195 us -> 193 us (0.990)
  waiting for transfers between devices: 17 us -> 14.4 us
  blocking collectives: 134 us -> 136 us
    ppermute x1, starting transfers between devices: 8.91 us -> 6.2 us  [body(): from_next = lax.ppermute(start, 'sub', to_before)]
    ppermute x1, starting transfers between devices: 1.92 us -> 4.63 us  [body(): from_before = lax.ppermute(start, 'sub', to_next)]
    ppermute x1, waiting for transfers between devices: 2.6 us -> 0.01 us  [body(): from_before = lax.ppermute(start, 'sub', to_next)]
  transfers between devices with their start and end apart: 7 -> 7, of which waited for: 5 -> 3; matrix products, arithmetic and copies ran while one was open for 0% -> 0% of each run, Pallas kernels for 2% -> 2%
where the time goes in v10:
time: 193 us; the launch traced here: 192 us
  blocking collectives  136 us (70%)
  starting transfers between devices  28.3 us (15%)
  waiting for transfers between devices  14.4 us (7%)
  Pallas kernels  9.05 us (5%)
    all_to_all x9, blocking collectives, exchange(): lax.all_to_all(blocks, axis, 0, 0, tiled=True, axis_index_groups=groups)  136 us
    ppermute x2, starting transfers between devices, body(): theirs = lax.ppermute(mine, 'sub', other_core)  9.66 us
    all_to_all x1, waiting for transfers between devices, exchange(): lax.all_to_all(blocks, axis, 0, 0, tiled=True, axis_index_groups=groups)  9.12 us
    pallas_call x11, Pallas kernels, run(): pl.pallas_call(kernel, out_shape=[jax.ShapeDtypeStruct(shape, dtype) for...  9.05 us
    ppermute x1, starting transfers between devices, body(): from_next = lax.ppermute(start, 'sub', to_before)  6.2 us
    ppermute x1, starting transfers between devices, body(): from_before = lax.ppermute(start, 'sub', to_next)  4.63 us
    ppermute x1, waiting for transfers between devices, body(): from_next = lax.ppermute(to_behind, 'sub', to_before)  4.46 us
  transfers between devices with their start and end apart: 7, of which 3 were waited for; matrix products, arithmetic and copies ran while one was open for 0% of the time, Pallas kernels for 2%

profile of v10, /device:TPU:1, one launch (start us, length us, event | category | flops | bytes accessed | tf_op | source)
XLA Modules:
  0.0 192.3 jit_solution(11391406414582294958)
XLA Ops:
  0.0 4.6 %collective-permute-start = (bf16[512,128]{1,0:T(8,128)(2,1)}, bf16[512,128]{1,0:T(8,128)(2,1)S(1)}, u32[]{:S(2)}, u32[]{:S(2)}) collective-permute-start(bf16[512,128]{1,0:T(8,128)(2,1)} %bitcast.46), channel_id=1, source_target_pairs={{0,8},{8,16},{16,24},{24,32},{32,40},{40,48},{48,56},{56,64},{64,7... | collective-permute-start | bytes 393224 | tf_op jit(solution)/shard_map/ppermute | solution.py:352
  4.6 6.2 %collective-permute-start.1 = (bf16[512,128]{1,0:T(8,128)(2,1)}, bf16[512,128]{1,0:T(8,128)(2,1)S(1)}, u32[]{:S(2)}, u32[]{:S(2)}) collective-permute-start(bf16[512,128]{1,0:T(8,128)(2,1)} %bitcast.47), channel_id=1, source_target_pairs={{8,0},{16,8},{24,16},{32,24},{40,32},{48,40},{56,48},{64,56},{72,6... | collective-permute-start | bytes 393224 | tf_op jit(solution)/shard_map/ppermute | solution.py:353
  11.7 0.9 copy-done.3
  12.6 1.8 shard_map.82
  15.4 23.0 %all_to_all.50 = f32[64,4,128]{2,1,0:T(4,128)S(1)} all-to-all(f32[64,4,128]{2,1,0:T(4,128)S(1)} %bitcast.49), channel_id=1, replica_groups=mesh['sub'=64,'coarse'=8] {'sub'}, dimensions={0} | all-to-all | bytes 262144 | tf_op jit(solution)/shard_map/all_to_all | solution.py:106
  38.8 15.3 %all_to_all.51.in_ref = f32[8,40,128]{2,1,0:T(8,128)S(1)} all-to-all(f32[8,40,128]{2,1,0:T(8,128)S(1)} %get-tuple-element.37), channel_id=1, replica_groups=mesh['sub'=64,'coarse'=8] {'coarse'}, dimensions={0} | all-to-all | bytes 327680 | tf_op jit(solution)/shard_map/all_to_all | solution.py:106
  54.2 13.6 %all_to_all.52.after_ref = bf16[32,32,128]{2,1,0:T(8,128)(2,1)S(1)} all-to-all(bf16[32,32,128]{2,1,0:T(8,128)(2,1)S(1)} %get-tuple-element.38), channel_id=1, replica_groups={{0,16,32,48,64,80,96,112,128,144,160,176,192,208,224,240,256,272,288,30..., dimensions={0} | all-to-all | bytes 524288 | tf_op jit(solution)/shard_map/all_to_all | solution.py:106
  67.7 5.6 %collective-permute-start.2 = (bf16[32,32,128]{2,1,0:T(8,128)(2,1)S(1)}, bf16[32,32,128]{2,1,0:T(8,128)(2,1)S(1)}, u32[]{:S(2)}, u32[]{:S(2)}) collective-permute-start(bf16[32,32,128]{2,1,0:T(8,128)(2,1)S(1)} %all_to_all.52.after_ref), channel_id=1, source_target_pairs={{0,8},{8,0},{16,24},{24,16},{32,40},{40,32},{48,56},{56,48},{64,72... | collective-permute-start | bytes 786440 | tf_op jit(solution)/shard_map/ppermute | solution.py:379
  73.3 1.2 shard_map.86
  75.3 1.4 shard_map.87
  76.6 3.5 %all-to-all-start.3 = ((f32[8,128,128]{2,1,0:T(8,128)}), f32[8,128,128]{2,1,0:T(8,128)S(1)}, u32[]{:S(2)}, u32[]{:S(2)}) async-start(f32[8,128,128]{2,1,0:T(8,128)} %shard_map.87), calls=%async_computation.3 | async-start | bytes 1048576 | tf_op jit(solution)/shard_map/all_to_all | solution.py:106
  80.1 1.9 collective-permute-start.3
  82.1 2.4 %collective-permute-start.4 = (f32[312,128]{1,0:T(8,128)S(1)}, f32[312,128]{1,0:T(8,128)S(1)}, u32[]{:S(2)}, u32[]{:S(2)}) collective-permute-start(f32[312,128]{1,0:T(8,128)S(1)} %get-tuple-element.46.own_behind_ref), channel_id=1, source_target_pairs={{8,0},{16,8},{24,16},{32,24},{40,32},{48,40},{56,48},{64,56},{72,6... | collective-permute-start | bytes 479240 | tf_op jit(solution)/shard_map/ppermute | solution.py:389
  84.5 4.5 %collective-permute-done.4.next_ref = f32[312,128]{1,0:T(8,128)S(1)} collective-permute-done((f32[312,128]{1,0:T(8,128)S(1)}, f32[312,128]{1,0:T(8,128)S(1)}, u32[]{:S(2)}, u32[]{:S(2)}) %collective-permute-start.4) | collective-permute-done | bytes 159776 | tf_op jit(solution)/shard_map/ppermute | solution.py:389
  89.0 9.1 %all-to-all-done.3.in_ref = f32[8,128,128]{2,1,0:T(8,128)S(1)} async-done(((f32[8,128,128]{2,1,0:T(8,128)}), f32[8,128,128]{2,1,0:T(8,128)S(1)}, u32[]{:S(2)}, u32[]{:S(2)}) %all-to-all-start.3) | async-done | bytes 524320 | tf_op jit(solution)/shard_map/all_to_all | solution.py:106
  98.4 14.9 %all_to_all.53 = bf16[64,8,128]{2,1,0:T(8,128)(2,1)S(1)} all-to-all(bf16[64,8,128]{2,1,0:T(8,128)(2,1)S(1)} %bitcast.41), channel_id=1, replica_groups=mesh['sub'=64,'coarse'=8] {'sub'}, dimensions={0} | all-to-all | bytes 262144 | tf_op jit(solution)/shard_map/all_to_all | solution.py:106
  113.3 1.5 shard_map.89
  114.8 13.8 %all_to_all.54.in_ref = f32[8,56,128]{2,1,0:T(8,128)S(1)} all-to-all(f32[8,56,128]{2,1,0:T(8,128)S(1)} %get-tuple-element.49), channel_id=1, replica_groups=mesh['sub'=64,'coarse'=8] {'coarse'}, dimensions={0} | all-to-all | bytes 458752 | tf_op jit(solution)/shard_map/all_to_all | solution.py:106
  128.9 18.5 %all_to_all.55 = bf16[64,16,128]{2,1,0:T(8,128)(2,1)S(1)} all-to-all(bf16[64,16,128]{2,1,0:T(8,128)(2,1)S(1)} %bitcast.42), channel_id=1, replica_groups=mesh['sub'=64,'coarse'=8] {'sub'}, dimensions={0} | all-to-all | bytes 524288 | tf_op jit(solution)/shard_map/all_to_all | solution.py:106
  147.5 0.9 shard_map.92
  148.4 15.0 %all_to_all.56 = bf16[32,32,128]{2,1,0:T(8,128)(2,1)S(1)} all-to-all(bf16[32,32,128]{2,1,0:T(8,128)(2,1)S(1)} %get-tuple-element.55), channel_id=1, replica_groups={{0,16,32,48,64,80,96,112,128,144,160,176,192,208,224,240,256,272,288,30..., dimensions={0} | all-to-all | bytes 524288 | tf_op jit(solution)/shard_map/all_to_all | solution.py:106
  163.4 4.1 %collective-permute-start.5 = (bf16[32,32,128]{2,1,0:T(8,128)(2,1)S(1)}, bf16[32,32,128]{2,1,0:T(8,128)(2,1)S(1)}, u32[]{:S(2)}, u32[]{:S(2)}) collective-permute-start(bf16[32,32,128]{2,1,0:T(8,128)(2,1)S(1)} %all_to_all.56), channel_id=1, source_target_pairs={{0,8},{8,0},{16,24},{24,16},{32,40},{40,32},{48,56},{56,48},{64,72... | collective-permute-start | bytes 786440 | tf_op jit(solution)/shard_map/ppermute | solution.py:416
  169.4 9.8 %all_to_all.57 = f32[16,2,128]{2,1,0:T(2,128)S(1)} all-to-all(f32[16,2,128]{2,1,0:T(2,128)S(1)} %broadcast_in_dim.9), channel_id=1, replica_groups={{0,1,2,3,4,5,6,7,8,9,10,11,12,13,14,15},{16,17,18,19,20,21,22,23,24,25,..., dimensions={0} | all-to-all | bytes 32768 | tf_op jit(solution)/shard_map/all_to_all | solution.py:106
  179.2 12.3 %all_to_all.58 = f32[32,2,128]{2,1,0:T(2,128)S(1)} all-to-all(f32[32,2,128]{2,1,0:T(2,128)S(1)} %broadcast_in_dim.10), channel_id=1, replica_groups={{0,16,32,48,64,80,96,112,128,144,160,176,192,208,224,240,256,272,288,30..., dimensions={0} | all-to-all | bytes 65536 | tf_op jit(solution)/shard_map/all_to_all | solution.py:106
  (33 shorter events, 6.3 us)
Async XLA Ops:
  0.0 74.7 %copy-start = (bf16[2048,256]{1,0:T(8,128)(2,1)S(1)}, bf16[2048,256]{1,0:T(8,128)(2,1)}, u32[]{:S(2)}) copy-start(bf16[2048,256]{1,0:T(8,128)(2,1)} %param.11) | copy-start | bytes 3145732
  0.0 11.7 %copy-start.2 = (bf16[1,24,512]{2,1,0:T(8,128)(2,1)S(1)}, bf16[1,24,512]{2,1,0:T(8,128)(2,1)}, u32[]{:S(2)}) copy-start(bf16[1,24,512]{2,1,0:T(8,128)(2,1)} %param.10) | copy-start | bytes 73732
  0.0 14.5 %collective-permute-start = (bf16[512,128]{1,0:T(8,128)(2,1)}, bf16[512,128]{1,0:T(8,128)(2,1)S(1)}, u32[]{:S(2)}, u32[]{:S(2)}) collective-permute-start(bf16[512,128]{1,0:T(8,128)(2,1)} %bitcast.46), channel_id=1, source_target_pairs={{0,8},{8,16},{16,24},{24,32},{32,40},{40,48},{48,56},{56,64},{64,7... | collective-permute-start | bytes 393224 | tf_op jit(solution)/shard_map/ppermute | solution.py:352
  4.6 9.8 %collective-permute-start.1 = (bf16[512,128]{1,0:T(8,128)(2,1)}, bf16[512,128]{1,0:T(8,128)(2,1)S(1)}, u32[]{:S(2)}, u32[]{:S(2)}) collective-permute-start(bf16[512,128]{1,0:T(8,128)(2,1)} %bitcast.47), channel_id=1, source_target_pairs={{8,0},{16,8},{24,16},{32,24},{40,32},{48,40},{56,48},{64,56},{72,6... | collective-permute-start | bytes 393224 | tf_op jit(solution)/shard_map/ppermute | solution.py:353
  11.7 0.9 copy-start.3
  38.8 34.5 %copy-start.1 = (bf16[1,512,512]{2,1,0:T(8,128)(2,1)S(1)}, bf16[1,512,512]{2,1,0:T(8,128)(2,1)}, u32[]{:S(2)}) copy-start(bf16[1,512,512]{2,1,0:T(8,128)(2,1)} %param.9) | copy-start | bytes 1572868
  67.7 6.8 %collective-permute-start.2 = (bf16[32,32,128]{2,1,0:T(8,128)(2,1)S(1)}, bf16[32,32,128]{2,1,0:T(8,128)(2,1)S(1)}, u32[]{:S(2)}, u32[]{:S(2)}) collective-permute-start(bf16[32,32,128]{2,1,0:T(8,128)(2,1)S(1)} %all_to_all.52.after_ref), channel_id=1, source_target_pairs={{0,8},{8,0},{16,24},{24,16},{32,40},{40,32},{48,56},{56,48},{64,72... | collective-permute-start | bytes 786440 | tf_op jit(solution)/shard_map/ppermute | solution.py:379
  76.6 21.4 %all-to-all-start.3 = ((f32[8,128,128]{2,1,0:T(8,128)}), f32[8,128,128]{2,1,0:T(8,128)S(1)}, u32[]{:S(2)}, u32[]{:S(2)}) async-start(f32[8,128,128]{2,1,0:T(8,128)} %shard_map.87), calls=%async_computation.3 | async-start | bytes 1048576 | tf_op jit(solution)/shard_map/all_to_all | solution.py:106
  80.1 4.3 %collective-permute-start.3 = (f32[312,128]{1,0:T(8,128)S(1)}, f32[312,128]{1,0:T(8,128)S(1)}, u32[]{:S(2)}, u32[]{:S(2)}) collective-permute-start(f32[312,128]{1,0:T(8,128)S(1)} %get-tuple-element.45.own_ahead_ref), channel_id=1, source_target_pairs={{0,8},{8,16},{16,24},{24,32},{32,40},{40,48},{48,56},{56,64},{64,7... | collective-permute-start | bytes 479240 | tf_op jit(solution)/shard_map/ppermute | solution.py:388
  82.1 6.9 %collective-permute-start.4 = (f32[312,128]{1,0:T(8,128)S(1)}, f32[312,128]{1,0:T(8,128)S(1)}, u32[]{:S(2)}, u32[]{:S(2)}) collective-permute-start(f32[312,128]{1,0:T(8,128)S(1)} %get-tuple-element.46.own_behind_ref), channel_id=1, source_target_pairs={{8,0},{16,8},{24,16},{32,24},{40,32},{48,40},{56,48},{64,56},{72,6... | collective-permute-start | bytes 479240 | tf_op jit(solution)/shard_map/ppermute | solution.py:389
  163.4 5.3 %collective-permute-start.5 = (bf16[32,32,128]{2,1,0:T(8,128)(2,1)S(1)}, bf16[32,32,128]{2,1,0:T(8,128)(2,1)S(1)}, u32[]{:S(2)}, u32[]{:S(2)}) collective-permute-start(bf16[32,32,128]{2,1,0:T(8,128)(2,1)S(1)} %all_to_all.56), channel_id=1, source_target_pairs={{0,8},{8,0},{16,24},{24,16},{32,40},{40,32},{48,56},{56,48},{64,72... | collective-permute-start | bytes 786440 | tf_op jit(solution)/shard_map/ppermute | solution.py:416

commit v11 on v10

--- a/solution.py
+++ b/solution.py
@@ -212,7 +212,7 @@
     def line_of(shape, dim):
         return (iota(shape, dim) & (LINES - 1)) * n_sub + (iota(shape, dim) >> 2)
 
-    def owner_sums(in_ref, codes_ref, out_ref, norm_ref, kept_ref):
+    def owner_sums(in_ref, codes_ref, before_ref, next_ref, out_ref, norm_ref, kept_ref):
         given = in_ref[...]
         line = iota((lines, cases), 0) & (LINES - 1)
         asked = jnp.sum(jnp.where(line == CAPACITY, given, 0.0), axis=0, keepdims=True)
@@ -245,14 +245,14 @@
         )
         return dot_t(coarse_inverse, both.reshape(rows, cases))
 
-    def answer(share_ref, sides_ref, after_ref, out_ref):
+    def answer(share_ref, sides_ref, out_ref):
         asked = jnp.transpose(sides_ref[:n_coarse])
         across = (iota((slots, block), 1) + 1).astype(F32)
         share = in_three(share_ref[...])
         for c in range(n_coarse):
             out_ref[c] = joined(dot(ones_where(across == asked[:, c : c + 1]), share), 3)
 
-    def reply(in_ref, given_ref, near_ref, before_ref, next_ref, out_ref):
+    def reply(in_ref, given_ref, near_ref, out_ref):
         solved = in_ref[0]
         for c in range(1, n_coarse):
             solved = solved + in_ref[c]
@@ -369,37 +369,30 @@
     residual, outgoing = run(
         first, [field, ((lines, cases), F32)], table, start, from_before, from_next, slotted, asked
     )
+    side = ((half * width + packed[0][0], cases), F32)
+    near, old, to_ahead, to_behind = run(
+        springs,
+        [row, ((prims, cases), F32), side, side],
+        table, residual, schur[0], coupling[0], ahead, behind, outgoing,
+        specs=[SMEM, VMEM, VMEM, VMEM, VMEM, VMEM, HBM],
+        scratch=[pltpu.VMEM((order, cases), F32)],
+    )
+    from_before = lax.ppermute(to_ahead, "sub", to_next)
+    from_next = lax.ppermute(to_behind, "sub", to_before)
     given = exchange(outgoing.reshape(n_sub, LINES, cases), "sub").reshape(lines, cases)
     outgoing, norm, kept = run(
-        owner_sums, [((n_coarse, piece + SIDES, cases), F32), row, ((slots, cases), F32)], given, codes
+        owner_sums,
+        [((n_coarse, piece + SIDES, cases), F32), row, ((slots, cases), F32)],
+        given, codes, from_before, from_next,
+        specs=[VMEM, VMEM, HBM, HBM],
     )
     incoming = exchange(outgoing, "coarse")
     rhs, sides = run(coarse_sums, [gathered, ((2 * SIDES, cases), F32)], incoming)
     mine = exchange(rhs, "sub", same_core)
     theirs = lax.ppermute(mine, "sub", other_core)
-    side = ((half * width + packed[0][0], cases), F32)
-    near, old, to_ahead, to_behind = run(
-        springs,
-        [row, ((prims, cases), F32), side, side],
-        table, residual, schur[0], coupling[0], ahead, behind, mine,
-        specs=[SMEM, VMEM, VMEM, VMEM, VMEM, VMEM, HBM],
-        scratch=[pltpu.VMEM((order, cases), F32)],
-    )
-    from_before = lax.ppermute(to_ahead, "sub", to_next)
-    from_next = lax.ppermute(to_behind, "sub", to_before)
-    (outgoing,) = run(
-        answer,
-        [((n_coarse, slots, cases), F32)],
-        product(mine, theirs), sides, near,
-        specs=[VMEM, VMEM, HBM],
-    )
+    (outgoing,) = run(answer, [((n_coarse, slots, cases), F32)], product(mine, theirs), sides)
     incoming = exchange(outgoing, "coarse")
-    (outgoing,) = run(
-        reply,
-        [((n_sub * REPLIES, cases), BF16)],
-        incoming, kept, near, from_before, from_next,
-        specs=[VMEM, VMEM, VMEM, HBM, HBM],
-    )
+    (outgoing,) = run(reply, [((n_sub * REPLIES, cases), BF16)], incoming, kept, near)
     replies = exchange(outgoing.reshape(n_sub, REPLIES, cases), "sub").reshape(n_sub * REPLIES, cases)
     image, outgoing = run(
         join,

time: 193 us -> 200 us (1.036)
  starting transfers between devices: 28.3 us -> 35 us
  blocking collectives: 136 us -> 142 us
  waiting for transfers between devices: 14.4 us -> 9.51 us
    all_to_all x1, waiting for transfers between devices: 9.12 us -> 0.01 us  [exchange(): lax.all_to_all(blocks, axis, 0, 0, tiled=True, axis_index_groups=groups)]
    all_to_all x1, starting transfers between devices: 3.49 us -> 10.9 us  [exchange(): lax.all_to_all(blocks, axis, 0, 0, tiled=True, axis_index_groups=groups)]
    all_to_all x9, blocking collectives: 136 us -> 142 us  [exchange(): lax.all_to_all(blocks, axis, 0, 0, tiled=True, axis_index_groups=groups)]
    ppermute x1, starting transfers between devices: 6.2 us -> 8.91 us  [body(): from_next = lax.ppermute(start, 'sub', to_before)]
    ppermute x1, starting transfers between devices: 4.63 us -> 1.92 us  [body(): from_before = lax.ppermute(start, 'sub', to_next)]
    ppermute x1, waiting for transfers between devices: 0.01 us -> 2.7 us  [body(): from_before = lax.ppermute(start, 'sub', to_next)]
  transfers between devices with their start and end apart: 7 -> 7, of which waited for: 3 -> 5; matrix products, arithmetic and copies ran while one was open for 0% -> 0% of each run, Pallas kernels for 2% -> 2%
where the time goes in v11:
time: 200 us
  blocking collectives  142 us (71%)
  starting transfers between devices  35 us (18%)
  waiting for transfers between devices  9.51 us (5%)
  Pallas kernels  8.91 us (4%)
    all_to_all x9, blocking collectives, exchange(): lax.all_to_all(blocks, axis, 0, 0, tiled=True, axis_index_groups=groups)  142 us
    all_to_all x1, starting transfers between devices, exchange(): lax.all_to_all(blocks, axis, 0, 0, tiled=True, axis_index_groups=groups)  10.9 us
    pallas_call x11, Pallas kernels, run(): pl.pallas_call(kernel, out_shape=[jax.ShapeDtypeStruct(shape, dtype) for...  8.91 us
    ppermute x1, starting transfers between devices, body(): from_next = lax.ppermute(start, 'sub', to_before)  8.91 us
    ppermute x2, starting transfers between devices, body(): theirs = lax.ppermute(mine, 'sub', other_core)  7.82 us
    ppermute x1, waiting for transfers between devices, body(): from_next = lax.ppermute(to_behind, 'sub', to_before)  4.31 us
  transfers between devices with their start and end apart: 7, of which 5 were waited for; matrix products, arithmetic and copies ran while one was open for 0% of the time, Pallas kernels for 2%

profile of v11, /device:TPU:1, one launch (start us, length us, event | category | flops | bytes accessed | tf_op | source)
XLA Modules:
  0.0 199.7 jit_solution(2900895472082976055)
XLA Ops:
  0.0 8.9 %collective-permute-start.1 = (bf16[512,128]{1,0:T(8,128)(2,1)}, bf16[512,128]{1,0:T(8,128)(2,1)S(1)}, u32[]{:S(2)}, u32[]{:S(2)}) collective-permute-start(bf16[512,128]{1,0:T(8,128)(2,1)} %bitcast.46), channel_id=1, source_target_pairs={{8,0},{16,8},{24,16},{32,24},{40,32},{48,40},{56,48},{64,56},{72,6... | collective-permute-start | bytes 393224 | tf_op jit(solution)/shard_map/ppermute | solution.py:353
  8.9 1.9 collective-permute-start
  12.6 1.8 shard_map.82
  14.5 2.7 %collective-permute-done.before_ref = bf16[512,128]{1,0:T(8,128)(2,1)S(1)} collective-permute-done((bf16[512,128]{1,0:T(8,128)(2,1)}, bf16[512,128]{1,0:T(8,128)(2,1)S(1)}, u32[]{:S(2)}, u32[]{:S(2)}) %collective-permute-start) | collective-permute-done | bytes 131104 | tf_op jit(solution)/shard_map/ppermute | solution.py:352
  17.2 1.5 shard_map.83
  18.7 10.9 %all-to-all-start = ((f32[64,4,128]{2,1,0:T(4,128)}), f32[64,4,128]{2,1,0:T(4,128)S(1)}, u32[]{:S(2)}, u32[]{:S(2)}) async-start(f32[64,4,128]{2,1,0:T(4,128)} %bitcast.6), calls=%async_computation | async-start | bytes 262144 | tf_op jit(solution)/shard_map/all_to_all | solution.py:106
  29.6 1.2 shard_map.84
  30.9 3.5 %collective-permute-start.2 = (f32[312,128]{1,0:T(8,128)S(1)}, f32[312,128]{1,0:T(8,128)S(1)}, u32[]{:S(2)}, u32[]{:S(2)}) collective-permute-start(f32[312,128]{1,0:T(8,128)S(1)} %get-tuple-element.40.own_ahead_ref), channel_id=1, source_target_pairs={{0,8},{8,16},{16,24},{24,32},{32,40},{40,48},{48,56},{56,64},{64,7... | collective-permute-start | bytes 479240 | tf_op jit(solution)/shard_map/ppermute | solution.py:380
  34.4 1.9 collective-permute-start.3
  36.9 4.3 %collective-permute-done.3.next_ref = f32[312,128]{1,0:T(8,128)S(1)} collective-permute-done((f32[312,128]{1,0:T(8,128)S(1)}, f32[312,128]{1,0:T(8,128)S(1)}, u32[]{:S(2)}, u32[]{:S(2)}) %collective-permute-start.3) | collective-permute-done | bytes 159776 | tf_op jit(solution)/shard_map/ppermute | solution.py:381
  41.6 15.0 %all_to_all.50.in_ref = f32[8,40,128]{2,1,0:T(8,128)S(1)} all-to-all(f32[8,40,128]{2,1,0:T(8,128)S(1)} %get-tuple-element.42), channel_id=1, replica_groups=mesh['sub'=64,'coarse'=8] {'coarse'}, dimensions={0} | all-to-all | bytes 327680 | tf_op jit(solution)/shard_map/all_to_all | solution.py:106
  56.7 23.2 %all_to_all.51 = bf16[32,32,128]{2,1,0:T(8,128)(2,1)S(1)} all-to-all(bf16[32,32,128]{2,1,0:T(8,128)(2,1)S(1)} %get-tuple-element.43), channel_id=1, replica_groups={{0,16,32,48,64,80,96,112,128,144,160,176,192,208,224,240,256,272,288,30..., dimensions={0} | all-to-all | bytes 524288 | tf_op jit(solution)/shard_map/all_to_all | solution.py:106
  79.8 3.7 %collective-permute-start.4 = (bf16[32,32,128]{2,1,0:T(8,128)(2,1)S(1)}, bf16[32,32,128]{2,1,0:T(8,128)(2,1)S(1)}, u32[]{:S(2)}, u32[]{:S(2)}) collective-permute-start(bf16[32,32,128]{2,1,0:T(8,128)(2,1)S(1)} %all_to_all.51), channel_id=1, source_target_pairs={{0,8},{8,0},{16,24},{24,16},{32,40},{40,32},{48,56},{56,48},{64,72... | collective-permute-start | bytes 786440 | tf_op jit(solution)/shard_map/ppermute | solution.py:392
  83.5 1.1 collective-permute-done.4
  86.0 20.4 %all_to_all.52.in_ref = f32[8,128,128]{2,1,0:T(8,128)S(1)} all-to-all(f32[8,128,128]{2,1,0:T(8,128)S(1)} %shard_map.87), channel_id=1, replica_groups=mesh['sub'=64,'coarse'=8] {'coarse'}, dimensions={0} | all-to-all | bytes 1048576 | tf_op jit(solution)/shard_map/all_to_all | solution.py:106
  106.6 15.3 %all_to_all.53 = bf16[64,8,128]{2,1,0:T(8,128)(2,1)S(1)} all-to-all(bf16[64,8,128]{2,1,0:T(8,128)(2,1)S(1)} %bitcast.40), channel_id=1, replica_groups=mesh['sub'=64,'coarse'=8] {'sub'}, dimensions={0} | all-to-all | bytes 262144 | tf_op jit(solution)/shard_map/all_to_all | solution.py:106
  121.9 1.5 shard_map.89
  123.4 13.9 %all_to_all.54.in_ref = f32[8,56,128]{2,1,0:T(8,128)S(1)} all-to-all(f32[8,56,128]{2,1,0:T(8,128)S(1)} %get-tuple-element.49), channel_id=1, replica_groups=mesh['sub'=64,'coarse'=8] {'coarse'}, dimensions={0} | all-to-all | bytes 458752 | tf_op jit(solution)/shard_map/all_to_all | solution.py:106
  137.7 17.1 %all_to_all.55 = bf16[64,16,128]{2,1,0:T(8,128)(2,1)S(1)} all-to-all(bf16[64,16,128]{2,1,0:T(8,128)(2,1)S(1)} %bitcast.42), channel_id=1, replica_groups=mesh['sub'=64,'coarse'=8] {'sub'}, dimensions={0} | all-to-all | bytes 524288 | tf_op jit(solution)/shard_map/all_to_all | solution.py:106
  154.8 0.9 shard_map.92
  155.8 15.0 %all_to_all.56 = bf16[32,32,128]{2,1,0:T(8,128)(2,1)S(1)} all-to-all(bf16[32,32,128]{2,1,0:T(8,128)(2,1)S(1)} %get-tuple-element.55), channel_id=1, replica_groups={{0,16,32,48,64,80,96,112,128,144,160,176,192,208,224,240,256,272,288,30..., dimensions={0} | all-to-all | bytes 524288 | tf_op jit(solution)/shard_map/all_to_all | solution.py:106
  170.8 4.1 %collective-permute-start.5 = (bf16[32,32,128]{2,1,0:T(8,128)(2,1)S(1)}, bf16[32,32,128]{2,1,0:T(8,128)(2,1)S(1)}, u32[]{:S(2)}, u32[]{:S(2)}) collective-permute-start(bf16[32,32,128]{2,1,0:T(8,128)(2,1)S(1)} %all_to_all.56), channel_id=1, source_target_pairs={{0,8},{8,0},{16,24},{24,16},{32,40},{40,32},{48,56},{56,48},{64,72... | collective-permute-start | bytes 786440 | tf_op jit(solution)/shard_map/ppermute | solution.py:409
  176.8 9.8 %all_to_all.57 = f32[16,2,128]{2,1,0:T(2,128)S(1)} all-to-all(f32[16,2,128]{2,1,0:T(2,128)S(1)} %broadcast_in_dim.9), channel_id=1, replica_groups={{0,1,2,3,4,5,6,7,8,9,10,11,12,13,14,15},{16,17,18,19,20,21,22,23,24,25,..., dimensions={0} | all-to-all | bytes 32768 | tf_op jit(solution)/shard_map/all_to_all | solution.py:106
  186.6 12.3 %all_to_all.58 = f32[32,2,128]{2,1,0:T(2,128)S(1)} all-to-all(f32[32,2,128]{2,1,0:T(2,128)S(1)} %broadcast_in_dim.10), channel_id=1, replica_groups={{0,16,32,48,64,80,96,112,128,144,160,176,192,208,224,240,256,272,288,30..., dimensions={0} | all-to-all | bytes 65536 | tf_op jit(solution)/shard_map/all_to_all | solution.py:106
  (33 shorter events, 7.4 us)
Async XLA Ops:
  0.0 84.8 %copy-start = (bf16[2048,256]{1,0:T(8,128)(2,1)S(1)}, bf16[2048,256]{1,0:T(8,128)(2,1)}, u32[]{:S(2)}) copy-start(bf16[2048,256]{1,0:T(8,128)(2,1)} %param.11) | copy-start | bytes 3145732
  0.0 11.7 %copy-start.2 = (bf16[1,24,512]{2,1,0:T(8,128)(2,1)S(1)}, bf16[1,24,512]{2,1,0:T(8,128)(2,1)}, u32[]{:S(2)}) copy-start(bf16[1,24,512]{2,1,0:T(8,128)(2,1)} %param.10) | copy-start | bytes 73732
  0.0 14.5 %collective-permute-start.1 = (bf16[512,128]{1,0:T(8,128)(2,1)}, bf16[512,128]{1,0:T(8,128)(2,1)S(1)}, u32[]{:S(2)}, u32[]{:S(2)}) collective-permute-start(bf16[512,128]{1,0:T(8,128)(2,1)} %bitcast.46), channel_id=1, source_target_pairs={{8,0},{16,8},{24,16},{32,24},{40,32},{48,40},{56,48},{64,56},{72,6... | collective-permute-start | bytes 393224 | tf_op jit(solution)/shard_map/ppermute | solution.py:353
  8.9 8.3 %collective-permute-start = (bf16[512,128]{1,0:T(8,128)(2,1)}, bf16[512,128]{1,0:T(8,128)(2,1)S(1)}, u32[]{:S(2)}, u32[]{:S(2)}) collective-permute-start(bf16[512,128]{1,0:T(8,128)(2,1)} %bitcast.47), channel_id=1, source_target_pairs={{0,8},{8,16},{16,24},{24,32},{32,40},{40,48},{48,56},{56,64},{64,7... | collective-permute-start | bytes 393224 | tf_op jit(solution)/shard_map/ppermute | solution.py:352
  11.7 0.9 copy-start.3
  17.2 12.5 %copy-start.1 = (bf16[1,512,512]{2,1,0:T(8,128)(2,1)S(1)}, bf16[1,512,512]{2,1,0:T(8,128)(2,1)}, u32[]{:S(2)}) copy-start(bf16[1,512,512]{2,1,0:T(8,128)(2,1)} %param.9) | copy-start | bytes 1572868
  18.7 22.5 %all-to-all-start = ((f32[64,4,128]{2,1,0:T(4,128)}), f32[64,4,128]{2,1,0:T(4,128)S(1)}, u32[]{:S(2)}, u32[]{:S(2)}) async-start(f32[64,4,128]{2,1,0:T(4,128)} %bitcast.6), calls=%async_computation | async-start | bytes 262144 | tf_op jit(solution)/shard_map/all_to_all | solution.py:106
  30.9 6.0 %collective-permute-start.2 = (f32[312,128]{1,0:T(8,128)S(1)}, f32[312,128]{1,0:T(8,128)S(1)}, u32[]{:S(2)}, u32[]{:S(2)}) collective-permute-start(f32[312,128]{1,0:T(8,128)S(1)} %get-tuple-element.40.own_ahead_ref), channel_id=1, source_target_pairs={{0,8},{8,16},{16,24},{24,32},{32,40},{40,48},{48,56},{56,64},{64,7... | collective-permute-start | bytes 479240 | tf_op jit(solution)/shard_map/ppermute | solution.py:380
  34.4 6.8 %collective-permute-start.3 = (f32[312,128]{1,0:T(8,128)S(1)}, f32[312,128]{1,0:T(8,128)S(1)}, u32[]{:S(2)}, u32[]{:S(2)}) collective-permute-start(f32[312,128]{1,0:T(8,128)S(1)} %get-tuple-element.41.own_behind_ref), channel_id=1, source_target_pairs={{8,0},{16,8},{24,16},{32,24},{40,32},{48,40},{56,48},{64,56},{72,6... | collective-permute-start | bytes 479240 | tf_op jit(solution)/shard_map/ppermute | solution.py:381
  79.8 4.9 %collective-permute-start.4 = (bf16[32,32,128]{2,1,0:T(8,128)(2,1)S(1)}, bf16[32,32,128]{2,1,0:T(8,128)(2,1)S(1)}, u32[]{:S(2)}, u32[]{:S(2)}) collective-permute-start(bf16[32,32,128]{2,1,0:T(8,128)(2,1)S(1)} %all_to_all.51), channel_id=1, source_target_pairs={{0,8},{8,0},{16,24},{24,16},{32,40},{40,32},{48,56},{56,48},{64,72... | collective-permute-start | bytes 786440 | tf_op jit(solution)/shard_map/ppermute | solution.py:392
  170.8 5.2 %collective-permute-start.5 = (bf16[32,32,128]{2,1,0:T(8,128)(2,1)S(1)}, bf16[32,32,128]{2,1,0:T(8,128)(2,1)S(1)}, u32[]{:S(2)}, u32[]{:S(2)}) collective-permute-start(bf16[32,32,128]{2,1,0:T(8,128)(2,1)S(1)} %all_to_all.56), channel_id=1, source_target_pairs={{0,8},{8,0},{16,24},{24,16},{32,40},{40,32},{48,56},{56,48},{64,72... | collective-permute-start | bytes 786440 | tf_op jit(solution)/shard_map/ppermute | solution.py:409

commit v12 on v10

--- a/solution.py
+++ b/solution.py
@@ -55,7 +55,7 @@
 VMEM = pl.BlockSpec(memory_space=pltpu.VMEM)
 
 
-def run(kernel, outs, *args, specs=None, scratch=()):
+def run(kernel, outs, *args, specs=None, out_specs=None, scratch=()):
     def spec(x):
         return SMEM if jnp.issubdtype(x.dtype, jnp.integer) and x.shape[1] <= 8 else VMEM
 
@@ -63,7 +63,7 @@
         kernel,
         out_shape=[jax.ShapeDtypeStruct(shape, dtype) for shape, dtype in outs],
         in_specs=specs or [spec(x) for x in args],
-        out_specs=[SMEM if dtype == I32 else VMEM for _, dtype in outs],
+        out_specs=out_specs or [SMEM if dtype == I32 else VMEM for _, dtype in outs],
         scratch_shapes=scratch,
         compiler_params=pltpu.CompilerParams(vmem_limit_bytes=32 * 1024 * 1024),
     )(*args)
@@ -245,12 +245,17 @@
         )
         return dot_t(coarse_inverse, both.reshape(rows, cases))
 
-    def answer(share_ref, sides_ref, after_ref, out_ref):
+    def answer(share_ref, sides_ref, after_ref, out_ref, block_ref, sems):
         asked = jnp.transpose(sides_ref[:n_coarse])
         across = (iota((slots, block), 1) + 1).astype(F32)
         share = in_three(share_ref[...])
+        moves = []
         for c in range(n_coarse):
-            out_ref[c] = joined(dot(ones_where(across == asked[:, c : c + 1]), share), 3)
+            block_ref[c] = joined(dot(ones_where(across == asked[:, c : c + 1]), share), 3)
+            moves.append(pltpu.make_async_copy(block_ref.at[c], out_ref.at[c], sems.at[c]))
+            moves[c].start()
+        for move in moves:
+            move.wait()
 
     def reply(in_ref, given_ref, near_ref, before_ref, next_ref, out_ref):
         solved = in_ref[0]
@@ -279,18 +284,17 @@
         curvature = jnp.sum(jnp.where(line >= 3 * CAPACITY, replies.astype(F32), 0.0), axis=0, keepdims=True)
         packed = half * width
         codes_at = packed + packed // cases * prims
-        codes = [own_ahead_ref[codes_at:], before_ref[codes_at:], next_ref[codes_at:]]
-        values = []
-        for k, code in enumerate(codes):
-            column = jnp.transpose(code)[:, :1] + float(k * CAPACITY)
-            chosen = ones_where(iota((cases, total), 1).astype(F32) == column)
-            values.append(dot(chosen, replies).astype(BF16))
-        wide_eye = ones_where(iota((prims, cases), 0) == iota((prims, cases), 1))
-        for side_ref, value, ref in ((before_ref, values[1], behind_ref), (next_ref, values[2], ahead_ref)):
-            there = [side_ref[packed + k * prims : packed + (k + 1) * prims] for k in range(packed // cases)]
-            turned = dot_t(jnp.concatenate(there, axis=1).astype(BF16), wide_eye).astype(BF16)
-            ref[...] = side_ref[:packed] + dot(turned, value)
-        back = dot(dot_t(coupling_ref[...], wide_eye).astype(BF16), values[0])
+        line = iota((SIDES, cases), 0)
+        codes = jnp.where(line == 0, own_ahead_ref[codes_at:], before_ref[codes_at:])
+        codes = jnp.transpose(jnp.where(line == 2, next_ref[codes_at:], codes))
+        column = jnp.concatenate([codes[:ROOM, k : k + 1] + float(k * CAPACITY) for k in range(3)], axis=0)
+        chosen = ones_where(iota((3 * ROOM, total), 1).astype(F32) == column)
+        values = dot(chosen, replies).astype(BF16)
+        for k, side_ref, ref in ((1, before_ref, behind_ref), (2, next_ref, ahead_ref)):
+            there = [side_ref[packed + n * prims : packed + (n + 1) * prims] for n in range(packed // cases)]
+            there = jnp.concatenate(there, axis=1).astype(BF16)
+            ref[...] = side_ref[:packed] + dot_t(there, values[k * ROOM : k * ROOM + prims])
+        back = dot_t(coupling_ref[...], values[:prims])
         for e in range(edges):
             place = pl.ds(pl.multiple_of(table_ref[1, e] * width, width), width)
             facing = jnp.where(table_ref[0, e] == 1, ahead_ref[place, :], behind_ref[place, :])
@@ -392,6 +396,8 @@
         [((n_coarse, slots, cases), F32)],
         product(mine, theirs), sides, near,
         specs=[VMEM, VMEM, HBM],
+        out_specs=[HBM],
+        scratch=[pltpu.VMEM((n_coarse, slots, cases), F32), pltpu.SemaphoreType.DMA((n_coarse,))],
     )
     incoming = exchange(outgoing, "coarse")
     (outgoing,) = run(

time: 193 us -> 193 us (level)
  no operation moved by 1% of the time
where the time goes in v12:
time: 193 us; the launch traced here: 192 us
  blocking collectives  136 us (70%)
  starting transfers between devices  28.3 us (15%)
  waiting for transfers between devices  14.4 us (7%)
  Pallas kernels  8.8 us (5%)
    all_to_all x9, blocking collectives, exchange(): lax.all_to_all(blocks, axis, 0, 0, tiled=True, axis_index_groups=groups)  136 us
    ppermute x2, starting transfers between devices, body(): theirs = lax.ppermute(mine, 'sub', other_core)  9.66 us
    all_to_all x1, waiting for transfers between devices, exchange(): lax.all_to_all(blocks, axis, 0, 0, tiled=True, axis_index_groups=groups)  9.12 us
    pallas_call x11, Pallas kernels, run(): pl.pallas_call(kernel, out_shape=[jax.ShapeDtypeStruct(shape, dtype) for...  8.8 us
    ppermute x1, starting transfers between devices, body(): from_next = lax.ppermute(start, 'sub', to_before)  6.2 us
    ppermute x1, starting transfers between devices, body(): from_before = lax.ppermute(start, 'sub', to_next)  4.63 us
    ppermute x1, waiting for transfers between devices, body(): from_next = lax.ppermute(to_behind, 'sub', to_before)  4.46 us
  transfers between devices with their start and end apart: 7, of which 3 were waited for; matrix products, arithmetic and copies ran while one was open for 0% of the time, Pallas kernels for 2%

profile of v12, /device:TPU:1, one launch (start us, length us, event | category | flops | bytes accessed | tf_op | source)
XLA Modules:
  0.0 192.1 jit_solution(9305792057502586)
XLA Ops:
  0.0 4.6 %collective-permute-start = (bf16[512,128]{1,0:T(8,128)(2,1)}, bf16[512,128]{1,0:T(8,128)(2,1)S(1)}, u32[]{:S(2)}, u32[]{:S(2)}) collective-permute-start(bf16[512,128]{1,0:T(8,128)(2,1)} %bitcast.46), channel_id=1, source_target_pairs={{0,8},{8,16},{16,24},{24,32},{32,40},{40,48},{48,56},{56,64},{64,7... | collective-permute-start | bytes 393224 | tf_op jit(solution)/shard_map/ppermute | solution.py:356
  4.6 6.2 %collective-permute-start.1 = (bf16[512,128]{1,0:T(8,128)(2,1)}, bf16[512,128]{1,0:T(8,128)(2,1)S(1)}, u32[]{:S(2)}, u32[]{:S(2)}) collective-permute-start(bf16[512,128]{1,0:T(8,128)(2,1)} %bitcast.47), channel_id=1, source_target_pairs={{8,0},{16,8},{24,16},{32,24},{40,32},{48,40},{56,48},{64,56},{72,6... | collective-permute-start | bytes 393224 | tf_op jit(solution)/shard_map/ppermute | solution.py:357
  11.7 0.9 copy-done.3
  12.6 1.8 shard_map.82
  15.4 23.0 %all_to_all.50 = f32[64,4,128]{2,1,0:T(4,128)S(1)} all-to-all(f32[64,4,128]{2,1,0:T(4,128)S(1)} %bitcast.49), channel_id=1, replica_groups=mesh['sub'=64,'coarse'=8] {'sub'}, dimensions={0} | all-to-all | bytes 262144 | tf_op jit(solution)/shard_map/all_to_all | solution.py:106
  38.8 15.3 %all_to_all.51.in_ref = f32[8,40,128]{2,1,0:T(8,128)S(1)} all-to-all(f32[8,40,128]{2,1,0:T(8,128)S(1)} %get-tuple-element.37), channel_id=1, replica_groups=mesh['sub'=64,'coarse'=8] {'coarse'}, dimensions={0} | all-to-all | bytes 327680 | tf_op jit(solution)/shard_map/all_to_all | solution.py:106
  54.2 13.6 %all_to_all.52.after_ref = bf16[32,32,128]{2,1,0:T(8,128)(2,1)S(1)} all-to-all(bf16[32,32,128]{2,1,0:T(8,128)(2,1)S(1)} %get-tuple-element.38), channel_id=1, replica_groups={{0,16,32,48,64,80,96,112,128,144,160,176,192,208,224,240,256,272,288,30..., dimensions={0} | all-to-all | bytes 524288 | tf_op jit(solution)/shard_map/all_to_all | solution.py:106
  67.7 5.6 %collective-permute-start.2 = (bf16[32,32,128]{2,1,0:T(8,128)(2,1)S(1)}, bf16[32,32,128]{2,1,0:T(8,128)(2,1)S(1)}, u32[]{:S(2)}, u32[]{:S(2)}) collective-permute-start(bf16[32,32,128]{2,1,0:T(8,128)(2,1)S(1)} %all_to_all.52.after_ref), channel_id=1, source_target_pairs={{0,8},{8,0},{16,24},{24,16},{32,40},{40,32},{48,56},{56,48},{64,72... | collective-permute-start | bytes 786440 | tf_op jit(solution)/shard_map/ppermute | solution.py:383
  73.3 1.2 shard_map.86
  75.3 1.3 shard_map.87
  76.5 3.5 %all-to-all-start.3 = ((f32[8,128,128]{2,1,0:T(8,128)}), f32[8,128,128]{2,1,0:T(8,128)S(1)}, u32[]{:S(2)}, u32[]{:S(2)}) async-start(f32[8,128,128]{2,1,0:T(8,128)} %shard_map.87), calls=%async_computation.3 | async-start | bytes 1048576 | tf_op jit(solution)/shard_map/all_to_all | solution.py:106
  80.0 1.9 collective-permute-start.3
  82.0 2.4 %collective-permute-start.4 = (f32[312,128]{1,0:T(8,128)S(1)}, f32[312,128]{1,0:T(8,128)S(1)}, u32[]{:S(2)}, u32[]{:S(2)}) collective-permute-start(f32[312,128]{1,0:T(8,128)S(1)} %get-tuple-element.46.own_behind_ref), channel_id=1, source_target_pairs={{8,0},{16,8},{24,16},{32,24},{40,32},{48,40},{56,48},{64,56},{72,6... | collective-permute-start | bytes 479240 | tf_op jit(solution)/shard_map/ppermute | solution.py:393
  84.4 4.5 %collective-permute-done.4.next_ref = f32[312,128]{1,0:T(8,128)S(1)} collective-permute-done((f32[312,128]{1,0:T(8,128)S(1)}, f32[312,128]{1,0:T(8,128)S(1)}, u32[]{:S(2)}, u32[]{:S(2)}) %collective-permute-start.4) | collective-permute-done | bytes 159776 | tf_op jit(solution)/shard_map/ppermute | solution.py:393
  88.9 9.1 %all-to-all-done.3.in_ref = f32[8,128,128]{2,1,0:T(8,128)S(1)} async-done(((f32[8,128,128]{2,1,0:T(8,128)}), f32[8,128,128]{2,1,0:T(8,128)S(1)}, u32[]{:S(2)}, u32[]{:S(2)}) %all-to-all-start.3) | async-done | bytes 524320 | tf_op jit(solution)/shard_map/all_to_all | solution.py:106
  98.3 14.9 %all_to_all.53 = bf16[64,8,128]{2,1,0:T(8,128)(2,1)S(1)} all-to-all(bf16[64,8,128]{2,1,0:T(8,128)(2,1)S(1)} %bitcast.41), channel_id=1, replica_groups=mesh['sub'=64,'coarse'=8] {'sub'}, dimensions={0} | all-to-all | bytes 262144 | tf_op jit(solution)/shard_map/all_to_all | solution.py:106
  113.2 1.4 shard_map.89
  114.5 13.8 %all_to_all.54.in_ref = f32[8,56,128]{2,1,0:T(8,128)S(1)} all-to-all(f32[8,56,128]{2,1,0:T(8,128)S(1)} %get-tuple-element.49), channel_id=1, replica_groups=mesh['sub'=64,'coarse'=8] {'coarse'}, dimensions={0} | all-to-all | bytes 458752 | tf_op jit(solution)/shard_map/all_to_all | solution.py:106
  128.7 18.5 %all_to_all.55 = bf16[64,16,128]{2,1,0:T(8,128)(2,1)S(1)} all-to-all(bf16[64,16,128]{2,1,0:T(8,128)(2,1)S(1)} %bitcast.42), channel_id=1, replica_groups=mesh['sub'=64,'coarse'=8] {'sub'}, dimensions={0} | all-to-all | bytes 524288 | tf_op jit(solution)/shard_map/all_to_all | solution.py:106
  147.2 0.9 shard_map.92
  148.2 15.0 %all_to_all.56 = bf16[32,32,128]{2,1,0:T(8,128)(2,1)S(1)} all-to-all(bf16[32,32,128]{2,1,0:T(8,128)(2,1)S(1)} %get-tuple-element.55), channel_id=1, replica_groups={{0,16,32,48,64,80,96,112,128,144,160,176,192,208,224,240,256,272,288,30..., dimensions={0} | all-to-all | bytes 524288 | tf_op jit(solution)/shard_map/all_to_all | solution.py:106
  163.1 4.1 %collective-permute-start.5 = (bf16[32,32,128]{2,1,0:T(8,128)(2,1)S(1)}, bf16[32,32,128]{2,1,0:T(8,128)(2,1)S(1)}, u32[]{:S(2)}, u32[]{:S(2)}) collective-permute-start(bf16[32,32,128]{2,1,0:T(8,128)(2,1)S(1)} %all_to_all.56), channel_id=1, source_target_pairs={{0,8},{8,0},{16,24},{24,16},{32,40},{40,32},{48,56},{56,48},{64,72... | collective-permute-start | bytes 786440 | tf_op jit(solution)/shard_map/ppermute | solution.py:422
  169.1 9.8 %all_to_all.57 = f32[16,2,128]{2,1,0:T(2,128)S(1)} all-to-all(f32[16,2,128]{2,1,0:T(2,128)S(1)} %broadcast_in_dim.9), channel_id=1, replica_groups={{0,1,2,3,4,5,6,7,8,9,10,11,12,13,14,15},{16,17,18,19,20,21,22,23,24,25,..., dimensions={0} | all-to-all | bytes 32768 | tf_op jit(solution)/shard_map/all_to_all | solution.py:106
  179.0 12.3 %all_to_all.58 = f32[32,2,128]{2,1,0:T(2,128)S(1)} all-to-all(f32[32,2,128]{2,1,0:T(2,128)S(1)} %broadcast_in_dim.10), channel_id=1, replica_groups={{0,16,32,48,64,80,96,112,128,144,160,176,192,208,224,240,256,272,288,30..., dimensions={0} | all-to-all | bytes 65536 | tf_op jit(solution)/shard_map/all_to_all | solution.py:106
  (33 shorter events, 6.3 us)
Async XLA Ops:
  0.0 74.7 %copy-start = (bf16[2048,256]{1,0:T(8,128)(2,1)S(1)}, bf16[2048,256]{1,0:T(8,128)(2,1)}, u32[]{:S(2)}) copy-start(bf16[2048,256]{1,0:T(8,128)(2,1)} %param.11) | copy-start | bytes 3145732
  0.0 11.7 %copy-start.2 = (bf16[1,24,512]{2,1,0:T(8,128)(2,1)S(1)}, bf16[1,24,512]{2,1,0:T(8,128)(2,1)}, u32[]{:S(2)}) copy-start(bf16[1,24,512]{2,1,0:T(8,128)(2,1)} %param.10) | copy-start | bytes 73732
  0.0 14.5 %collective-permute-start = (bf16[512,128]{1,0:T(8,128)(2,1)}, bf16[512,128]{1,0:T(8,128)(2,1)S(1)}, u32[]{:S(2)}, u32[]{:S(2)}) collective-permute-start(bf16[512,128]{1,0:T(8,128)(2,1)} %bitcast.46), channel_id=1, source_target_pairs={{0,8},{8,16},{16,24},{24,32},{32,40},{40,48},{48,56},{56,64},{64,7... | collective-permute-start | bytes 393224 | tf_op jit(solution)/shard_map/ppermute | solution.py:356
  4.6 9.8 %collective-permute-start.1 = (bf16[512,128]{1,0:T(8,128)(2,1)}, bf16[512,128]{1,0:T(8,128)(2,1)S(1)}, u32[]{:S(2)}, u32[]{:S(2)}) collective-permute-start(bf16[512,128]{1,0:T(8,128)(2,1)} %bitcast.47), channel_id=1, source_target_pairs={{8,0},{16,8},{24,16},{32,24},{40,32},{48,40},{56,48},{64,56},{72,6... | collective-permute-start | bytes 393224 | tf_op jit(solution)/shard_map/ppermute | solution.py:357
  11.7 0.9 copy-start.3
  38.8 34.5 %copy-start.1 = (bf16[1,512,512]{2,1,0:T(8,128)(2,1)S(1)}, bf16[1,512,512]{2,1,0:T(8,128)(2,1)}, u32[]{:S(2)}) copy-start(bf16[1,512,512]{2,1,0:T(8,128)(2,1)} %param.9) | copy-start | bytes 1572868
  67.7 6.8 %collective-permute-start.2 = (bf16[32,32,128]{2,1,0:T(8,128)(2,1)S(1)}, bf16[32,32,128]{2,1,0:T(8,128)(2,1)S(1)}, u32[]{:S(2)}, u32[]{:S(2)}) collective-permute-start(bf16[32,32,128]{2,1,0:T(8,128)(2,1)S(1)} %all_to_all.52.after_ref), channel_id=1, source_target_pairs={{0,8},{8,0},{16,24},{24,16},{32,40},{40,32},{48,56},{56,48},{64,72... | collective-permute-start | bytes 786440 | tf_op jit(solution)/shard_map/ppermute | solution.py:383
  76.5 21.5 %all-to-all-start.3 = ((f32[8,128,128]{2,1,0:T(8,128)}), f32[8,128,128]{2,1,0:T(8,128)S(1)}, u32[]{:S(2)}, u32[]{:S(2)}) async-start(f32[8,128,128]{2,1,0:T(8,128)} %shard_map.87), calls=%async_computation.3 | async-start | bytes 1048576 | tf_op jit(solution)/shard_map/all_to_all | solution.py:106
  80.0 4.3 %collective-permute-start.3 = (f32[312,128]{1,0:T(8,128)S(1)}, f32[312,128]{1,0:T(8,128)S(1)}, u32[]{:S(2)}, u32[]{:S(2)}) collective-permute-start(f32[312,128]{1,0:T(8,128)S(1)} %get-tuple-element.45.own_ahead_ref), channel_id=1, source_target_pairs={{0,8},{8,16},{16,24},{24,32},{32,40},{40,48},{48,56},{56,64},{64,7... | collective-permute-start | bytes 479240 | tf_op jit(solution)/shard_map/ppermute | solution.py:392
  82.0 6.9 %collective-permute-start.4 = (f32[312,128]{1,0:T(8,128)S(1)}, f32[312,128]{1,0:T(8,128)S(1)}, u32[]{:S(2)}, u32[]{:S(2)}) collective-permute-start(f32[312,128]{1,0:T(8,128)S(1)} %get-tuple-element.46.own_behind_ref), channel_id=1, source_target_pairs={{8,0},{16,8},{24,16},{32,24},{40,32},{48,40},{56,48},{64,56},{72,6... | collective-permute-start | bytes 479240 | tf_op jit(solution)/shard_map/ppermute | solution.py:393
  163.1 5.2 %collective-permute-start.5 = (bf16[32,32,128]{2,1,0:T(8,128)(2,1)S(1)}, bf16[32,32,128]{2,1,0:T(8,128)(2,1)S(1)}, u32[]{:S(2)}, u32[]{:S(2)}) collective-permute-start(bf16[32,32,128]{2,1,0:T(8,128)(2,1)S(1)} %all_to_all.56), channel_id=1, source_target_pairs={{0,8},{8,0},{16,24},{24,16},{32,40},{40,32},{48,56},{56,48},{64,72... | collective-permute-start | bytes 786440 | tf_op jit(solution)/shard_map/ppermute | solution.py:422

commit v13 on v12

--- a/solution.py
+++ b/solution.py
@@ -130,8 +130,8 @@
                     lower = (faces[other] == faces[e]) & (named_edge[other] < named_edge[e])
                     place = place + lower.astype(I32)
             table_ref[0, e] = faces[e]
-            table_ref[1, e] = place
-            table_ref[2, e] = faces[e] * ahead + (1 - faces[e]) * (e - ahead)
+            table_ref[1, e] = lax.rem(place, half)
+            table_ref[2, e] = lax.rem(faces[e] * ahead + (1 - faces[e]) * (e - ahead), half)
             table_ref[3, e] = named_edge[e]
             table_ref[4, e] = coarse_at
             ahead = ahead + faces[e]

time: 193 us -> 193 us (level)
  no operation moved by 1% of the time
where the time goes in v13:
time: 193 us; the launch traced here: 192 us
  blocking collectives  136 us (70%)
  starting transfers between devices  28.3 us (15%)
  waiting for transfers between devices  14.4 us (7%)
  Pallas kernels  8.82 us (5%)
    all_to_all x9, blocking collectives, exchange(): lax.all_to_all(blocks, axis, 0, 0, tiled=True, axis_index_groups=groups)  136 us
    ppermute x2, starting transfers between devices, body(): theirs = lax.ppermute(mine, 'sub', other_core)  9.66 us
    all_to_all x1, waiting for transfers between devices, exchange(): lax.all_to_all(blocks, axis, 0, 0, tiled=True, axis_index_groups=groups)  9.12 us
    pallas_call x11, Pallas kernels, run(): pl.pallas_call(kernel, out_shape=[jax.ShapeDtypeStruct(shape, dtype) for...  8.82 us
    ppermute x1, starting transfers between devices, body(): from_next = lax.ppermute(start, 'sub', to_before)  6.2 us
    ppermute x1, starting transfers between devices, body(): from_before = lax.ppermute(start, 'sub', to_next)  4.63 us
    ppermute x1, waiting for transfers between devices, body(): from_next = lax.ppermute(to_behind, 'sub', to_before)  4.46 us
  transfers between devices with their start and end apart: 7, of which 3 were waited for; matrix products, arithmetic and copies ran while one was open for 0% of the time, Pallas kernels for 2%

profile of v13, /device:TPU:1, one launch (start us, length us, event | category | flops | bytes accessed | tf_op | source)
XLA Modules:
  0.0 192.1 jit_solution(1719385008681493728)
XLA Ops:
  0.0 4.6 %collective-permute-start = (bf16[512,128]{1,0:T(8,128)(2,1)}, bf16[512,128]{1,0:T(8,128)(2,1)S(1)}, u32[]{:S(2)}, u32[]{:S(2)}) collective-permute-start(bf16[512,128]{1,0:T(8,128)(2,1)} %bitcast.46), channel_id=1, source_target_pairs={{0,8},{8,16},{16,24},{24,32},{32,40},{40,48},{48,56},{56,64},{64,7... | collective-permute-start | bytes 393224 | tf_op jit(solution)/shard_map/ppermute | solution.py:356
  4.6 6.2 %collective-permute-start.1 = (bf16[512,128]{1,0:T(8,128)(2,1)}, bf16[512,128]{1,0:T(8,128)(2,1)S(1)}, u32[]{:S(2)}, u32[]{:S(2)}) collective-permute-start(bf16[512,128]{1,0:T(8,128)(2,1)} %bitcast.47), channel_id=1, source_target_pairs={{8,0},{16,8},{24,16},{32,24},{40,32},{48,40},{56,48},{64,56},{72,6... | collective-permute-start | bytes 393224 | tf_op jit(solution)/shard_map/ppermute | solution.py:357
  11.7 0.9 copy-done.3
  12.6 1.9 shard_map.82
  15.4 23.0 %all_to_all.50 = f32[64,4,128]{2,1,0:T(4,128)S(1)} all-to-all(f32[64,4,128]{2,1,0:T(4,128)S(1)} %bitcast.49), channel_id=1, replica_groups=mesh['sub'=64,'coarse'=8] {'sub'}, dimensions={0} | all-to-all | bytes 262144 | tf_op jit(solution)/shard_map/all_to_all | solution.py:106
  38.8 15.3 %all_to_all.51.in_ref = f32[8,40,128]{2,1,0:T(8,128)S(1)} all-to-all(f32[8,40,128]{2,1,0:T(8,128)S(1)} %get-tuple-element.37), channel_id=1, replica_groups=mesh['sub'=64,'coarse'=8] {'coarse'}, dimensions={0} | all-to-all | bytes 327680 | tf_op jit(solution)/shard_map/all_to_all | solution.py:106
  54.2 13.6 %all_to_all.52.after_ref = bf16[32,32,128]{2,1,0:T(8,128)(2,1)S(1)} all-to-all(bf16[32,32,128]{2,1,0:T(8,128)(2,1)S(1)} %get-tuple-element.38), channel_id=1, replica_groups={{0,16,32,48,64,80,96,112,128,144,160,176,192,208,224,240,256,272,288,30..., dimensions={0} | all-to-all | bytes 524288 | tf_op jit(solution)/shard_map/all_to_all | solution.py:106
  67.7 5.6 %collective-permute-start.2 = (bf16[32,32,128]{2,1,0:T(8,128)(2,1)S(1)}, bf16[32,32,128]{2,1,0:T(8,128)(2,1)S(1)}, u32[]{:S(2)}, u32[]{:S(2)}) collective-permute-start(bf16[32,32,128]{2,1,0:T(8,128)(2,1)S(1)} %all_to_all.52.after_ref), channel_id=1, source_target_pairs={{0,8},{8,0},{16,24},{24,16},{32,40},{40,32},{48,56},{56,48},{64,72... | collective-permute-start | bytes 786440 | tf_op jit(solution)/shard_map/ppermute | solution.py:383
  73.3 1.2 shard_map.86
  75.3 1.3 shard_map.87
  76.5 3.5 %all-to-all-start.3 = ((f32[8,128,128]{2,1,0:T(8,128)}), f32[8,128,128]{2,1,0:T(8,128)S(1)}, u32[]{:S(2)}, u32[]{:S(2)}) async-start(f32[8,128,128]{2,1,0:T(8,128)} %shard_map.87), calls=%async_computation.3 | async-start | bytes 1048576 | tf_op jit(solution)/shard_map/all_to_all | solution.py:106
  80.0 1.9 collective-permute-start.3
  82.0 2.4 %collective-permute-start.4 = (f32[312,128]{1,0:T(8,128)S(1)}, f32[312,128]{1,0:T(8,128)S(1)}, u32[]{:S(2)}, u32[]{:S(2)}) collective-permute-start(f32[312,128]{1,0:T(8,128)S(1)} %get-tuple-element.46.own_behind_ref), channel_id=1, source_target_pairs={{8,0},{16,8},{24,16},{32,24},{40,32},{48,40},{56,48},{64,56},{72,6... | collective-permute-start | bytes 479240 | tf_op jit(solution)/shard_map/ppermute | solution.py:393
  84.4 4.5 %collective-permute-done.4.next_ref = f32[312,128]{1,0:T(8,128)S(1)} collective-permute-done((f32[312,128]{1,0:T(8,128)S(1)}, f32[312,128]{1,0:T(8,128)S(1)}, u32[]{:S(2)}, u32[]{:S(2)}) %collective-permute-start.4) | collective-permute-done | bytes 159776 | tf_op jit(solution)/shard_map/ppermute | solution.py:393
  88.9 9.1 %all-to-all-done.3.in_ref = f32[8,128,128]{2,1,0:T(8,128)S(1)} async-done(((f32[8,128,128]{2,1,0:T(8,128)}), f32[8,128,128]{2,1,0:T(8,128)S(1)}, u32[]{:S(2)}, u32[]{:S(2)}) %all-to-all-start.3) | async-done | bytes 524320 | tf_op jit(solution)/shard_map/all_to_all | solution.py:106
  98.3 14.9 %all_to_all.53 = bf16[64,8,128]{2,1,0:T(8,128)(2,1)S(1)} all-to-all(bf16[64,8,128]{2,1,0:T(8,128)(2,1)S(1)} %bitcast.41), channel_id=1, replica_groups=mesh['sub'=64,'coarse'=8] {'sub'}, dimensions={0} | all-to-all | bytes 262144 | tf_op jit(solution)/shard_map/all_to_all | solution.py:106
  113.2 1.4 shard_map.89
  114.5 13.8 %all_to_all.54.in_ref = f32[8,56,128]{2,1,0:T(8,128)S(1)} all-to-all(f32[8,56,128]{2,1,0:T(8,128)S(1)} %get-tuple-element.49), channel_id=1, replica_groups=mesh['sub'=64,'coarse'=8] {'coarse'}, dimensions={0} | all-to-all | bytes 458752 | tf_op jit(solution)/shard_map/all_to_all | solution.py:106
  128.7 18.5 %all_to_all.55 = bf16[64,16,128]{2,1,0:T(8,128)(2,1)S(1)} all-to-all(bf16[64,16,128]{2,1,0:T(8,128)(2,1)S(1)} %bitcast.42), channel_id=1, replica_groups=mesh['sub'=64,'coarse'=8] {'sub'}, dimensions={0} | all-to-all | bytes 524288 | tf_op jit(solution)/shard_map/all_to_all | solution.py:106
  147.2 0.9 shard_map.92
  148.2 15.0 %all_to_all.56 = bf16[32,32,128]{2,1,0:T(8,128)(2,1)S(1)} all-to-all(bf16[32,32,128]{2,1,0:T(8,128)(2,1)S(1)} %get-tuple-element.55), channel_id=1, replica_groups={{0,16,32,48,64,80,96,112,128,144,160,176,192,208,224,240,256,272,288,30..., dimensions={0} | all-to-all | bytes 524288 | tf_op jit(solution)/shard_map/all_to_all | solution.py:106
  163.1 4.1 %collective-permute-start.5 = (bf16[32,32,128]{2,1,0:T(8,128)(2,1)S(1)}, bf16[32,32,128]{2,1,0:T(8,128)(2,1)S(1)}, u32[]{:S(2)}, u32[]{:S(2)}) collective-permute-start(bf16[32,32,128]{2,1,0:T(8,128)(2,1)S(1)} %all_to_all.56), channel_id=1, source_target_pairs={{0,8},{8,0},{16,24},{24,16},{32,40},{40,32},{48,56},{56,48},{64,72... | collective-permute-start | bytes 786440 | tf_op jit(solution)/shard_map/ppermute | solution.py:422
  169.1 9.8 %all_to_all.57 = f32[16,2,128]{2,1,0:T(2,128)S(1)} all-to-all(f32[16,2,128]{2,1,0:T(2,128)S(1)} %broadcast_in_dim.9), channel_id=1, replica_groups={{0,1,2,3,4,5,6,7,8,9,10,11,12,13,14,15},{16,17,18,19,20,21,22,23,24,25,..., dimensions={0} | all-to-all | bytes 32768 | tf_op jit(solution)/shard_map/all_to_all | solution.py:106
  179.0 12.3 %all_to_all.58 = f32[32,2,128]{2,1,0:T(2,128)S(1)} all-to-all(f32[32,2,128]{2,1,0:T(2,128)S(1)} %broadcast_in_dim.10), channel_id=1, replica_groups={{0,16,32,48,64,80,96,112,128,144,160,176,192,208,224,240,256,272,288,30..., dimensions={0} | all-to-all | bytes 65536 | tf_op jit(solution)/shard_map/all_to_all | solution.py:106
  (33 shorter events, 6.3 us)
Async XLA Ops:
  0.0 74.7 %copy-start = (bf16[2048,256]{1,0:T(8,128)(2,1)S(1)}, bf16[2048,256]{1,0:T(8,128)(2,1)}, u32[]{:S(2)}) copy-start(bf16[2048,256]{1,0:T(8,128)(2,1)} %param.11) | copy-start | bytes 3145732
  0.0 11.7 %copy-start.2 = (bf16[1,24,512]{2,1,0:T(8,128)(2,1)S(1)}, bf16[1,24,512]{2,1,0:T(8,128)(2,1)}, u32[]{:S(2)}) copy-start(bf16[1,24,512]{2,1,0:T(8,128)(2,1)} %param.10) | copy-start | bytes 73732
  0.0 14.5 %collective-permute-start = (bf16[512,128]{1,0:T(8,128)(2,1)}, bf16[512,128]{1,0:T(8,128)(2,1)S(1)}, u32[]{:S(2)}, u32[]{:S(2)}) collective-permute-start(bf16[512,128]{1,0:T(8,128)(2,1)} %bitcast.46), channel_id=1, source_target_pairs={{0,8},{8,16},{16,24},{24,32},{32,40},{40,48},{48,56},{56,64},{64,7... | collective-permute-start | bytes 393224 | tf_op jit(solution)/shard_map/ppermute | solution.py:356
  4.6 9.9 %collective-permute-start.1 = (bf16[512,128]{1,0:T(8,128)(2,1)}, bf16[512,128]{1,0:T(8,128)(2,1)S(1)}, u32[]{:S(2)}, u32[]{:S(2)}) collective-permute-start(bf16[512,128]{1,0:T(8,128)(2,1)} %bitcast.47), channel_id=1, source_target_pairs={{8,0},{16,8},{24,16},{32,24},{40,32},{48,40},{56,48},{64,56},{72,6... | collective-permute-start | bytes 393224 | tf_op jit(solution)/shard_map/ppermute | solution.py:357
  11.7 0.9 copy-start.3
  38.8 34.5 %copy-start.1 = (bf16[1,512,512]{2,1,0:T(8,128)(2,1)S(1)}, bf16[1,512,512]{2,1,0:T(8,128)(2,1)}, u32[]{:S(2)}) copy-start(bf16[1,512,512]{2,1,0:T(8,128)(2,1)} %param.9) | copy-start | bytes 1572868
  67.7 6.8 %collective-permute-start.2 = (bf16[32,32,128]{2,1,0:T(8,128)(2,1)S(1)}, bf16[32,32,128]{2,1,0:T(8,128)(2,1)S(1)}, u32[]{:S(2)}, u32[]{:S(2)}) collective-permute-start(bf16[32,32,128]{2,1,0:T(8,128)(2,1)S(1)} %all_to_all.52.after_ref), channel_id=1, source_target_pairs={{0,8},{8,0},{16,24},{24,16},{32,40},{40,32},{48,56},{56,48},{64,72... | collective-permute-start | bytes 786440 | tf_op jit(solution)/shard_map/ppermute | solution.py:383
  76.5 21.5 %all-to-all-start.3 = ((f32[8,128,128]{2,1,0:T(8,128)}), f32[8,128,128]{2,1,0:T(8,128)S(1)}, u32[]{:S(2)}, u32[]{:S(2)}) async-start(f32[8,128,128]{2,1,0:T(8,128)} %shard_map.87), calls=%async_computation.3 | async-start | bytes 1048576 | tf_op jit(solution)/shard_map/all_to_all | solution.py:106
  80.0 4.3 %collective-permute-start.3 = (f32[312,128]{1,0:T(8,128)S(1)}, f32[312,128]{1,0:T(8,128)S(1)}, u32[]{:S(2)}, u32[]{:S(2)}) collective-permute-start(f32[312,128]{1,0:T(8,128)S(1)} %get-tuple-element.45.own_ahead_ref), channel_id=1, source_target_pairs={{0,8},{8,16},{16,24},{24,32},{32,40},{40,48},{48,56},{56,64},{64,7... | collective-permute-start | bytes 479240 | tf_op jit(solution)/shard_map/ppermute | solution.py:392
  82.0 6.9 %collective-permute-start.4 = (f32[312,128]{1,0:T(8,128)S(1)}, f32[312,128]{1,0:T(8,128)S(1)}, u32[]{:S(2)}, u32[]{:S(2)}) collective-permute-start(f32[312,128]{1,0:T(8,128)S(1)} %get-tuple-element.46.own_behind_ref), channel_id=1, source_target_pairs={{8,0},{16,8},{24,16},{32,24},{40,32},{48,40},{56,48},{64,56},{72,6... | collective-permute-start | bytes 479240 | tf_op jit(solution)/shard_map/ppermute | solution.py:393
  163.1 5.2 %collective-permute-start.5 = (bf16[32,32,128]{2,1,0:T(8,128)(2,1)S(1)}, bf16[32,32,128]{2,1,0:T(8,128)(2,1)S(1)}, u32[]{:S(2)}, u32[]{:S(2)}) collective-permute-start(bf16[32,32,128]{2,1,0:T(8,128)(2,1)S(1)} %all_to_all.56), channel_id=1, source_target_pairs={{0,8},{8,0},{16,24},{24,16},{32,40},{40,32},{48,56},{56,48},{64,72... | collective-permute-start | bytes 786440 | tf_op jit(solution)/shard_map/ppermute | solution.py:422

commit v14 on v13

--- a/solution.py
+++ b/solution.py
@@ -329,8 +329,11 @@
 
     def owner_rows(table_ref, in_ref, sides_ref, weights_ref, rhs_ref):
         down = (iota((block, slots), 0) + 1).astype(F32)
-        marks = jnp.concatenate([ones_where(down == sides_ref[c : c + 1]) for c in range(n_coarse)], axis=1)
-        weights_ref[...] = dot(marks, in_ref[...])
+        weights = jnp.zeros((block, cases), F32)
+        for c in range(0, n_coarse, 2):
+            marks = jnp.concatenate([ones_where(down == sides_ref[c + k : c + k + 1]) for k in range(2)], axis=1)
+            weights = weights + dot(marks, in_ref[c * slots : (c + 2) * slots])
+        weights_ref[...] = weights
         start = pl.multiple_of(table_ref[4, 0] * piece, piece)
         rhs = weights_ref[pl.ds(start, piece), :].astype(BF16)
         for k in range(chips):

time: 193 us -> 193 us (level)
  no operation moved by 1% of the time
where the time goes in v14:
time: 193 us; the launch traced here: 192 us
  blocking collectives  136 us (70%)
  starting transfers between devices  28.3 us (15%)
  waiting for transfers between devices  14.4 us (7%)
  Pallas kernels  8.82 us (5%)
    all_to_all x9, blocking collectives, exchange(): lax.all_to_all(blocks, axis, 0, 0, tiled=True, axis_index_groups=groups)  136 us
    ppermute x2, starting transfers between devices, body(): theirs = lax.ppermute(mine, 'sub', other_core)  9.66 us
    all_to_all x1, waiting for transfers between devices, exchange(): lax.all_to_all(blocks, axis, 0, 0, tiled=True, axis_index_groups=groups)  9.12 us
    pallas_call x11, Pallas kernels, run(): pl.pallas_call(kernel, out_shape=[jax.ShapeDtypeStruct(shape, dtype) for...  8.82 us
    ppermute x1, starting transfers between devices, body(): from_next = lax.ppermute(start, 'sub', to_before)  6.2 us
    ppermute x1, starting transfers between devices, body(): from_before = lax.ppermute(start, 'sub', to_next)  4.63 us
    ppermute x1, waiting for transfers between devices, body(): from_next = lax.ppermute(to_behind, 'sub', to_before)  4.46 us
  transfers between devices with their start and end apart: 7, of which 3 were waited for; matrix products, arithmetic and copies ran while one was open for 0% of the time, Pallas kernels for 2%

profile of v14, /device:TPU:1, one launch (start us, length us, event | category | flops | bytes accessed | tf_op | source)
XLA Modules:
  0.0 192.1 jit_solution(3724041737761503393)
XLA Ops:
  0.0 4.6 %collective-permute-start = (bf16[512,128]{1,0:T(8,128)(2,1)}, bf16[512,128]{1,0:T(8,128)(2,1)S(1)}, u32[]{:S(2)}, u32[]{:S(2)}) collective-permute-start(bf16[512,128]{1,0:T(8,128)(2,1)} %bitcast.46), channel_id=1, source_target_pairs={{0,8},{8,16},{16,24},{24,32},{32,40},{40,48},{48,56},{56,64},{64,7... | collective-permute-start | bytes 393224 | tf_op jit(solution)/shard_map/ppermute | solution.py:359
  4.6 6.2 %collective-permute-start.1 = (bf16[512,128]{1,0:T(8,128)(2,1)}, bf16[512,128]{1,0:T(8,128)(2,1)S(1)}, u32[]{:S(2)}, u32[]{:S(2)}) collective-permute-start(bf16[512,128]{1,0:T(8,128)(2,1)} %bitcast.47), channel_id=1, source_target_pairs={{8,0},{16,8},{24,16},{32,24},{40,32},{48,40},{56,48},{64,56},{72,6... | collective-permute-start | bytes 393224 | tf_op jit(solution)/shard_map/ppermute | solution.py:360
  11.7 0.9 copy-done.3
  12.6 1.9 shard_map.82
  15.4 23.0 %all_to_all.50 = f32[64,4,128]{2,1,0:T(4,128)S(1)} all-to-all(f32[64,4,128]{2,1,0:T(4,128)S(1)} %bitcast.49), channel_id=1, replica_groups=mesh['sub'=64,'coarse'=8] {'sub'}, dimensions={0} | all-to-all | bytes 262144 | tf_op jit(solution)/shard_map/all_to_all | solution.py:106
  38.8 15.3 %all_to_all.51.in_ref = f32[8,40,128]{2,1,0:T(8,128)S(1)} all-to-all(f32[8,40,128]{2,1,0:T(8,128)S(1)} %get-tuple-element.37), channel_id=1, replica_groups=mesh['sub'=64,'coarse'=8] {'coarse'}, dimensions={0} | all-to-all | bytes 327680 | tf_op jit(solution)/shard_map/all_to_all | solution.py:106
  54.2 13.6 %all_to_all.52.after_ref = bf16[32,32,128]{2,1,0:T(8,128)(2,1)S(1)} all-to-all(bf16[32,32,128]{2,1,0:T(8,128)(2,1)S(1)} %get-tuple-element.38), channel_id=1, replica_groups={{0,16,32,48,64,80,96,112,128,144,160,176,192,208,224,240,256,272,288,30..., dimensions={0} | all-to-all | bytes 524288 | tf_op jit(solution)/shard_map/all_to_all | solution.py:106
  67.7 5.6 %collective-permute-start.2 = (bf16[32,32,128]{2,1,0:T(8,128)(2,1)S(1)}, bf16[32,32,128]{2,1,0:T(8,128)(2,1)S(1)}, u32[]{:S(2)}, u32[]{:S(2)}) collective-permute-start(bf16[32,32,128]{2,1,0:T(8,128)(2,1)S(1)} %all_to_all.52.after_ref), channel_id=1, source_target_pairs={{0,8},{8,0},{16,24},{24,16},{32,40},{40,32},{48,56},{56,48},{64,72... | collective-permute-start | bytes 786440 | tf_op jit(solution)/shard_map/ppermute | solution.py:386
  73.3 1.2 shard_map.86
  75.3 1.3 shard_map.87
  76.5 3.5 %all-to-all-start.3 = ((f32[8,128,128]{2,1,0:T(8,128)}), f32[8,128,128]{2,1,0:T(8,128)S(1)}, u32[]{:S(2)}, u32[]{:S(2)}) async-start(f32[8,128,128]{2,1,0:T(8,128)} %shard_map.87), calls=%async_computation.3 | async-start | bytes 1048576 | tf_op jit(solution)/shard_map/all_to_all | solution.py:106
  80.0 1.9 collective-permute-start.3
  82.0 2.4 %collective-permute-start.4 = (f32[312,128]{1,0:T(8,128)S(1)}, f32[312,128]{1,0:T(8,128)S(1)}, u32[]{:S(2)}, u32[]{:S(2)}) collective-permute-start(f32[312,128]{1,0:T(8,128)S(1)} %get-tuple-element.46.own_behind_ref), channel_id=1, source_target_pairs={{8,0},{16,8},{24,16},{32,24},{40,32},{48,40},{56,48},{64,56},{72,6... | collective-permute-start | bytes 479240 | tf_op jit(solution)/shard_map/ppermute | solution.py:396
  84.4 4.5 %collective-permute-done.4.next_ref = f32[312,128]{1,0:T(8,128)S(1)} collective-permute-done((f32[312,128]{1,0:T(8,128)S(1)}, f32[312,128]{1,0:T(8,128)S(1)}, u32[]{:S(2)}, u32[]{:S(2)}) %collective-permute-start.4) | collective-permute-done | bytes 159776 | tf_op jit(solution)/shard_map/ppermute | solution.py:396
  88.9 9.1 %all-to-all-done.3.in_ref = f32[8,128,128]{2,1,0:T(8,128)S(1)} async-done(((f32[8,128,128]{2,1,0:T(8,128)}), f32[8,128,128]{2,1,0:T(8,128)S(1)}, u32[]{:S(2)}, u32[]{:S(2)}) %all-to-all-start.3) | async-done | bytes 524320 | tf_op jit(solution)/shard_map/all_to_all | solution.py:106
  98.3 14.9 %all_to_all.53 = bf16[64,8,128]{2,1,0:T(8,128)(2,1)S(1)} all-to-all(bf16[64,8,128]{2,1,0:T(8,128)(2,1)S(1)} %bitcast.41), channel_id=1, replica_groups=mesh['sub'=64,'coarse'=8] {'sub'}, dimensions={0} | all-to-all | bytes 262144 | tf_op jit(solution)/shard_map/all_to_all | solution.py:106
  113.2 1.4 shard_map.89
  114.5 13.8 %all_to_all.54.in_ref = f32[8,56,128]{2,1,0:T(8,128)S(1)} all-to-all(f32[8,56,128]{2,1,0:T(8,128)S(1)} %get-tuple-element.49), channel_id=1, replica_groups=mesh['sub'=64,'coarse'=8] {'coarse'}, dimensions={0} | all-to-all | bytes 458752 | tf_op jit(solution)/shard_map/all_to_all | solution.py:106
  128.7 18.5 %all_to_all.55 = bf16[64,16,128]{2,1,0:T(8,128)(2,1)S(1)} all-to-all(bf16[64,16,128]{2,1,0:T(8,128)(2,1)S(1)} %bitcast.42), channel_id=1, replica_groups=mesh['sub'=64,'coarse'=8] {'sub'}, dimensions={0} | all-to-all | bytes 524288 | tf_op jit(solution)/shard_map/all_to_all | solution.py:106
  147.2 0.9 shard_map.92
  148.2 15.0 %all_to_all.56 = bf16[32,32,128]{2,1,0:T(8,128)(2,1)S(1)} all-to-all(bf16[32,32,128]{2,1,0:T(8,128)(2,1)S(1)} %get-tuple-element.55), channel_id=1, replica_groups={{0,16,32,48,64,80,96,112,128,144,160,176,192,208,224,240,256,272,288,30..., dimensions={0} | all-to-all | bytes 524288 | tf_op jit(solution)/shard_map/all_to_all | solution.py:106
  163.1 4.1 %collective-permute-start.5 = (bf16[32,32,128]{2,1,0:T(8,128)(2,1)S(1)}, bf16[32,32,128]{2,1,0:T(8,128)(2,1)S(1)}, u32[]{:S(2)}, u32[]{:S(2)}) collective-permute-start(bf16[32,32,128]{2,1,0:T(8,128)(2,1)S(1)} %all_to_all.56), channel_id=1, source_target_pairs={{0,8},{8,0},{16,24},{24,16},{32,40},{40,32},{48,56},{56,48},{64,72... | collective-permute-start | bytes 786440 | tf_op jit(solution)/shard_map/ppermute | solution.py:425
  169.1 9.8 %all_to_all.57 = f32[16,2,128]{2,1,0:T(2,128)S(1)} all-to-all(f32[16,2,128]{2,1,0:T(2,128)S(1)} %broadcast_in_dim.9), channel_id=1, replica_groups={{0,1,2,3,4,5,6,7,8,9,10,11,12,13,14,15},{16,17,18,19,20,21,22,23,24,25,..., dimensions={0} | all-to-all | bytes 32768 | tf_op jit(solution)/shard_map/all_to_all | solution.py:106
  179.0 12.3 %all_to_all.58 = f32[32,2,128]{2,1,0:T(2,128)S(1)} all-to-all(f32[32,2,128]{2,1,0:T(2,128)S(1)} %broadcast_in_dim.10), channel_id=1, replica_groups={{0,16,32,48,64,80,96,112,128,144,160,176,192,208,224,240,256,272,288,30..., dimensions={0} | all-to-all | bytes 65536 | tf_op jit(solution)/shard_map/all_to_all | solution.py:106
  (33 shorter events, 6.3 us)
Async XLA Ops:
  0.0 74.7 %copy-start = (bf16[2048,256]{1,0:T(8,128)(2,1)S(1)}, bf16[2048,256]{1,0:T(8,128)(2,1)}, u32[]{:S(2)}) copy-start(bf16[2048,256]{1,0:T(8,128)(2,1)} %param.11) | copy-start | bytes 3145732
  0.0 11.7 %copy-start.2 = (bf16[1,24,512]{2,1,0:T(8,128)(2,1)S(1)}, bf16[1,24,512]{2,1,0:T(8,128)(2,1)}, u32[]{:S(2)}) copy-start(bf16[1,24,512]{2,1,0:T(8,128)(2,1)} %param.10) | copy-start | bytes 73732
  0.0 14.5 %collective-permute-start = (bf16[512,128]{1,0:T(8,128)(2,1)}, bf16[512,128]{1,0:T(8,128)(2,1)S(1)}, u32[]{:S(2)}, u32[]{:S(2)}) collective-permute-start(bf16[512,128]{1,0:T(8,128)(2,1)} %bitcast.46), channel_id=1, source_target_pairs={{0,8},{8,16},{16,24},{24,32},{32,40},{40,48},{48,56},{56,64},{64,7... | collective-permute-start | bytes 393224 | tf_op jit(solution)/shard_map/ppermute | solution.py:359
  4.6 9.9 %collective-permute-start.1 = (bf16[512,128]{1,0:T(8,128)(2,1)}, bf16[512,128]{1,0:T(8,128)(2,1)S(1)}, u32[]{:S(2)}, u32[]{:S(2)}) collective-permute-start(bf16[512,128]{1,0:T(8,128)(2,1)} %bitcast.47), channel_id=1, source_target_pairs={{8,0},{16,8},{24,16},{32,24},{40,32},{48,40},{56,48},{64,56},{72,6... | collective-permute-start | bytes 393224 | tf_op jit(solution)/shard_map/ppermute | solution.py:360
  11.7 0.9 copy-start.3
  38.8 34.5 %copy-start.1 = (bf16[1,512,512]{2,1,0:T(8,128)(2,1)S(1)}, bf16[1,512,512]{2,1,0:T(8,128)(2,1)}, u32[]{:S(2)}) copy-start(bf16[1,512,512]{2,1,0:T(8,128)(2,1)} %param.9) | copy-start | bytes 1572868
  67.7 6.8 %collective-permute-start.2 = (bf16[32,32,128]{2,1,0:T(8,128)(2,1)S(1)}, bf16[32,32,128]{2,1,0:T(8,128)(2,1)S(1)}, u32[]{:S(2)}, u32[]{:S(2)}) collective-permute-start(bf16[32,32,128]{2,1,0:T(8,128)(2,1)S(1)} %all_to_all.52.after_ref), channel_id=1, source_target_pairs={{0,8},{8,0},{16,24},{24,16},{32,40},{40,32},{48,56},{56,48},{64,72... | collective-permute-start | bytes 786440 | tf_op jit(solution)/shard_map/ppermute | solution.py:386
  76.5 21.5 %all-to-all-start.3 = ((f32[8,128,128]{2,1,0:T(8,128)}), f32[8,128,128]{2,1,0:T(8,128)S(1)}, u32[]{:S(2)}, u32[]{:S(2)}) async-start(f32[8,128,128]{2,1,0:T(8,128)} %shard_map.87), calls=%async_computation.3 | async-start | bytes 1048576 | tf_op jit(solution)/shard_map/all_to_all | solution.py:106
  80.0 4.3 %collective-permute-start.3 = (f32[312,128]{1,0:T(8,128)S(1)}, f32[312,128]{1,0:T(8,128)S(1)}, u32[]{:S(2)}, u32[]{:S(2)}) collective-permute-start(f32[312,128]{1,0:T(8,128)S(1)} %get-tuple-element.45.own_ahead_ref), channel_id=1, source_target_pairs={{0,8},{8,16},{16,24},{24,32},{32,40},{40,48},{48,56},{56,64},{64,7... | collective-permute-start | bytes 479240 | tf_op jit(solution)/shard_map/ppermute | solution.py:395
  82.0 6.9 %collective-permute-start.4 = (f32[312,128]{1,0:T(8,128)S(1)}, f32[312,128]{1,0:T(8,128)S(1)}, u32[]{:S(2)}, u32[]{:S(2)}) collective-permute-start(f32[312,128]{1,0:T(8,128)S(1)} %get-tuple-element.46.own_behind_ref), channel_id=1, source_target_pairs={{8,0},{16,8},{24,16},{32,24},{40,32},{48,40},{56,48},{64,56},{72,6... | collective-permute-start | bytes 479240 | tf_op jit(solution)/shard_map/ppermute | solution.py:396
  163.1 5.2 %collective-permute-start.5 = (bf16[32,32,128]{2,1,0:T(8,128)(2,1)S(1)}, bf16[32,32,128]{2,1,0:T(8,128)(2,1)S(1)}, u32[]{:S(2)}, u32[]{:S(2)}) collective-permute-start(bf16[32,32,128]{2,1,0:T(8,128)(2,1)S(1)} %all_to_all.56), channel_id=1, source_target_pairs={{0,8},{8,0},{16,24},{24,16},{32,40},{40,32},{48,56},{56,48},{64,72... | collective-permute-start | bytes 786440 | tf_op jit(solution)/shard_map/ppermute | solution.py:425
